TPU v7x, 32 devices: a whole 2x2x4 slice. The times are simulated.
32 devices in a mesh: swath: 16 (over z, x, core), chan: 2 (over y).
Axes of the slice: x: 2, y: 2, z: 4, core: 2. Of those that a mesh axis runs over, the one named last changes fastest.
Arguments:
- grid_profiles: bfloat16 [16384, 256], P('swath'), may hold values from -6 to 6
- send_lists: int32 [16, 16, 256], P('swath'), may hold values from 0 to 1023
- counts: int32 [16, 16], P('swath'), may hold values from 1 to 256, as said below
- angle_index: int32 [128], replicated, may hold values from 0 to 7
- jacobian: bfloat16 [3, 256, 608], P(None, None, 'chan'), may hold values from -0.375 to 0.375
- observed: bfloat16 [608, 65536], P('chan', 'swath'), may hold values from -6 to 6
- kappa: float32 [2, 608], P(None, 'chan'), may hold values from 0.04 to 0.24
- factor: bfloat16 [608, 608], P('chan')
Outputs:
- weighted: float32 [608, 65536], P('chan', 'swath')
Inputs may be any that keep to these rules, and one draw needn't show every extreme that they name: `counts`: some receiver gets 256 live slots from every sender; every entry is at least one.
All inputs are finite; a program needn't handle non-finite values.
Results may differ from a plain program's by a relative error of at most 0.0029.
Values may be sent and summed in bfloat16 or wider, within the bound.
No kernel may reach another device: no remote copies, remote signals or barrier semaphores. Data moves between devices by JAX's collectives and lax.ppermute only.
A program may use at most 128 MiB of HBM per device.

v0:
```python
import math

import jax
import jax.numpy as jnp
from jax import lax
from jax.sharding import PartitionSpec as P

XTRACK = 128
NANG = 8


max_zenith = math.pi / 3.0


def extended_2(block, sides, width):
    for axis, dim in sides:
        count = lax.axis_size(axis)
        forward = [(i, i + 1) for i in range(count - 1)]
        backward = [(target, source) for source, target in forward]
        low = lax.ppermute(
            lax.slice_in_dim(block, block.shape[dim] - width, None, axis=dim), axis, forward
        )
        high = lax.ppermute(lax.slice_in_dim(block, 0, width, axis=dim), axis, backward)
        block = jnp.concatenate([low, block, high], axis=dim)
    return block


def diffuse_once(extended, along_rate, cross_rate):
    center = extended[:, 1:-1]
    along_sum = extended[:, 2:] + extended[:, :-2] - 2.0 * center
    side_pad = jnp.pad(center, ((0, 0), (0, 0), (1, 1)))
    cross_sum = side_pad[:, :, 2:] + side_pad[:, :, :-2] - 2.0 * center
    return center + along_rate * along_sum + cross_rate * cross_sum


def line_rims(smooth_field):
    return extended_2(smooth_field, (("swath", 1),), 1)


def on_device(grid_profiles, send_lists, counts, angle_index, jacobian, observed, kappa, factor):
    slot_rows = send_lists[0]
    slots = slot_rows.shape[1]
    own_chan = observed.shape[0]
    pixel_count = observed.shape[1]
    line_count = pixel_count // XTRACK
    live_slot = jnp.arange(slots, dtype=jnp.int32)[None, :] < counts[0][:, None]
    zero_value = jnp.zeros((), grid_profiles.dtype)
    outgoing = jnp.where(live_slot[:, :, None], grid_profiles[slot_rows], zero_value)
    incoming = lax.all_to_all(outgoing, "swath", split_axis=0, concat_axis=0, tiled=True)
    pixel_profiles = incoming.reshape(pixel_count, grid_profiles.shape[1])
    model = jnp.einsum("mkc,pk->mcp", jacobian, pixel_profiles, preferred_element_type=jnp.float32)
    zenith = angle_index.astype(jnp.float32) * (max_zenith / (NANG - 1))
    slant_path = 1.0 / jnp.cos(zenith) - 1.0
    model = model.reshape(3, own_chan, line_count, XTRACK)
    departure = observed.astype(jnp.float32).reshape(own_chan, line_count, XTRACK) - (
        model[0] + slant_path * model[1] + slant_path * slant_path * model[2]
    )
    along_rate = kappa[0][:, None, None]
    cross_rate = kappa[1][:, None, None]
    smooth_field = departure
    for sweep in range(3):
        smooth_field = diffuse_once(line_rims(smooth_field), along_rate, cross_rate)
    smoothed = smooth_field.reshape(own_chan, pixel_count).astype(jnp.bfloat16)
    return jnp.dot(
        factor,
        lax.all_gather(smoothed, "chan", axis=0, tiled=True),
        preferred_element_type=jnp.float32,
    )


def solution(mesh):
    in_specs = (
        P("swath", None),
        P("swath", None, None),
        P("swath", None),
        P(),
        P(None, None, "chan"),
        P("chan", "swath"),
        P(None, "chan"),
        P("chan", None),
    )
    out_specs = P("chan", "swath")
    return jax.shard_map(
        on_device, mesh=mesh, in_specs=in_specs, out_specs=out_specs, check_vma=False
    )
```

profile of v0, /device:TPU:16, one launch (start us, length us, event | category | flops | bytes accessed | tf_op | source)
XLA Modules:
  0.0 244.4 jit_solution(9459271592340459102)
XLA Ops:
  6.5 0.0 copy-start
  6.5 0.8 fusion.28
  7.3 0.7 iota_compare_fusion
  8.1 0.0 copy-done
  8.1 14.6 %gather_fusion = bf16[4096,256]{1,0:T(8,128)(2,1)S(1)} fusion(bf16[1024,256]{1,0:T(8,128)(2,1)S(1)} %copy-done, s32[4096]{0:T(1024)S(1)} %broadcast_clamp_fusion), kind=kCustom, calls=%fused_computation | custom fusion | bytes 4210688 | tf_op jit(solution)/shard_map/gather | solution.py:48
  22.7 1.7 broadcast_select_fusion
  24.4 6.2 %all-to-all-start = ((bf16[16,256,256]{2,1,0:T(8,128)(2,1)}), bf16[16,256,256]{2,1,0:T(8,128)(2,1)S(1)}, u32[]{:S(2)}, u32[]{:S(2)}) async-start(bf16[16,256,256]{2,1,0:T(8,128)(2,1)} %broadcast_select_fusion), calls=%async_computation | async-start | bytes 4194304 | tf_op jit(solution)/shard_map/all_to_all | solution.py:49
  30.5 0.0 all-gather.2.cloned.1.call-start
  30.6 2.3 convert_bitcast_fusion
  32.9 0.0 copy-start.6
  32.9 0.0 copy-start.4
  32.9 3.1 %copy.9 = f32[38,8,32,128]{3,2,1,0:T(8,128)} copy(f32[38,8,32,128]{3,1,2,0:T(8,128)S(1)} %convert_bitcast_fusion) | data formatting | bytes 9961472
  36.0 0.0 copy-done.6
  36.1 42.1 %all-to-all-done = bf16[16,256,256]{2,1,0:T(8,128)(2,1)S(1)} async-done(((bf16[16,256,256]{2,1,0:T(8,128)(2,1)}), bf16[16,256,256]{2,1,0:T(8,128)(2,1)S(1)}, u32[]{:S(2)}, u32[]{:S(2)}) %all-to-all-start) | async-done | bytes 2097184 | tf_op jit(solution)/shard_map/all_to_all | solution.py:49
  78.2 0.0 copy-done.4
  78.2 7.4 %convolution_bitcast_fusion = f32[3,304,4096]{2,1,0:T(8,128)} fusion(bf16[4096,256,1]{1,0,2:T(8,128)(2,1)S(1)} %bitcast.55, bf16[3,256,304]{1,2,0:T(8,128)(2,1)S(1)} %copy-done.4), kind=kOutput, calls=%fused_computation.7 | convolution fusion | flops 1912602624 | bytes 17506304 | tf_op jit(solution)/shard_map/mkc,pk->mcp/dot_general | solution.py:51
  85.6 11.3 %slice_bitcast_fusion.2 = (f32[38,8,32,128]{3,1,2,0:T(8,128)}, f32[38,8,32,128]{3,1,2,0:T(8,128)}, f32[38,8,32,128]{3,1,2,0:T(8,128)}) fusion(f32[3,304,4096]{2,1,0:T(8,128)} %convolution_bitcast_fusion), kind=kLoop, calls=%fused_computation.47 | loop fusion | bytes 29884416
  96.9 0.0 copy-start.2
  96.9 0.0 slice-start
  96.9 5.9 %copy.11 = f32[38,8,32,128]{3,2,1,0:T(8,128)} copy(f32[38,8,32,128]{3,1,2,0:T(8,128)} %get-tuple-element.9) | data formatting | bytes 9961472
  102.9 0.0 copy-done.2
  102.9 0.0 slice-start.1
  102.9 3.2 %copy.12 = f32[38,8,32,128]{3,2,1,0:T(8,128)} copy(f32[38,8,32,128]{3,1,2,0:T(8,128)S(1)} %copy-done.2) | data formatting | bytes 9961472
  106.1 0.0 slice-done
  106.1 0.0 slice-done.1
  106.1 3.2 %copy.13 = f32[38,8,32,128]{3,2,1,0:T(8,128)} copy(f32[38,8,32,128]{3,1,2,0:T(8,128)S(1)} %bitcast.51) | data formatting | bytes 9961472
  109.3 0.0 copy-start.5
  109.3 9.3 %fusion.14 = f32[304,32,128]{2,1,0:T(8,128)S(1)} fusion(f32[38,8,32,128]{3,2,1,0:T(8,128)} %copy.13, f32[38,8,32,128]{3,2,1,0:T(8,128)} %copy.12, f32[38,8,32,128]{3,2,1,0:T(8,128)} %copy.11, f32[38,8,32,128]{3,2,1,0:T(8,128)} %copy.9, f32[128]{0:T(128)S(1)} %get-tuple-element.7, f32[128]{0:T(128)S(1)} %get-tuple-element.8), kind=kLoop, calls=%fused_computation.24 | loop fusion | flops 6225920 | bytes 24904704 | tf_op jit(solution)/shard_map/sub | solution.py:55
  118.6 0.2 fusion.32
  118.8 2.9 %collective-permute-start = (f32[304,1,128]{2,1,0:T(1,128)S(1)}, f32[304,1,128]{2,1,0:T(1,128)S(1)}, u32[]{:S(2)}, u32[]{:S(2)}) collective-permute-start(f32[304,1,128]{2,1,0:T(1,128)S(1)} %get-tuple-element.16), channel_id=1, source_target_pairs={{2,0},{4,2},{6,4},{8,6},{10,8},{12,10},{14,12},{16,14},{18,16},{20... | collective-permute-start | bytes 466952 | tf_op jit(solution)/shard_map/ppermute | solution.py:23
  121.7 2.1 collective-permute-start.1
  123.8 0.0 copy-done.5
  123.9 0.6 collective-permute-done
  124.5 4.7 %collective-permute-done.1 = f32[304,1,128]{2,1,0:T(1,128)S(1)} collective-permute-done((f32[304,1,128]{2,1,0:T(1,128)S(1)}, f32[304,1,128]{2,1,0:T(1,128)S(1)}, u32[]{:S(2)}, u32[]{:S(2)}) %collective-permute-start.1) | collective-permute-done | bytes 155680 | tf_op jit(solution)/shard_map/ppermute | solution.py:20
  129.2 4.8 %fusion.3 = f32[304,32,128]{2,1,0:T(8,128)S(1)} fusion(f32[304,32,128]{2,1,0:T(8,128)S(1)} %fusion.14, f32[304,1,128]{2,1,0:T(1,128)S(1)} %collective-permute-done.1, f32[304,1,128]{2,1,0:T(1,128)S(1)} %collective-permute-done, f32[304]{0:T(512)S(1)} %get-tuple-element.6, f32[304]{0:T(512)S(1)} %get-tuple-element.5), kind=kLoop, calls=%fused_computation.12 | loop fusion | flops 13697024 | bytes 10275200 | tf_op jit(solution)/shard_map/add | solution.py:33
  134.0 0.2 fusion.31
  134.2 1.9 collective-permute-start.2
  136.1 2.4 collective-permute-start.3
  138.5 0.3 collective-permute-done.2
  138.9 4.7 %collective-permute-done.3 = f32[304,1,128]{2,1,0:T(1,128)S(1)} collective-permute-done((f32[304,1,128]{2,1,0:T(1,128)S(1)}, f32[304,1,128]{2,1,0:T(1,128)S(1)}, u32[]{:S(2)}, u32[]{:S(2)}) %collective-permute-start.3) | collective-permute-done | bytes 155680 | tf_op jit(solution)/shard_map/ppermute | solution.py:20
  143.6 4.8 %fusion.7 = f32[304,32,128]{2,1,0:T(8,128)S(1)} fusion(f32[304,32,128]{2,1,0:T(8,128)S(1)} %fusion.3, f32[304,1,128]{2,1,0:T(1,128)S(1)} %collective-permute-done.3, f32[304,1,128]{2,1,0:T(1,128)S(1)} %collective-permute-done.2, f32[304]{0:T(512)S(1)} %get-tuple-element.6, f32[304]{0:T(512)S(1)} %get-tuple-element.5), kind=kLoop, calls=%fused_computation.16 | loop fusion | flops 13697024 | bytes 10275200 | tf_op jit(solution)/shard_map/add | solution.py:33
  148.4 0.2 fusion.30
  148.6 1.9 collective-permute-start.4
  150.5 2.4 collective-permute-start.5
  152.9 0.3 collective-permute-done.4
  153.3 4.7 %collective-permute-done.5 = f32[304,1,128]{2,1,0:T(1,128)S(1)} collective-permute-done((f32[304,1,128]{2,1,0:T(1,128)S(1)}, f32[304,1,128]{2,1,0:T(1,128)S(1)}, u32[]{:S(2)}, u32[]{:S(2)}) %collective-permute-start.5) | collective-permute-done | bytes 155680 | tf_op jit(solution)/shard_map/ppermute | solution.py:20
  158.0 5.2 %fusion.12 = bf16[304,32,128]{2,1,0:T(8,128)(2,1)S(1)} fusion(f32[304,32,128]{2,1,0:T(8,128)S(1)} %fusion.7, f32[304,1,128]{2,1,0:T(1,128)S(1)} %collective-permute-done.5, f32[304,1,128]{2,1,0:T(1,128)S(1)} %collective-permute-done.4, f32[304]{0:T(512)S(1)} %get-tuple-element.6, f32[304]{0:T(512)S(1)} %get-tuple-element.5), kind=kLoop, calls=%fused_computation.21 | loop fusion | flops 14942208 | bytes 7784832 | tf_op jit(solution)/shard_map/convert_element_type | solution.py:63
  163.2 0.0 copy-start.3
  163.2 2.6 %copy.16 = bf16[38,8,32,128]{3,1,2,0:T(8,128)(2,1)} copy(bf16[38,8,32,128]{3,2,1,0:T(8,128)(2,1)S(1)} %bitcast.53) | data formatting | bytes 4980736
  165.8 0.0 all-gather.2.cloned.1.call-update
  165.8 0.0 copy-start.1
  165.9 64.9 %all-gather.2.cloned.1.call-done = bf16[608,4096]{1,0:T(8,128)(2,1)} async-done(((bf16[304,4096]{1,0:T(8,128)(2,1)}), bf16[608,4096]{1,0:T(8,128)(2,1)}) %all-gather.2.cloned.1.call-update) | async-done | bytes 4980752 | tf_op jit(solution)/shard_map/all_gather | solution.py:66
  230.7 0.0 copy-done.3
  230.7 6.8 %convolution_bitcast_fusion.1 = f32[304,4096]{1,0:T(8,128)} fusion(bf16[304,608]{1,0:T(8,128)(2,1)S(1)} %copy-done.3, bf16[608,4096]{1,0:T(8,128)(2,1)} %all-gather.2.cloned.1.call-done), kind=kOutput, calls=%fused_computation.8 | convolution fusion | flops 1514143744 | bytes 10331136 | tf_op jit(solution)/shard_map/dot_general | solution.py:64
  237.5 0.0 copy-done.1
  (5 shorter events, 0.1 us)
Async XLA Ops:
  6.5 1.5 copy-start
  24.4 53.8 %all-to-all-start = ((bf16[16,256,256]{2,1,0:T(8,128)(2,1)}), bf16[16,256,256]{2,1,0:T(8,128)(2,1)S(1)}, u32[]{:S(2)}, u32[]{:S(2)}) async-start(bf16[16,256,256]{2,1,0:T(8,128)(2,1)} %broadcast_select_fusion), calls=%async_computation | async-start | bytes 4194304 | tf_op jit(solution)/shard_map/all_to_all | solution.py:49
  30.5 200.2 %all-gather.2.cloned.1.call-start = ((), (), s32[]{:S(2)}) async-start(), calls=%async_computation.1 | async-start | bytes 7471104 | tf_op jit(solution)/shard_map/all_gather | solution.py:66
  32.9 3.2 %copy-start.6 = (s32[128]{0:T(128)S(1)}, s32[128]{0:T(128)}, u32[]{:S(2)}) copy-start(s32[128]{0:T(128)} %param.11) | copy-start | bytes 1540
  32.9 45.3 %copy-start.4 = (bf16[3,256,304]{1,2,0:T(8,128)(2,1)S(1)}, bf16[3,256,304]{1,2,0:T(8,128)(2,1)}, u32[]{:S(2)}) copy-start(bf16[3,256,304]{1,2,0:T(8,128)(2,1)} %param.12) | copy-start | bytes 1400836
  96.9 6.0 %copy-start.2 = (f32[38,8,32,128]{3,1,2,0:T(8,128)S(1)}, f32[38,8,32,128]{3,1,2,0:T(8,128)}, u32[]{:S(2)}) copy-start(f32[38,8,32,128]{3,1,2,0:T(8,128)} %get-tuple-element.11) | copy-start | bytes 14942212
  96.9 9.1 %slice-start = ((s8[4980736]{0:T(1024)(128)(4,1)}), s8[4194304]{0:T(1024)(128)(4,1)S(1)}, s32[]{:S(2)}) async-start(s8[4980736]{0:T(1024)(128)(4,1)} %bitcast.50), calls=%async_computation.2 | async-start | bytes 8388608
  102.9 3.2 %slice-start.1 = ((s8[4980736]{0:T(1024)(128)(4,1)}), s8[786432]{0:T(1024)(128)(4,1)S(1)}, s32[]{:S(2)}) async-start(s8[4980736]{0:T(1024)(128)(4,1)} %bitcast.50), calls=%async_computation.3 | async-start | bytes 1572864
  109.3 14.5 %copy-start.5 = (f32[2,304]{1,0:T(2,128)S(1)}, f32[2,304]{1,0:T(2,128)}, u32[]{:S(2)}) copy-start(f32[2,304]{1,0:T(2,128)} %param.14) | copy-start | bytes 7300
  118.8 5.6 %collective-permute-start = (f32[304,1,128]{2,1,0:T(1,128)S(1)}, f32[304,1,128]{2,1,0:T(1,128)S(1)}, u32[]{:S(2)}, u32[]{:S(2)}) collective-permute-start(f32[304,1,128]{2,1,0:T(1,128)S(1)} %get-tuple-element.16), channel_id=1, source_target_pairs={{2,0},{4,2},{6,4},{8,6},{10,8},{12,10},{14,12},{16,14},{18,16},{20... | collective-permute-start | bytes 466952 | tf_op jit(solution)/shard_map/ppermute | solution.py:23
  121.7 7.4 %collective-permute-start.1 = (f32[304,1,128]{2,1,0:T(1,128)S(1)}, f32[304,1,128]{2,1,0:T(1,128)S(1)}, u32[]{:S(2)}, u32[]{:S(2)}) collective-permute-start(f32[304,1,128]{2,1,0:T(1,128)S(1)} %get-tuple-element.17), channel_id=1, source_target_pairs={{0,2},{2,4},{4,6},{6,8},{8,10},{10,12},{12,14},{14,16},{16,18},{18... | collective-permute-start | bytes 466952 | tf_op jit(solution)/shard_map/ppermute | solution.py:20
  134.2 4.7 %collective-permute-start.2 = (f32[304,1,128]{2,1,0:T(1,128)S(1)}, f32[304,1,128]{2,1,0:T(1,128)S(1)}, u32[]{:S(2)}, u32[]{:S(2)}) collective-permute-start(f32[304,1,128]{2,1,0:T(1,128)S(1)} %get-tuple-element.14), channel_id=1, source_target_pairs={{2,0},{4,2},{6,4},{8,6},{10,8},{12,10},{14,12},{16,14},{18,16},{20... | collective-permute-start | bytes 466952 | tf_op jit(solution)/shard_map/ppermute | solution.py:23
  136.1 7.4 %collective-permute-start.3 = (f32[304,1,128]{2,1,0:T(1,128)S(1)}, f32[304,1,128]{2,1,0:T(1,128)S(1)}, u32[]{:S(2)}, u32[]{:S(2)}) collective-permute-start(f32[304,1,128]{2,1,0:T(1,128)S(1)} %get-tuple-element.15), channel_id=1, source_target_pairs={{0,2},{2,4},{4,6},{6,8},{8,10},{10,12},{12,14},{14,16},{16,18},{18... | collective-permute-start | bytes 466952 | tf_op jit(solution)/shard_map/ppermute | solution.py:20
  148.6 4.7 %collective-permute-start.4 = (f32[304,1,128]{2,1,0:T(1,128)S(1)}, f32[304,1,128]{2,1,0:T(1,128)S(1)}, u32[]{:S(2)}, u32[]{:S(2)}) collective-permute-start(f32[304,1,128]{2,1,0:T(1,128)S(1)} %get-tuple-element.12), channel_id=1, source_target_pairs={{2,0},{4,2},{6,4},{8,6},{10,8},{12,10},{14,12},{16,14},{18,16},{20... | collective-permute-start | bytes 466952 | tf_op jit(solution)/shard_map/ppermute | solution.py:23
  150.5 7.4 %collective-permute-start.5 = (f32[304,1,128]{2,1,0:T(1,128)S(1)}, f32[304,1,128]{2,1,0:T(1,128)S(1)}, u32[]{:S(2)}, u32[]{:S(2)}) collective-permute-start(f32[304,1,128]{2,1,0:T(1,128)S(1)} %get-tuple-element.13), channel_id=1, source_target_pairs={{0,2},{2,4},{4,6},{6,8},{8,10},{10,12},{12,14},{14,16},{16,18},{18... | collective-permute-start | bytes 466952 | tf_op jit(solution)/shard_map/ppermute | solution.py:20
  163.2 67.6 %copy-start.3 = (bf16[304,608]{1,0:T(8,128)(2,1)S(1)}, bf16[304,608]{1,0:T(8,128)(2,1)}, u32[]{:S(2)}) copy-start(bf16[304,608]{1,0:T(8,128)(2,1)} %param.15) | copy-start | bytes 1108996
  165.8 71.7 %copy-start.1 = (bf16[1024,256]{1,0:T(8,128)(2,1)S(1)}, bf16[1024,256]{1,0:T(8,128)(2,1)}, u32[]{:S(2)}) copy-start(bf16[1024,256]{1,0:T(8,128)(2,1)} %param.8) | copy-start | bytes 1572868
Sparse Core Ops, SparseCore 0:
  166.0 64.7 all-gather.1
where the time goes:
time: 246 us; the launch traced here: 244 us
  waiting for transfers between devices  122 us (50%)
  local copies, waits for them, and re-layouts  44.8 us (18%)
  other arithmetic  29.6 us (12%)
  starting transfers between devices  19.8 us (8%)
  matrix products  14.2 us (6%)
  between operations  13.6 us (6%)
    all_gather x1, waiting for transfers between devices, on_device(): lax.all_gather(smoothed, 'chan', axis=0, tiled=True)  64.9 us
    all_to_all x1, waiting for transfers between devices, on_device(): lax.all_to_all(outgoing, 'swath', split_axis=0, concat_axis=0, tiled=True)  42.1 us
    unnamed x25, local copies, waits for them, and re-layouts  29.5 us
    gather x1, local copies, waits for them, and re-layouts, on_device(): grid_profiles[slot_rows]  14.6 us
    ppermute x3, waiting for transfers between devices, extended_2(): lax.ppermute(lax.slice_in_dim(block, block.shape[dim] - width, None, axis...  14.2 us
    add x2, other arithmetic, diffuse_once(): return center + along_rate * along_sum + cross_rate * cross_sum  9.58 us
    sub x1, other arithmetic, on_device(): observed.astype(jnp.float32).reshape(own_chan, line_count, XTRACK)  9.29 us
    dot_general x1, matrix products, on_device(): jnp.einsum('mkc,pk->mcp', jacobian, pixel_profiles, preferred_element_typ...  7.43 us
  transfers between devices with their start and end apart: 8, of which 8 were waited for; matrix products, arithmetic and copies ran while one was open for 2% of the time, Pallas kernels for 0%

commit v1 on v0

--- a/solution.py
+++ b/solution.py
@@ -1,12 +1,17 @@
+import functools
 import math
 
 import jax
 import jax.numpy as jnp
 from jax import lax
+from jax.experimental import pallas as pl
+from jax.experimental.pallas import tpu as pltpu
 from jax.sharding import PartitionSpec as P
 
 XTRACK = 128
 NANG = 8
+HALO = 3
+VMEM_LIMIT = 60 * 1024 * 1024
 
 
 max_zenith = math.pi / 3.0
@@ -37,7 +42,12 @@
     return extended_2(smooth_field, (("swath", 1),), 1)
 
 
-def on_device(grid_profiles, send_lists, counts, angle_index, jacobian, observed, kappa, factor):
+def slant_of(angle_index):
+    zenith = angle_index.astype(jnp.float32) * (max_zenith / (NANG - 1))
+    return 1.0 / jnp.cos(zenith) - 1.0
+
+
+def on_device_plain(grid_profiles, send_lists, counts, angle_index, jacobian, observed, kappa, factor):
     slot_rows = send_lists[0]
     slots = slot_rows.shape[1]
     own_chan = observed.shape[0]
@@ -49,8 +59,7 @@
     incoming = lax.all_to_all(outgoing, "swath", split_axis=0, concat_axis=0, tiled=True)
     pixel_profiles = incoming.reshape(pixel_count, grid_profiles.shape[1])
     model = jnp.einsum("mkc,pk->mcp", jacobian, pixel_profiles, preferred_element_type=jnp.float32)
-    zenith = angle_index.astype(jnp.float32) * (max_zenith / (NANG - 1))
-    slant_path = 1.0 / jnp.cos(zenith) - 1.0
+    slant_path = slant_of(angle_index)
     model = model.reshape(3, own_chan, line_count, XTRACK)
     departure = observed.astype(jnp.float32).reshape(own_chan, line_count, XTRACK) - (
         model[0] + slant_path * model[1] + slant_path * slant_path * model[2]
@@ -68,6 +77,199 @@
     )
 
 
+def gather_kernel(idx_ref, grid_ref, out_ref):
+    grid_rows = grid_ref.shape[0]
+    slots, parts = idx_ref.shape
+    row_number = lax.broadcasted_iota(jnp.int32, (slots, grid_rows), 1)
+    for part in range(parts):
+        one_hot = (idx_ref[:, part : part + 1] == row_number).astype(jnp.float32).astype(jnp.bfloat16)
+        rows = jnp.dot(one_hot, grid_ref[...], preferred_element_type=jnp.float32)
+        out_ref[part] = rows.astype(out_ref.dtype)
+
+
+def gather_rows(grid_profiles, slot_rows, counts):
+    parts, slots = slot_rows.shape
+    live_slot = jnp.arange(slots, dtype=jnp.int32)[None, :] < counts[:, None]
+    picks = jnp.where(live_slot, slot_rows, -1).T
+    return pl.pallas_call(
+        gather_kernel,
+        out_shape=jax.ShapeDtypeStruct((parts, slots, grid_profiles.shape[1]), grid_profiles.dtype),
+        compiler_params=pltpu.CompilerParams(vmem_limit_bytes=VMEM_LIMIT),
+        name="pick_rows",
+    )(picks, grid_profiles)
+
+
+def main_kernel(
+    prof_ref, prof_top_ref, prof_bot_ref,
+    jac_own_ref, jac_oth_ref,
+    obs_ref, mid_ref, bnd_ref, top_ref, bot_ref,
+    rates_ref, rows_ref, factor_ref,
+    out_ref,
+    dep, smooth,
+):
+    own = obs_ref.shape[0]
+    pixels = obs_ref.shape[1]
+    rim = top_ref.shape[1]
+    chans = 2 * own
+    lines = pixels // XTRACK
+    s1 = rows_ref[0:1, :]
+    s2 = rows_ref[1:2, :]
+
+    def model(jac, prof, obs, width):
+        terms = [
+            lax.dot_general(
+                jac[m], prof, (((1,), (1,)), ((), ())), preferred_element_type=jnp.float32
+            )
+            for m in range(3)
+        ]
+        t1 = jnp.concatenate([s1] * (width // XTRACK), axis=1)
+        t2 = jnp.concatenate([s2] * (width // XTRACK), axis=1)
+        return obs.astype(jnp.float32) - (terms[0] + t1 * terms[1] + t2 * terms[2])
+
+    for part, jac in enumerate((jac_own_ref, jac_oth_ref)):
+        chan = slice(part * own, (part + 1) * own)
+        dep[chan, 0:rim] = model(jac, prof_top_ref[...], top_ref[chan, :], rim)
+        dep[chan, rim + pixels : pixels + 2 * rim] = model(jac, prof_bot_ref[...], bot_ref[chan, :], rim)
+
+    wide = 2 * XTRACK
+
+    def own_block(t, carry):
+        at = pl.multiple_of(t * wide, wide)
+        dep[0:own, pl.ds(pl.multiple_of(rim + at, XTRACK), wide)] = model(
+            jac_own_ref, prof_ref[pl.ds(at, wide), :], obs_ref[:, pl.ds(at, wide)], wide
+        )
+        return carry
+
+    lax.fori_loop(0, pixels // wide, own_block, 0)
+
+    dep[own:chans, rim : 2 * rim] = model(jac_oth_ref, prof_ref[0:rim, :], bnd_ref[:, 0:rim], rim)
+    dep[own:chans, pixels : pixels + rim] = model(
+        jac_oth_ref, prof_ref[pixels - rim : pixels, :], bnd_ref[:, rim : 2 * rim], rim
+    )
+
+    def other_block(t, carry):
+        at = pl.multiple_of(t * wide, wide)
+        dep[own:chans, pl.ds(pl.multiple_of(2 * rim + at, XTRACK), wide)] = model(
+            jac_oth_ref, prof_ref[pl.ds(pl.multiple_of(rim + at, XTRACK), wide), :],
+            mid_ref[:, pl.ds(at, wide)], wide
+        )
+        return carry
+
+    lax.fori_loop(0, (pixels - 2 * rim) // wide, other_block, 0)
+
+    inside_top = rows_ref[2:3, :]
+    inside_bot = rows_ref[3:4, :]
+    total = lines + 2 * HALO
+
+    def diffuse(i, carry):
+        chan = pl.ds(pl.multiple_of(i * 16, 16), 16)
+        along = rates_ref[0, chan, :]
+        left = rates_ref[1, chan, :]
+        right = rates_ref[2, chan, :]
+        stay = rates_ref[3, chan, :]
+
+        def sweep(before, here, after):
+            return (
+                stay * here
+                + along * (before + after)
+                + left * pltpu.roll(here, 1, 1)
+                + right * pltpu.roll(here, XTRACK - 1, 1)
+            )
+
+        fields = [{}, {}, {}, {}]
+        for j in range(total):
+            fields[0][j] = dep[chan, j * XTRACK : (j + 1) * XTRACK]
+            for k in range(1, HALO + 1):
+                at = j - k
+                if at < k:
+                    continue
+                prev = fields[k - 1]
+                new = sweep(prev[at - 1], prev[at], prev[at + 1])
+                if at < HALO:
+                    new = new * inside_top
+                if at >= HALO + lines:
+                    new = new * inside_bot
+                fields[k][at] = new
+                del prev[at - 1]
+                if k == HALO:
+                    line = at - HALO
+                    smooth[chan, line * XTRACK : (line + 1) * XTRACK] = new.astype(smooth.dtype)
+        return carry
+
+    lax.fori_loop(0, chans // 16, diffuse, 0)
+
+    def factor_block(t, carry):
+        at = pl.multiple_of(t * wide, wide)
+        out_ref[:, pl.ds(at, wide)] = jnp.dot(
+            factor_ref[...], smooth[:, pl.ds(at, wide)], preferred_element_type=jnp.float32
+        )
+        return carry
+
+    lax.fori_loop(0, pixels // wide, factor_block, 0)
+
+
+def on_device_two(grid_profiles, send_lists, counts, angle_index, jacobian, observed, kappa, factor):
+    own, pixels = observed.shape
+    rim = HALO * XTRACK
+    swath = lax.axis_size("swath")
+    place = lax.axis_index("swath")
+    half = lax.axis_index("chan")
+    swap = [(0, 1), (1, 0)]
+    forward = [(i, i + 1) for i in range(swath - 1)]
+    backward = [(i + 1, i) for i in range(swath - 1)]
+
+    jac_own = jnp.swapaxes(jacobian, 1, 2)
+    jac_oth = lax.ppermute(jac_own, "chan", swap)
+    bnd_own = jnp.concatenate([observed[:, :rim], observed[:, pixels - rim :]], axis=1)
+    bnd_oth = lax.ppermute(bnd_own, "chan", swap)
+    mid_oth = lax.ppermute(observed[:, rim : pixels - rim], "chan", swap)
+    kappa_oth = lax.ppermute(kappa, "chan", swap)
+
+    outgoing = gather_rows(grid_profiles, send_lists[0], counts[0])
+    incoming = lax.all_to_all(outgoing, "swath", split_axis=0, concat_axis=0, tiled=True)
+    profiles = incoming.reshape(pixels, grid_profiles.shape[1])
+    prof_top = lax.ppermute(profiles[pixels - rim :], "swath", forward)
+    prof_bot = lax.ppermute(profiles[:rim], "swath", backward)
+
+    both = jnp.concatenate([bnd_own, bnd_oth], axis=0)
+    obs_top = lax.ppermute(both[:, rim:], "swath", forward)
+    obs_bot = lax.ppermute(both[:, :rim], "swath", backward)
+
+    rate = jnp.concatenate([kappa, kappa_oth], axis=1)[:, :, None]
+    lane = jnp.arange(XTRACK, dtype=jnp.int32)[None, :]
+    along, cross = rate[0], rate[1]
+    ones = jnp.ones((1, XTRACK), jnp.float32)
+    rates = jnp.stack([
+        along * ones,
+        cross * (lane > 0),
+        cross * (lane < XTRACK - 1),
+        (1.0 - 2.0 * along - 2.0 * cross) * ones,
+    ])
+    slant = slant_of(angle_index)
+    rows = jnp.stack([
+        slant,
+        slant * slant,
+        jnp.where(place > 0, ones[0], 0.0),
+        jnp.where(place < swath - 1, ones[0], 0.0),
+    ])
+    factor_two = jnp.where(half == 0, factor, jnp.roll(factor, own, axis=1))
+
+    return pl.pallas_call(
+        main_kernel,
+        out_shape=jax.ShapeDtypeStruct((own, pixels), jnp.float32),
+        scratch_shapes=[
+            pltpu.VMEM((2 * own, pixels + 2 * rim), jnp.float32),
+            pltpu.VMEM((2 * own, pixels), jnp.bfloat16),
+        ],
+        compiler_params=pltpu.CompilerParams(vmem_limit_bytes=VMEM_LIMIT),
+        name="departures_sweeps_factor",
+    )(
+        profiles, prof_top, prof_bot, jac_own, jac_oth,
+        observed, mid_oth, bnd_oth, obs_top, obs_bot,
+        rates, rows, factor_two,
+    )
+
+
 def solution(mesh):
     in_specs = (
         P("swath", None),
@@ -80,6 +282,7 @@
         P("chan", None),
     )
     out_specs = P("chan", "swath")
+    on_device = on_device_two if mesh.shape["chan"] == 2 else on_device_plain
     return jax.shard_map(
         on_device, mesh=mesh, in_specs=in_specs, out_specs=out_specs, check_vma=False
     )

time: 246 us -> 155 us (0.63)
  waiting for transfers between devices: 122 us -> 46 us
  Pallas kernels: 0 us -> 73.3 us
  local copies, waits for them, and re-layouts: 44.8 us -> 7.88 us
  other arithmetic: 29.6 us -> 5.97 us
  matrix products: 14.2 us -> 0 us
  between operations: 13.6 us -> 0.15 us
    pallas_call x0 -> x2, Pallas kernels: none -> 73.3 us  [the longest x1 68.5 us: on_device_two(): pl.pallas_call(main_kernel, out_shape=jax.ShapeDtypeStruct((own, pixels),...]
    all_gather x1 -> x0, waiting for transfers between devices: 64.9 us -> none  [on_device(): lax.all_gather(smoothed, 'chan', axis=0, tiled=True)]
    unnamed x25 -> x19, local copies, waits for them, and re-layouts: 29.5 us -> 2.18 us
    all_to_all x1, waiting for transfers between devices: 42.1 us -> 25.4 us  [on_device_two(): lax.all_to_all(outgoing, 'swath', split_axis=0, concat_axis=0, tiled=True)]
    gather x1 -> x0, local copies, waits for them, and re-layouts: 14.6 us -> none  [on_device(): grid_profiles[slot_rows]]
    dot_general x2 -> x0, matrix products: 14.2 us -> none  [the longest x1 7.43 us: on_device(): jnp.einsum('mkc,pk->mcp', jacobian, pixel_profiles, preferred_element_typ...]
    add x2 -> x0, other arithmetic: 9.58 us -> none  [diffuse_once(): return center + along_rate * along_sum + cross_rate * cross_sum]
    sub x1, other arithmetic: 9.29 us -> 0.01 us  [on_device_two(): 1.0 - 2.0 * along - 2.0 * cross]
  transfers between devices with their start and end apart: 8 -> 9, of which waited for: 8 -> 3; matrix products, arithmetic and copies ran while one was open for 2% -> 7% of each run, Pallas kernels for 0% -> 0%
where the time goes in v1:
time: 155 us; the launch traced here: 153 us
  Pallas kernels  73.3 us (47%)
  waiting for transfers between devices  46 us (30%)
  starting transfers between devices  19.5 us (13%)
  local copies, waits for them, and re-layouts  7.88 us (5%)
  other arithmetic  5.97 us (4%)
    pallas_call x1, Pallas kernels, on_device_two(): pl.pallas_call(main_kernel, out_shape=jax.ShapeDtypeStruct((own, pixels),...  68.5 us
    all_to_all x1, waiting for transfers between devices, on_device_two(): lax.all_to_all(outgoing, 'swath', split_axis=0, concat_axis=0, tiled=True)  25.4 us
    ppermute x1, waiting for transfers between devices, on_device_two(): mid_oth = lax.ppermute(observed[:, rim:pixels - rim], 'chan', swap)  15.3 us
    all_to_all x1, starting transfers between devices, on_device_two(): lax.all_to_all(outgoing, 'swath', split_axis=0, concat_axis=0, tiled=True)  6.29 us
    ppermute x1, waiting for transfers between devices, on_device_two(): bnd_oth = lax.ppermute(bnd_own, 'chan', swap)  5.33 us
    pallas_call x1, Pallas kernels, gather_rows(): pl.pallas_call(gather_kernel, out_shape=jax.ShapeDtypeStruct((parts, slot...  4.83 us
  transfers between devices with their start and end apart: 9, of which 3 were waited for; matrix products, arithmetic and copies ran while one was open for 7% of the time, Pallas kernels for 0%

profile of v1, /device:TPU:16, one launch (start us, length us, event | category | flops | bytes accessed | tf_op | source)
XLA Modules:
  0.0 152.8 jit_solution(6554283644754214109)
XLA Ops:
  0.0 0.8 copy.9
  0.8 1.3 fusion.idx_ref
  2.1 4.8 %pick_rows.1 = bf16[16,256,256]{2,1,0:T(8,128)(2,1)} custom-call(s32[256,16]{1,0:T(8,128)} %fusion.idx_ref, bf16[1024,256]{1,0:T(8,128)(2,1)} %grid_ref.1), custom_call_target="tpu_custom_call" | custom-call | tf_op jit(solution)/shard_map/pick_rows/pallas_call | solution.py:94
  7.0 0.0 copy-start.7
  7.0 6.3 %all-to-all-start = ((bf16[16,256,256]{2,1,0:T(8,128)(2,1)}), bf16[16,256,256]{2,1,0:T(8,128)(2,1)S(1)}, u32[]{:S(2)}, u32[]{:S(2)}) async-start(bf16[16,256,256]{2,1,0:T(8,128)(2,1)} %pick_rows.1), calls=%async_computation | async-start | bytes 4194304 | tf_op jit(solution)/shard_map/all_to_all | solution.py:229
  13.3 0.0 copy-done.7
  13.3 1.6 %collective-permute-start.7 = (f32[2,304]{1,0:T(2,128)S(1)}, f32[2,304]{1,0:T(2,128)S(1)}, u32[]{:S(2)}, u32[]{:S(2)}) collective-permute-start(f32[2,304]{1,0:T(2,128)S(1)} %copy-done.7), channel_id=1, source_target_pairs={{0,1},{1,0},{2,3},{3,2},{4,5},{5,4},{6,7},{7,6},{8,9},{9,8},{10,11... | collective-permute-start | bytes 7304 | tf_op jit(solution)/shard_map/ppermute | solution.py:226
  14.8 1.1 fusion.4
  15.9 0.8 pad_maximum_fusion.2
  16.8 0.5 collective-permute-start.4
  17.3 0.0 copy-start.1
  17.3 0.0 copy-start.8
  17.3 1.5 collective-permute-start.2
  18.8 3.0 %slice.41 = bf16[304,3328]{1,0:T(8,128)(2,1)} slice(bf16[304,4096]{1,0:T(8,128)(2,1)} %obs_ref.1), slice={[0:304], [384:3712]} | slice | bytes 4046848 | tf_op jit(solution)/shard_map/slice | solution.py:225
  21.8 0.5 collective-permute-start.3
  22.3 0.1 pad.4.clone
  22.4 0.1 pad.5.clone
  22.5 0.0 copy-done.1
  22.5 0.1 fusion.7
  22.6 0.0 copy-done.8
  22.7 0.9 maximum_select_fusion.factor_ref
  23.6 0.7 maximum_maximum_fusion.rows_ref
  24.3 0.0 collective-permute-done.7
  24.3 0.1 fusion.3
  24.4 0.9 broadcast_multiply_fusion.1
  25.2 5.3 %collective-permute-done.4.bnd_ref = bf16[304,768]{1,0:T(8,128)(2,1)S(1)} collective-permute-done((bf16[304,768]{1,0:T(8,128)(2,1)}, bf16[304,768]{1,0:T(8,128)(2,1)S(1)}, u32[]{:S(2)}, u32[]{:S(2)}) %collective-permute-start.4) | collective-permute-done | bytes 466976 | tf_op jit(solution)/shard_map/ppermute | solution.py:224
  30.6 0.0 copy-start.2
  30.6 0.1 pad_maximum_fusion.1
  30.6 0.0 copy-start.3
  30.7 1.0 fusion.6
  31.7 0.0 copy-done.2
  31.7 1.9 %collective-permute-start.6 = (bf16[608,384]{1,0:T(8,128)(2,1)}, bf16[608,384]{1,0:T(8,128)(2,1)S(1)}, u32[]{:S(2)}, u32[]{:S(2)}) collective-permute-start(bf16[608,384]{1,0:T(8,128)(2,1)} %get-tuple-element.13), channel_id=1, source_target_pairs={{2,0},{4,2},{6,4},{8,6},{10,8},{12,10},{14,12},{16,14},{18,16},{20... | collective-permute-start | bytes 1400840 | tf_op jit(solution)/shard_map/ppermute | solution.py:236
  33.6 2.4 %collective-permute-start.5 = (bf16[608,384]{1,0:T(8,128)(2,1)}, bf16[608,384]{1,0:T(8,128)(2,1)}, u32[]{:S(2)}, u32[]{:S(2)}) collective-permute-start(bf16[608,384]{1,0:T(8,128)(2,1)} %get-tuple-element.14), channel_id=1, source_target_pairs={{0,2},{2,4},{4,6},{6,8},{8,10},{10,12},{12,14},{14,16},{16,18},{18... | collective-permute-start | bytes 1400840 | tf_op jit(solution)/shard_map/ppermute | solution.py:235
  36.0 25.4 %all-to-all-done = bf16[16,256,256]{2,1,0:T(8,128)(2,1)S(1)} async-done(((bf16[16,256,256]{2,1,0:T(8,128)(2,1)}), bf16[16,256,256]{2,1,0:T(8,128)(2,1)S(1)}, u32[]{:S(2)}, u32[]{:S(2)}) %all-to-all-start) | async-done | bytes 2097184 | tf_op jit(solution)/shard_map/all_to_all | solution.py:229
  61.4 0.0 copy-start
  61.4 2.8 %collective-permute-start.1 = (bf16[384,256]{1,0:T(8,128)(2,1)S(1)}, bf16[384,256]{1,0:T(8,128)(2,1)S(1)}, u32[]{:S(2)}, u32[]{:S(2)}) collective-permute-start(bf16[384,256]{1,0:T(8,128)(2,1)S(1)} %get-tuple-element.11), channel_id=1, source_target_pairs={{2,0},{4,2},{6,4},{8,6},{10,8},{12,10},{14,12},{16,14},{18,16},{20... | collective-permute-start | bytes 589832 | tf_op jit(solution)/shard_map/ppermute | solution.py:232
  64.3 0.0 collective-permute-done.2.jac_oth_ref
  64.3 1.9 %collective-permute-start = (bf16[384,256]{1,0:T(8,128)(2,1)S(1)}, bf16[384,256]{1,0:T(8,128)(2,1)S(1)}, u32[]{:S(2)}, u32[]{:S(2)}) collective-permute-start(bf16[384,256]{1,0:T(8,128)(2,1)S(1)} %get-tuple-element.12), channel_id=1, source_target_pairs={{0,2},{2,4},{4,6},{6,8},{8,10},{10,12},{12,14},{14,16},{16,18},{18... | collective-permute-start | bytes 589832 | tf_op jit(solution)/shard_map/ppermute | solution.py:231
  66.2 0.1 stack.26
  66.4 0.1 stack.27
  66.5 0.0 copy-done.3
  66.5 1.1 pad_maximum_fusion.rates_ref
  67.7 0.0 copy-done
  67.7 0.0 collective-permute-done.6.bot_ref
  67.7 0.0 copy-start.4
  67.7 0.0 collective-permute-done.5.top_ref
  67.7 15.3 %collective-permute-done.3.mid_ref = bf16[304,3328]{1,0:T(8,128)(2,1)} collective-permute-done((bf16[304,3328]{1,0:T(8,128)(2,1)}, bf16[304,3328]{1,0:T(8,128)(2,1)}, u32[]{:S(2)}, u32[]{:S(2)}) %collective-permute-start.3) | collective-permute-done | bytes 2023456 | tf_op jit(solution)/shard_map/ppermute | solution.py:225
  82.9 0.0 collective-permute-done.1.prof_bot_ref
  82.9 0.0 copy-start.5
  82.9 0.0 collective-permute-done.prof_top_ref
  83.0 0.0 copy-done.4
  83.0 0.7 copy-done.5
  83.6 0.0 copy-start.6
  83.6 0.7 copy-done.6
  84.3 68.5 %departures_sweeps_factor.1 = f32[304,4096]{1,0:T(8,128)} custom-call(bf16[4096,256]{1,0:T(8,128)(2,1)} %bitcast.15, bf16[384,256]{1,0:T(8,128)(2,1)} %copy-done.6, bf16[384,256]{1,0:T(8,128)(2,1)} %copy-done.5, bf16[3,304,256]{2,1,0:T(8,128)(2,1)} %bitcast.4.jac_own_ref, bf16[3,304,256]{2,1,0:T(8,128)(2,1)} %collective-permute-done.2.jac_oth_ref, ...), custom_call_target="tpu_custom_call" | custom-call | tf_op jit(solution)/shard_map/departures_sweeps_factor/pallas_call | solution.py:257
  (4 shorter events, 0.1 us)
Async XLA Ops:
  7.0 6.3 %copy-start.7 = (f32[2,304]{1,0:T(2,128)S(1)}, f32[2,304]{1,0:T(2,128)}, u32[]{:S(2)}) copy-start(f32[2,304]{1,0:T(2,128)} %param.14) | copy-start | bytes 7300
  7.0 54.4 %all-to-all-start = ((bf16[16,256,256]{2,1,0:T(8,128)(2,1)}), bf16[16,256,256]{2,1,0:T(8,128)(2,1)S(1)}, u32[]{:S(2)}, u32[]{:S(2)}) async-start(bf16[16,256,256]{2,1,0:T(8,128)(2,1)} %pick_rows.1), calls=%async_computation | async-start | bytes 4194304 | tf_op jit(solution)/shard_map/all_to_all | solution.py:229
  13.3 11.0 %collective-permute-start.7 = (f32[2,304]{1,0:T(2,128)S(1)}, f32[2,304]{1,0:T(2,128)S(1)}, u32[]{:S(2)}, u32[]{:S(2)}) collective-permute-start(f32[2,304]{1,0:T(2,128)S(1)} %copy-done.7), channel_id=1, source_target_pairs={{0,1},{1,0},{2,3},{3,2},{4,5},{5,4},{6,7},{7,6},{8,9},{9,8},{10,11... | collective-permute-start | bytes 7304 | tf_op jit(solution)/shard_map/ppermute | solution.py:226
  16.8 13.8 %collective-permute-start.4 = (bf16[304,768]{1,0:T(8,128)(2,1)}, bf16[304,768]{1,0:T(8,128)(2,1)S(1)}, u32[]{:S(2)}, u32[]{:S(2)}) collective-permute-start(bf16[304,768]{1,0:T(8,128)(2,1)} %pad_maximum_fusion.2), channel_id=1, source_target_pairs={{0,1},{1,0},{2,3},{3,2},{4,5},{5,4},{6,7},{7,6},{8,9},{9,8},{10,11... | collective-permute-start | bytes 1400840 | tf_op jit(solution)/shard_map/ppermute | solution.py:224
  17.3 5.2 %copy-start.1 = (bf16[304,608]{1,0:T(8,128)(2,1)S(1)}, bf16[304,608]{1,0:T(8,128)(2,1)}, u32[]{:S(2)}) copy-start(bf16[304,608]{1,0:T(8,128)(2,1)} %param.15) | copy-start | bytes 1108996
  17.3 5.3 %copy-start.8 = (s32[128]{0:T(128)S(1)}, s32[128]{0:T(128)}, u32[]{:S(2)}) copy-start(s32[128]{0:T(128)} %param.11) | copy-start | bytes 1540
  17.3 47.0 %collective-permute-start.2 = (bf16[3,304,256]{2,1,0:T(8,128)(2,1)}, bf16[3,304,256]{2,1,0:T(8,128)(2,1)}, u32[]{:S(2)}, u32[]{:S(2)}) collective-permute-start(bf16[3,304,256]{2,1,0:T(8,128)(2,1)} %bitcast.4.jac_own_ref), channel_id=1, source_target_pairs={{0,1},{1,0},{2,3},{3,2},{4,5},{5,4},{6,7},{7,6},{8,9},{9,8},{10,11... | collective-permute-start | bytes 1400840 | tf_op jit(solution)/shard_map/ppermute | solution.py:222
  21.8 61.1 %collective-permute-start.3 = (bf16[304,3328]{1,0:T(8,128)(2,1)}, bf16[304,3328]{1,0:T(8,128)(2,1)}, u32[]{:S(2)}, u32[]{:S(2)}) collective-permute-start(bf16[304,3328]{1,0:T(8,128)(2,1)} %slice.41), channel_id=1, source_target_pairs={{0,1},{1,0},{2,3},{3,2},{4,5},{5,4},{6,7},{7,6},{8,9},{9,8},{10,11... | collective-permute-start | bytes 6070280 | tf_op jit(solution)/shard_map/ppermute | solution.py:225
  30.6 1.1 copy-start.2
  30.6 35.9 %copy-start.3 = (f32[1,608,128]{2,1,0:T(8,128)S(1)}, f32[1,608,128]{2,1,0:T(8,128)}, u32[]{:S(2)}) copy-start(f32[1,608,128]{2,1,0:T(8,128)} %get-tuple-element.18) | copy-start | bytes 933892
  31.7 36.0 %collective-permute-start.6 = (bf16[608,384]{1,0:T(8,128)(2,1)}, bf16[608,384]{1,0:T(8,128)(2,1)S(1)}, u32[]{:S(2)}, u32[]{:S(2)}) collective-permute-start(bf16[608,384]{1,0:T(8,128)(2,1)} %get-tuple-element.13), channel_id=1, source_target_pairs={{2,0},{4,2},{6,4},{8,6},{10,8},{12,10},{14,12},{16,14},{18,16},{20... | collective-permute-start | bytes 1400840 | tf_op jit(solution)/shard_map/ppermute | solution.py:236
  33.6 34.1 %collective-permute-start.5 = (bf16[608,384]{1,0:T(8,128)(2,1)}, bf16[608,384]{1,0:T(8,128)(2,1)}, u32[]{:S(2)}, u32[]{:S(2)}) collective-permute-start(bf16[608,384]{1,0:T(8,128)(2,1)} %get-tuple-element.14), channel_id=1, source_target_pairs={{0,2},{2,4},{4,6},{6,8},{8,10},{10,12},{12,14},{14,16},{16,18},{18... | collective-permute-start | bytes 1400840 | tf_op jit(solution)/shard_map/ppermute | solution.py:235
  61.4 6.3 %copy-start = (bf16[16,256,256]{2,1,0:T(8,128)(2,1)}, bf16[16,256,256]{2,1,0:T(8,128)(2,1)S(1)}, u32[]{:S(2)}) copy-start(bf16[16,256,256]{2,1,0:T(8,128)(2,1)S(1)} %all-to-all-done) | copy-start | bytes 6291460
  61.4 21.5 %collective-permute-start.1 = (bf16[384,256]{1,0:T(8,128)(2,1)S(1)}, bf16[384,256]{1,0:T(8,128)(2,1)S(1)}, u32[]{:S(2)}, u32[]{:S(2)}) collective-permute-start(bf16[384,256]{1,0:T(8,128)(2,1)S(1)} %get-tuple-element.11), channel_id=1, source_target_pairs={{2,0},{4,2},{6,4},{8,6},{10,8},{12,10},{14,12},{16,14},{18,16},{20... | collective-permute-start | bytes 589832 | tf_op jit(solution)/shard_map/ppermute | solution.py:232
  64.3 18.7 %collective-permute-start = (bf16[384,256]{1,0:T(8,128)(2,1)S(1)}, bf16[384,256]{1,0:T(8,128)(2,1)S(1)}, u32[]{:S(2)}, u32[]{:S(2)}) collective-permute-start(bf16[384,256]{1,0:T(8,128)(2,1)S(1)} %get-tuple-element.12), channel_id=1, source_target_pairs={{0,2},{2,4},{4,6},{6,8},{8,10},{10,12},{12,14},{14,16},{16,18},{18... | collective-permute-start | bytes 589832 | tf_op jit(solution)/shard_map/ppermute | solution.py:231
  67.7 15.3 %copy-start.4 = (bf16[608,384]{1,0:T(8,128)(2,1)}, bf16[608,384]{1,0:T(8,128)(2,1)S(1)}, u32[]{:S(2)}) copy-start(bf16[608,384]{1,0:T(8,128)(2,1)S(1)} %collective-permute-done.6.bot_ref) | copy-start | bytes 1400836
  82.9 0.7 copy-start.5
  83.6 0.7 copy-start.6

commit v2 on v1

--- a/solution.py
+++ b/solution.py
@@ -3,6 +3,7 @@
 
 import jax
 import jax.numpy as jnp
+import numpy as np
 from jax import lax
 from jax.experimental import pallas as pl
 from jax.experimental.pallas import tpu as pltpu
@@ -11,6 +12,7 @@
 XTRACK = 128
 NANG = 8
 HALO = 3
+OUT_BLOCK = 1024
 VMEM_LIMIT = 60 * 1024 * 1024
 
 
@@ -100,91 +102,77 @@
 
 
 def main_kernel(
-    prof_ref, prof_top_ref, prof_bot_ref,
-    jac_own_ref, jac_oth_ref,
-    obs_ref, mid_ref, bnd_ref, top_ref, bot_ref,
-    rates_ref, rows_ref, factor_ref,
-    out_ref,
-    dep, smooth,
+    prof_hbm, prof_top_hbm, prof_bot_hbm, obs_hbm, mid_hbm, bnd_hbm, top_hbm, bot_hbm,
+    jac_own_ref, jac_oth_ref, rates_ref, rows_ref, shift_ref, factor_ref,
+    out_hbm,
+    prof, obs, field, smooth, out, sems, out_sems,
 ):
-    own = obs_ref.shape[0]
-    pixels = obs_ref.shape[1]
-    rim = top_ref.shape[1]
-    chans = 2 * own
+    own, pixels = obs_hbm.shape
+    rim = top_hbm.shape[1]
     lines = pixels // XTRACK
-    s1 = rows_ref[0:1, :]
-    s2 = rows_ref[1:2, :]
-
-    def model(jac, prof, obs, width):
+    wide = 2 * XTRACK
+    full = pixels + 2 * rim
+    mine, theirs = pl.ds(0, own), pl.ds(own, own)
+    copies = [
+        (prof_hbm, prof.at[pl.ds(rim, pixels), :]),
+        (prof_top_hbm, prof.at[pl.ds(0, rim), :]),
+        (prof_bot_hbm, prof.at[pl.ds(rim + pixels, rim), :]),
+        (obs_hbm, obs.at[mine, pl.ds(rim, pixels)]),
+        (top_hbm, obs.at[:, pl.ds(0, rim)]),
+        (bot_hbm, obs.at[:, pl.ds(rim + pixels, rim)]),
+        (mid_hbm, obs.at[theirs, pl.ds(2 * rim, pixels - 2 * rim)]),
+        (bnd_hbm.at[:, pl.ds(0, rim)], obs.at[theirs, pl.ds(rim, rim)]),
+        (bnd_hbm.at[:, pl.ds(rim, rim)], obs.at[theirs, pl.ds(pixels, rim)]),
+    ]
+    copies = [pltpu.make_async_copy(src, dst, sems.at[n]) for n, (src, dst) in enumerate(copies)]
+    for copy in copies:
+        copy.start()
+    s1 = jnp.concatenate([rows_ref[0:1, :]] * 2, axis=1)
+    s2 = jnp.concatenate([rows_ref[1:2, :]] * 2, axis=1)
+    inside_top = rows_ref[2:3, :]
+    inside_bot = rows_ref[3:4, :]
+    shift = shift_ref[...]
+
+    def departures(part, jac, t):
+        at = pl.multiple_of(t * wide, wide)
+        here = prof[pl.ds(at, wide), :]
         terms = [
-            lax.dot_general(
-                jac[m], prof, (((1,), (1,)), ((), ())), preferred_element_type=jnp.float32
-            )
+            lax.dot_general(jac[m], here, (((1,), (1,)), ((), ())), preferred_element_type=jnp.float32)
             for m in range(3)
         ]
-        t1 = jnp.concatenate([s1] * (width // XTRACK), axis=1)
-        t2 = jnp.concatenate([s2] * (width // XTRACK), axis=1)
-        return obs.astype(jnp.float32) - (terms[0] + t1 * terms[1] + t2 * terms[2])
-
-    for part, jac in enumerate((jac_own_ref, jac_oth_ref)):
-        chan = slice(part * own, (part + 1) * own)
-        dep[chan, 0:rim] = model(jac, prof_top_ref[...], top_ref[chan, :], rim)
-        dep[chan, rim + pixels : pixels + 2 * rim] = model(jac, prof_bot_ref[...], bot_ref[chan, :], rim)
-
-    wide = 2 * XTRACK
-
-    def own_block(t, carry):
-        at = pl.multiple_of(t * wide, wide)
-        dep[0:own, pl.ds(pl.multiple_of(rim + at, XTRACK), wide)] = model(
-            jac_own_ref, prof_ref[pl.ds(at, wide), :], obs_ref[:, pl.ds(at, wide)], wide
+        dep = obs[pl.ds(part * own, own), pl.ds(at, wide)].astype(jnp.float32) - (
+            terms[0] + s1 * terms[1] + s2 * terms[2]
         )
-        return carry
-
-    lax.fori_loop(0, pixels // wide, own_block, 0)
-
-    dep[own:chans, rim : 2 * rim] = model(jac_oth_ref, prof_ref[0:rim, :], bnd_ref[:, 0:rim], rim)
-    dep[own:chans, pixels : pixels + rim] = model(
-        jac_oth_ref, prof_ref[pixels - rim : pixels, :], bnd_ref[:, rim : 2 * rim], rim
-    )
-
-    def other_block(t, carry):
-        at = pl.multiple_of(t * wide, wide)
-        dep[own:chans, pl.ds(pl.multiple_of(2 * rim + at, XTRACK), wide)] = model(
-            jac_oth_ref, prof_ref[pl.ds(pl.multiple_of(rim + at, XTRACK), wide), :],
-            mid_ref[:, pl.ds(at, wide)], wide
-        )
-        return carry
-
-    lax.fori_loop(0, (pixels - 2 * rim) // wide, other_block, 0)
-
-    inside_top = rows_ref[2:3, :]
-    inside_bot = rows_ref[3:4, :]
-    total = lines + 2 * HALO
-
-    def diffuse(i, carry):
-        chan = pl.ds(pl.multiple_of(i * 16, 16), 16)
-        along = rates_ref[0, chan, :]
-        left = rates_ref[1, chan, :]
-        right = rates_ref[2, chan, :]
-        stay = rates_ref[3, chan, :]
-
-        def sweep(before, here, after):
-            return (
-                stay * here
-                + along * (before + after)
-                + left * pltpu.roll(here, 1, 1)
-                + right * pltpu.roll(here, XTRACK - 1, 1)
-            )
-
+        field[0, :, pl.ds(at, wide)] = dep
+        high = dep.astype(jnp.bfloat16)
+        low = (dep - high.astype(jnp.float32)).astype(jnp.bfloat16)
+        for n in range(2):
+            lanes = slice(n * XTRACK, (n + 1) * XTRACK)
+            pair = jnp.concatenate([high[:, lanes], low[:, lanes]], axis=1)
+            moved = jnp.dot(pair, shift, preferred_element_type=jnp.float32)
+            for k in range(HALO):
+                field[k + 1, :, pl.ds(pl.multiple_of(at + n * XTRACK, XTRACK), XTRACK)] = moved[
+                    :, k * XTRACK : (k + 1) * XTRACK
+                ]
+
+    def sweeps(part, i):
+        rows = pl.ds(pl.multiple_of(i * 16, 16), 16)
+        chan = pl.ds(pl.multiple_of(part * own + i * 16, 16), 16)
+        stay, along = rates_ref[0, chan, :], rates_ref[1, chan, :]
+        cross = [rates_ref[2 + k, chan, :] for k in range(HALO)]
         fields = [{}, {}, {}, {}]
-        for j in range(total):
-            fields[0][j] = dep[chan, j * XTRACK : (j + 1) * XTRACK]
+        for j in range(lines + 2 * HALO):
+            fields[0][j] = field[0, rows, j * XTRACK : (j + 1) * XTRACK]
             for k in range(1, HALO + 1):
                 at = j - k
                 if at < k:
                     continue
                 prev = fields[k - 1]
-                new = sweep(prev[at - 1], prev[at], prev[at + 1])
+                new = (
+                    stay * prev[at]
+                    + along * (prev[at - 1] + prev[at + 1])
+                    + cross[k - 1] * field[k, rows, at * XTRACK : (at + 1) * XTRACK]
+                )
                 if at < HALO:
                     new = new * inside_top
                 if at >= HALO + lines:
@@ -194,19 +182,29 @@
                 if k == HALO:
                     line = at - HALO
                     smooth[chan, line * XTRACK : (line + 1) * XTRACK] = new.astype(smooth.dtype)
-        return carry
-
-    lax.fori_loop(0, chans // 16, diffuse, 0)
-
-    def factor_block(t, carry):
-        at = pl.multiple_of(t * wide, wide)
-        out_ref[:, pl.ds(at, wide)] = jnp.dot(
-            factor_ref[...], smooth[:, pl.ds(at, wide)], preferred_element_type=jnp.float32
+
+    for part, jac in enumerate((jac_own_ref, jac_oth_ref)):
+        for copy in copies[:6] if part == 0 else copies[6:]:
+            copy.wait()
+        pl.loop(0, full // wide, unroll=4)(functools.partial(departures, part, jac))
+        pl.loop(0, own // 16)(functools.partial(sweeps, part))
+
+    def out_copy(t):
+        at = pl.multiple_of(t * OUT_BLOCK, OUT_BLOCK)
+        return pltpu.make_async_copy(
+            out.at[:, pl.ds(at, OUT_BLOCK)], out_hbm.at[:, pl.ds(at, OUT_BLOCK)], out_sems.at[t]
         )
-        return carry
-
-    lax.fori_loop(0, pixels // wide, factor_block, 0)
-
+
+    def weigh(t):
+        at = pl.multiple_of(t * OUT_BLOCK, OUT_BLOCK)
+        out[:, pl.ds(at, OUT_BLOCK)] = jnp.dot(
+            factor_ref[...], smooth[:, pl.ds(at, OUT_BLOCK)], preferred_element_type=jnp.float32
+        )
+        out_copy(t).start()
+
+    blocks = pixels // (OUT_BLOCK)
+    pl.loop(0, blocks)(weigh)
+    pl.loop(0, blocks)(lambda t: out_copy(t).wait())
 
 def on_device_two(grid_profiles, send_lists, counts, angle_index, jacobian, observed, kappa, factor):
     own, pixels = observed.shape
@@ -218,12 +216,20 @@
     forward = [(i, i + 1) for i in range(swath - 1)]
     backward = [(i + 1, i) for i in range(swath - 1)]
 
-    jac_own = jnp.swapaxes(jacobian, 1, 2)
-    jac_oth = lax.ppermute(jac_own, "chan", swap)
     bnd_own = jnp.concatenate([observed[:, :rim], observed[:, pixels - rim :]], axis=1)
     bnd_oth = lax.ppermute(bnd_own, "chan", swap)
-    mid_oth = lax.ppermute(observed[:, rim : pixels - rim], "chan", swap)
+    jac_own = jnp.swapaxes(jacobian, 1, 2)
+    jac_half = lax.dynamic_slice_in_dim(jac_own, (place % 2) * (own // 2), own // 2, axis=1)
+    jac_near = lax.ppermute(jac_half, "chan", swap)
+    jac_far = lax.ppermute(jac_near, "swath", [(i, i ^ 1) for i in range(swath)])
+    jac_oth = jnp.where(
+        place % 2 == 0,
+        jnp.concatenate([jac_near, jac_far], axis=1),
+        jnp.concatenate([jac_far, jac_near], axis=1),
+    )
     kappa_oth = lax.ppermute(kappa, "chan", swap)
+    bnd_held, middle = lax.optimization_barrier((bnd_own, observed[:, rim : pixels - rim]))
+    mid_oth = lax.ppermute(middle, "chan", swap)
 
     outgoing = gather_rows(grid_profiles, send_lists[0], counts[0])
     incoming = lax.all_to_all(outgoing, "swath", split_axis=0, concat_axis=0, tiled=True)
@@ -231,20 +237,23 @@
     prof_top = lax.ppermute(profiles[pixels - rim :], "swath", forward)
     prof_bot = lax.ppermute(profiles[:rim], "swath", backward)
 
-    both = jnp.concatenate([bnd_own, bnd_oth], axis=0)
+    both = jnp.concatenate([bnd_held, bnd_oth], axis=0)
     obs_top = lax.ppermute(both[:, rim:], "swath", forward)
     obs_bot = lax.ppermute(both[:, :rim], "swath", backward)
 
     rate = jnp.concatenate([kappa, kappa_oth], axis=1)[:, :, None]
-    lane = jnp.arange(XTRACK, dtype=jnp.int32)[None, :]
     along, cross = rate[0], rate[1]
     ones = jnp.ones((1, XTRACK), jnp.float32)
     rates = jnp.stack([
+        (1.0 - 2.0 * along - 2.0 * cross) * ones,
         along * ones,
-        cross * (lane > 0),
-        cross * (lane < XTRACK - 1),
-        (1.0 - 2.0 * along - 2.0 * cross) * ones,
+        3.0 * cross * ones,
+        3.0 * cross * cross * ones,
+        cross * cross * cross * ones,
     ])
+    near = np.eye(XTRACK, k=1) + np.eye(XTRACK, k=-1)
+    moves = np.concatenate([near, near @ near, near @ near @ near], axis=1)
+    shift = jnp.asarray(np.concatenate([moves, moves], axis=0), jnp.bfloat16)
     slant = slant_of(angle_index)
     rows = jnp.stack([
         slant,
@@ -254,19 +263,26 @@
     ])
     factor_two = jnp.where(half == 0, factor, jnp.roll(factor, own, axis=1))
 
+    full = pixels + 2 * rim
     return pl.pallas_call(
         main_kernel,
         out_shape=jax.ShapeDtypeStruct((own, pixels), jnp.float32),
+        in_specs=[pl.BlockSpec(memory_space=pl.ANY)] * 8 + [pl.BlockSpec(memory_space=pltpu.VMEM)] * 6,
+        out_specs=pl.BlockSpec(memory_space=pl.ANY),
         scratch_shapes=[
-            pltpu.VMEM((2 * own, pixels + 2 * rim), jnp.float32),
+            pltpu.VMEM((full, profiles.shape[1]), jnp.bfloat16),
+            pltpu.VMEM((2 * own, full), jnp.bfloat16),
+            pltpu.VMEM((HALO + 1, own, full), jnp.float32),
             pltpu.VMEM((2 * own, pixels), jnp.bfloat16),
+            pltpu.VMEM((own, pixels), jnp.float32),
+            pltpu.SemaphoreType.DMA((9,)),
+            pltpu.SemaphoreType.DMA((pixels // OUT_BLOCK,)),
         ],
         compiler_params=pltpu.CompilerParams(vmem_limit_bytes=VMEM_LIMIT),
         name="departures_sweeps_factor",
     )(
-        profiles, prof_top, prof_bot, jac_own, jac_oth,
-        observed, mid_oth, bnd_oth, obs_top, obs_bot,
-        rates, rows, factor_two,
+        profiles, prof_top, prof_bot, observed, mid_oth, bnd_oth, obs_top, obs_bot,
+        jac_own, jac_oth, rates, rows, shift, factor_two,
     )
 
 

time: 155 us -> 113 us (0.73)
  Pallas kernels: 73.3 us -> 38.2 us
  waiting for transfers between devices: 46 us -> 34.7 us
  local copies, waits for them, and re-layouts: 7.88 us -> 13 us
    pallas_call x1, Pallas kernels: 68.5 us -> 33.4 us  [on_device_two(): pl.pallas_call(main_kernel, out_shape=jax.ShapeDtypeStruct((own, pixels),...]
    ppermute x2 -> x3, waiting for transfers between devices: 15.3 us -> 7.47 us  [the longest x1 7.47 us: on_device_two(): mid_oth = lax.ppermute(middle, 'chan', swap)]
    all_to_all x1, waiting for transfers between devices: 25.4 us -> 20.6 us  [on_device_two(): lax.all_to_all(outgoing, 'swath', split_axis=0, concat_axis=0, tiled=True)]
    unnamed x19 -> x24, local copies, waits for them, and re-layouts: 2.18 us -> 5.07 us
    select_n x0 -> x1, other arithmetic: none -> 2.2 us  [on_device_two(): jnp.where(place % 2 == 0, jnp.concatenate([jac_near, jac_far], axis=1), j...]
  transfers between devices with their start and end apart: 9 -> 10, of which waited for: 3 -> 3; matrix products, arithmetic and copies ran while one was open for 7% -> 14% of each run, Pallas kernels for 0% -> 0%
where the time goes in v2:
time: 113 us; the launch traced here: 111 us
  Pallas kernels  38.2 us (34%)
  waiting for transfers between devices  34.7 us (31%)
  starting transfers between devices  19.5 us (17%)
  local copies, waits for them, and re-layouts  13 us (12%)
  other arithmetic  5.32 us (5%)
    pallas_call x1, Pallas kernels, on_device_two(): pl.pallas_call(main_kernel, out_shape=jax.ShapeDtypeStruct((own, pixels),...  33.4 us
    all_to_all x1, waiting for transfers between devices, on_device_two(): lax.all_to_all(outgoing, 'swath', split_axis=0, concat_axis=0, tiled=True)  20.6 us
    ppermute x1, waiting for transfers between devices, on_device_two(): mid_oth = lax.ppermute(middle, 'chan', swap)  7.47 us
    ppermute x1, waiting for transfers between devices, on_device_two(): bnd_oth = lax.ppermute(bnd_own, 'chan', swap)  6.52 us
    all_to_all x1, starting transfers between devices, on_device_two(): lax.all_to_all(outgoing, 'swath', split_axis=0, concat_axis=0, tiled=True)  6.29 us
    unnamed x24, local copies, waits for them, and re-layouts  5.07 us
    pallas_call x1, Pallas kernels, gather_rows(): pl.pallas_call(gather_kernel, out_shape=jax.ShapeDtypeStruct((parts, slot...  4.83 us
    slice x1, local copies, waits for them, and re-layouts, on_device_two(): observed[:, rim:pixels - rim]  3 us
  transfers between devices with their start and end apart: 10, of which 3 were waited for; matrix products, arithmetic and copies ran while one was open for 14% of the time, Pallas kernels for 0%

profile of v2, /device:TPU:16, one launch (start us, length us, event | category | flops | bytes accessed | tf_op | source)
XLA Modules:
  0.0 110.9 jit_solution(13504659557276553853)
XLA Ops:
  0.0 0.8 copy.10
  0.8 1.3 %fusion.idx_ref = s32[256,16]{1,0:T(8,128)} fusion(s32[1,16,256]{1,2,0:T(8,128)S(1)} %copy.10, s32[16]{0:T(128)} %bitcast.19), kind=kLoop, calls=%fused_computation.10 | loop fusion | flops 8192 | bytes 32832 | tf_op jit(solution)/shard_map/transpose | solution.py:95
  2.1 4.8 %pick_rows.1 = bf16[16,256,256]{2,1,0:T(8,128)(2,1)} custom-call(s32[256,16]{1,0:T(8,128)} %fusion.idx_ref, bf16[1024,256]{1,0:T(8,128)(2,1)} %grid_ref.1), custom_call_target="tpu_custom_call" | custom-call | tf_op jit(solution)/shard_map/pick_rows/pallas_call | solution.py:96
  7.0 0.0 copy-start.7
  7.0 0.0 copy-start.2
  7.0 6.3 %all-to-all-start = ((bf16[16,256,256]{2,1,0:T(8,128)(2,1)}), bf16[16,256,256]{2,1,0:T(8,128)(2,1)S(1)}, u32[]{:S(2)}, u32[]{:S(2)}) async-start(bf16[16,256,256]{2,1,0:T(8,128)(2,1)} %pick_rows.1), calls=%async_computation | async-start | bytes 4194304 | tf_op jit(solution)/shard_map/all_to_all | solution.py:235
  13.3 0.0 copy-done.7
  13.3 1.6 %collective-permute-start.8 = (f32[2,304]{1,0:T(2,128)S(1)}, f32[2,304]{1,0:T(2,128)S(1)}, u32[]{:S(2)}, u32[]{:S(2)}) collective-permute-start(f32[2,304]{1,0:T(2,128)S(1)} %copy-done.7), channel_id=1, source_target_pairs={{0,1},{1,0},{2,3},{3,2},{4,5},{5,4},{6,7},{7,6},{8,9},{9,8},{10,11... | collective-permute-start | bytes 7304 | tf_op jit(solution)/shard_map/ppermute | solution.py:230
  14.8 0.0 copy-done.2
  14.8 0.7 dynamic-slice_bitcast_fusion
  15.6 0.5 collective-permute-start.6
  16.1 1.1 fusion.5
  17.2 0.0 copy-start.8
  17.3 0.0 copy-start.1
  17.3 1.6 %collective-permute-start.3 = (bf16[304,768]{1,0:T(8,128)(2,1)S(1)}, bf16[304,768]{1,0:T(8,128)(2,1)}, u32[]{:S(2)}, u32[]{:S(2)}) collective-permute-start(bf16[304,768]{1,0:T(8,128)(2,1)S(1)} %pad_maximum_fusion), channel_id=1, source_target_pairs={{0,1},{1,0},{2,3},{3,2},{4,5},{5,4},{6,7},{7,6},{8,9},{9,8},{10,11... | collective-permute-start | bytes 1400840 | tf_op jit(solution)/shard_map/ppermute | solution.py:220
  18.9 3.0 %slice.41 = bf16[304,3328]{1,0:T(8,128)(2,1)} slice(bf16[304,4096]{1,0:T(8,128)(2,1)} %obs_hbm.1), slice={[0:304], [384:3712]} | slice | bytes 4046848 | tf_op jit(solution)/shard_map/slice | solution.py:231
  21.8 0.5 collective-permute-start.2
  22.4 0.1 pad.4.clone
  22.4 0.1 pad.5.clone
  22.5 0.0 copy-done.8
  22.6 0.7 maximum_maximum_fusion.rows_ref
  23.2 0.0 copy-done.1
  23.2 0.1 fusion.8
  23.4 0.9 maximum_select_fusion.1.factor_ref
  24.4 0.0 collective-permute-done.8
  24.4 0.1 fusion.3
  24.5 0.9 broadcast_dynamic-update-slice_fusion.4
  25.3 0.9 broadcast_dynamic-update-slice_fusion.3
  26.2 0.9 broadcast_dynamic-update-slice_fusion.2
  27.1 0.9 broadcast_dynamic-update-slice_fusion.1
  27.9 0.0 collective-permute-done.6
  28.0 0.0 collective-permute-start.7
  28.0 6.5 %collective-permute-done.3.bnd_hbm = bf16[304,768]{1,0:T(8,128)(2,1)} collective-permute-done((bf16[304,768]{1,0:T(8,128)(2,1)S(1)}, bf16[304,768]{1,0:T(8,128)(2,1)}, u32[]{:S(2)}, u32[]{:S(2)}) %collective-permute-start.3) | collective-permute-done | bytes 466976 | tf_op jit(solution)/shard_map/ppermute | solution.py:220
  34.5 1.1 constant_dynamic-update-slice_fusion
  35.5 0.9 fusion.7
  36.4 1.9 %collective-permute-start.5 = (bf16[608,384]{1,0:T(8,128)(2,1)}, bf16[608,384]{1,0:T(8,128)(2,1)S(1)}, u32[]{:S(2)}, u32[]{:S(2)}) collective-permute-start(bf16[608,384]{1,0:T(8,128)(2,1)} %get-tuple-element.17), channel_id=1, source_target_pairs={{2,0},{4,2},{6,4},{8,6},{10,8},{12,10},{14,12},{16,14},{18,16},{20... | collective-permute-start | bytes 1400840 | tf_op jit(solution)/shard_map/ppermute | solution.py:242
  38.4 2.4 %collective-permute-start.4 = (bf16[608,384]{1,0:T(8,128)(2,1)S(1)}, bf16[608,384]{1,0:T(8,128)(2,1)S(1)}, u32[]{:S(2)}, u32[]{:S(2)}) collective-permute-start(bf16[608,384]{1,0:T(8,128)(2,1)S(1)} %get-tuple-element.18), channel_id=1, source_target_pairs={{0,2},{2,4},{4,6},{6,8},{8,10},{10,12},{12,14},{14,16},{16,18},{18... | collective-permute-start | bytes 1400840 | tf_op jit(solution)/shard_map/ppermute | solution.py:241
  40.8 20.6 %all-to-all-done = bf16[16,256,256]{2,1,0:T(8,128)(2,1)S(1)} async-done(((bf16[16,256,256]{2,1,0:T(8,128)(2,1)}), bf16[16,256,256]{2,1,0:T(8,128)(2,1)S(1)}, u32[]{:S(2)}, u32[]{:S(2)}) %all-to-all-start) | async-done | bytes 2097184 | tf_op jit(solution)/shard_map/all_to_all | solution.py:235
  61.4 0.0 copy-start
  61.5 2.8 %collective-permute-start.1 = (bf16[384,256]{1,0:T(8,128)(2,1)S(1)}, bf16[384,256]{1,0:T(8,128)(2,1)S(1)}, u32[]{:S(2)}, u32[]{:S(2)}) collective-permute-start(bf16[384,256]{1,0:T(8,128)(2,1)S(1)} %get-tuple-element.15), channel_id=1, source_target_pairs={{2,0},{4,2},{6,4},{8,6},{10,8},{12,10},{14,12},{16,14},{18,16},{20... | collective-permute-start | bytes 589832 | tf_op jit(solution)/shard_map/ppermute | solution.py:238
  64.2 0.0 collective-permute-done.7
  64.2 1.9 %collective-permute-start = (bf16[384,256]{1,0:T(8,128)(2,1)S(1)}, bf16[384,256]{1,0:T(8,128)(2,1)S(1)}, u32[]{:S(2)}, u32[]{:S(2)}) collective-permute-start(bf16[384,256]{1,0:T(8,128)(2,1)S(1)} %get-tuple-element.16), channel_id=1, source_target_pairs={{0,2},{2,4},{4,6},{6,8},{8,10},{10,12},{12,14},{14,16},{16,18},{18... | collective-permute-start | bytes 589832 | tf_op jit(solution)/shard_map/ppermute | solution.py:237
  66.2 0.9 broadcast_dynamic-update-slice_fusion.rates_ref
  67.0 2.2 %maximum_select_fusion.jac_oth_ref = bf16[3,304,256]{2,1,0:T(8,128)(2,1)} fusion(bf16[3,152,256]{2,1,0:T(8,128)(2,1)} %collective-permute-done.7, bf16[3,152,256]{2,1,0:T(8,128)(2,1)} %collective-permute-done.6, pred[]{:T(512)S(6)} %eq.9), kind=kLoop, calls=%fused_computation.1 | loop fusion | flops 2101248 | bytes 933889 | tf_op jit(solution)/shard_map/jit(_where)/select_n | solution.py:225
  69.2 0.0 collective-permute-done.5.bot_hbm
  69.2 0.0 copy-start.3
  69.2 0.0 collective-permute-done.4.top_hbm
  69.3 0.0 copy-start.4
  69.3 7.5 %collective-permute-done.2.mid_hbm = bf16[304,3328]{1,0:T(8,128)(2,1)} collective-permute-done((bf16[304,3328]{1,0:T(8,128)(2,1)}, bf16[304,3328]{1,0:T(8,128)(2,1)}, u32[]{:S(2)}, u32[]{:S(2)}) %collective-permute-start.2) | collective-permute-done | bytes 2023456 | tf_op jit(solution)/shard_map/ppermute | solution.py:232
  76.7 0.0 collective-permute-done.1.prof_bot_hbm
  76.7 0.0 copy-start.5
  76.7 0.0 collective-permute-done.prof_top_hbm
  76.7 0.0 copy-start.6
  76.8 0.0 copy-done
  76.8 0.0 copy-done.3
  76.8 0.0 copy-done.4
  76.8 0.6 copy-done.5
  77.4 0.1 copy-done.6
  77.5 33.4 %departures_sweeps_factor.1 = f32[304,4096]{1,0:T(8,128)} custom-call(bf16[4096,256]{1,0:T(8,128)(2,1)} %bitcast.17, bf16[384,256]{1,0:T(8,128)(2,1)} %copy-done.6, bf16[384,256]{1,0:T(8,128)(2,1)} %copy-done.5, bf16[304,4096]{1,0:T(8,128)(2,1)} %obs_hbm.1, bf16[304,3328]{1,0:T(8,128)(2,1)} %collective-permute-done.2.mid_hbm, ...), custom_call_target="tpu_custom_call" | custom-call | tf_op jit(solution)/shard_map/departures_sweeps_factor/pallas_call | solution.py:267
  (5 shorter events, 0.1 us)
Async XLA Ops:
  7.0 6.3 %copy-start.7 = (f32[2,304]{1,0:T(2,128)S(1)}, f32[2,304]{1,0:T(2,128)}, u32[]{:S(2)}) copy-start(f32[2,304]{1,0:T(2,128)} %param.15) | copy-start | bytes 7300
  7.0 7.9 %copy-start.2 = (bf16[3,256,304]{1,2,0:T(8,128)(2,1)S(1)}, bf16[3,256,304]{1,2,0:T(8,128)(2,1)}, u32[]{:S(2)}) copy-start(bf16[3,256,304]{1,2,0:T(8,128)(2,1)} %param.13) | copy-start | bytes 1400836
  7.0 54.5 %all-to-all-start = ((bf16[16,256,256]{2,1,0:T(8,128)(2,1)}), bf16[16,256,256]{2,1,0:T(8,128)(2,1)S(1)}, u32[]{:S(2)}, u32[]{:S(2)}) async-start(bf16[16,256,256]{2,1,0:T(8,128)(2,1)} %pick_rows.1), calls=%async_computation | async-start | bytes 4194304 | tf_op jit(solution)/shard_map/all_to_all | solution.py:235
  13.3 11.1 %collective-permute-start.8 = (f32[2,304]{1,0:T(2,128)S(1)}, f32[2,304]{1,0:T(2,128)S(1)}, u32[]{:S(2)}, u32[]{:S(2)}) collective-permute-start(f32[2,304]{1,0:T(2,128)S(1)} %copy-done.7), channel_id=1, source_target_pairs={{0,1},{1,0},{2,3},{3,2},{4,5},{5,4},{6,7},{7,6},{8,9},{9,8},{10,11... | collective-permute-start | bytes 7304 | tf_op jit(solution)/shard_map/ppermute | solution.py:230
  15.6 12.4 %collective-permute-start.6 = (bf16[3,152,256]{2,1,0:T(8,128)(2,1)}, bf16[3,152,256]{2,1,0:T(8,128)(2,1)}, u32[]{:S(2)}, u32[]{:S(2)}) collective-permute-start(bf16[3,152,256]{2,1,0:T(8,128)(2,1)} %dynamic-slice_bitcast_fusion), channel_id=1, source_target_pairs={{0,1},{1,0},{2,3},{3,2},{4,5},{5,4},{6,7},{7,6},{8,9},{9,8},{10,11... | collective-permute-start | bytes 700424 | tf_op jit(solution)/shard_map/ppermute | solution.py:223
  17.2 5.3 %copy-start.8 = (s32[128]{0:T(128)S(1)}, s32[128]{0:T(128)}, u32[]{:S(2)}) copy-start(s32[128]{0:T(128)} %param.12) | copy-start | bytes 1540
  17.3 6.0 %copy-start.1 = (bf16[304,608]{1,0:T(8,128)(2,1)S(1)}, bf16[304,608]{1,0:T(8,128)(2,1)}, u32[]{:S(2)}) copy-start(bf16[304,608]{1,0:T(8,128)(2,1)} %param.16) | copy-start | bytes 1108996
  17.3 17.2 %collective-permute-start.3 = (bf16[304,768]{1,0:T(8,128)(2,1)S(1)}, bf16[304,768]{1,0:T(8,128)(2,1)}, u32[]{:S(2)}, u32[]{:S(2)}) collective-permute-start(bf16[304,768]{1,0:T(8,128)(2,1)S(1)} %pad_maximum_fusion), channel_id=1, source_target_pairs={{0,1},{1,0},{2,3},{3,2},{4,5},{5,4},{6,7},{7,6},{8,9},{9,8},{10,11... | collective-permute-start | bytes 1400840 | tf_op jit(solution)/shard_map/ppermute | solution.py:220
  21.8 54.9 %collective-permute-start.2 = (bf16[304,3328]{1,0:T(8,128)(2,1)}, bf16[304,3328]{1,0:T(8,128)(2,1)}, u32[]{:S(2)}, u32[]{:S(2)}) collective-permute-start(bf16[304,3328]{1,0:T(8,128)(2,1)} %slice.41), channel_id=1, source_target_pairs={{0,1},{1,0},{2,3},{3,2},{4,5},{5,4},{6,7},{7,6},{8,9},{9,8},{10,11... | collective-permute-start | bytes 6070280 | tf_op jit(solution)/shard_map/ppermute | solution.py:232
  28.0 36.3 %collective-permute-start.7 = (bf16[3,152,256]{2,1,0:T(8,128)(2,1)}, bf16[3,152,256]{2,1,0:T(8,128)(2,1)}, u32[]{:S(2)}, u32[]{:S(2)}) collective-permute-start(bf16[3,152,256]{2,1,0:T(8,128)(2,1)} %collective-permute-done.6), channel_id=1, source_target_pairs={{0,2},{2,0},{4,6},{6,4},{8,10},{10,8},{12,14},{14,12},{16,18},{18,... | collective-permute-start | bytes 700424 | tf_op jit(solution)/shard_map/ppermute | solution.py:224
  36.4 32.8 %collective-permute-start.5 = (bf16[608,384]{1,0:T(8,128)(2,1)}, bf16[608,384]{1,0:T(8,128)(2,1)S(1)}, u32[]{:S(2)}, u32[]{:S(2)}) collective-permute-start(bf16[608,384]{1,0:T(8,128)(2,1)} %get-tuple-element.17), channel_id=1, source_target_pairs={{2,0},{4,2},{6,4},{8,6},{10,8},{12,10},{14,12},{16,14},{18,16},{20... | collective-permute-start | bytes 1400840 | tf_op jit(solution)/shard_map/ppermute | solution.py:242
  38.4 30.9 %collective-permute-start.4 = (bf16[608,384]{1,0:T(8,128)(2,1)S(1)}, bf16[608,384]{1,0:T(8,128)(2,1)S(1)}, u32[]{:S(2)}, u32[]{:S(2)}) collective-permute-start(bf16[608,384]{1,0:T(8,128)(2,1)S(1)} %get-tuple-element.18), channel_id=1, source_target_pairs={{0,2},{2,4},{4,6},{6,8},{8,10},{10,12},{12,14},{14,16},{16,18},{18... | collective-permute-start | bytes 1400840 | tf_op jit(solution)/shard_map/ppermute | solution.py:241
  61.4 15.3 %copy-start = (bf16[16,256,256]{2,1,0:T(8,128)(2,1)}, bf16[16,256,256]{2,1,0:T(8,128)(2,1)S(1)}, u32[]{:S(2)}) copy-start(bf16[16,256,256]{2,1,0:T(8,128)(2,1)S(1)} %all-to-all-done) | copy-start | bytes 6291460
  61.5 15.3 %collective-permute-start.1 = (bf16[384,256]{1,0:T(8,128)(2,1)S(1)}, bf16[384,256]{1,0:T(8,128)(2,1)S(1)}, u32[]{:S(2)}, u32[]{:S(2)}) collective-permute-start(bf16[384,256]{1,0:T(8,128)(2,1)S(1)} %get-tuple-element.15), channel_id=1, source_target_pairs={{2,0},{4,2},{6,4},{8,6},{10,8},{12,10},{14,12},{16,14},{18,16},{20... | collective-permute-start | bytes 589832 | tf_op jit(solution)/shard_map/ppermute | solution.py:238
  64.2 12.5 %collective-permute-start = (bf16[384,256]{1,0:T(8,128)(2,1)S(1)}, bf16[384,256]{1,0:T(8,128)(2,1)S(1)}, u32[]{:S(2)}, u32[]{:S(2)}) collective-permute-start(bf16[384,256]{1,0:T(8,128)(2,1)S(1)} %get-tuple-element.16), channel_id=1, source_target_pairs={{0,2},{2,4},{4,6},{6,8},{8,10},{10,12},{12,14},{14,16},{16,18},{18... | collective-permute-start | bytes 589832 | tf_op jit(solution)/shard_map/ppermute | solution.py:237
  69.2 7.5 %copy-start.3 = (bf16[608,384]{1,0:T(8,128)(2,1)}, bf16[608,384]{1,0:T(8,128)(2,1)S(1)}, u32[]{:S(2)}) copy-start(bf16[608,384]{1,0:T(8,128)(2,1)S(1)} %collective-permute-done.5.bot_hbm) | copy-start | bytes 1400836
  69.3 7.5 %copy-start.4 = (bf16[608,384]{1,0:T(8,128)(2,1)}, bf16[608,384]{1,0:T(8,128)(2,1)S(1)}, u32[]{:S(2)}) copy-start(bf16[608,384]{1,0:T(8,128)(2,1)S(1)} %collective-permute-done.4.top_hbm) | copy-start | bytes 1400836
  76.7 0.7 copy-start.5
  76.7 0.8 copy-start.6

commit v3 on v2

v3 whole, which is shorter than its diff:
```python
import functools
import math

import jax
import jax.numpy as jnp
import numpy as np
from jax import lax
from jax.experimental import pallas as pl
from jax.experimental.pallas import tpu as pltpu
from jax.sharding import PartitionSpec as P

XTRACK = 128
NANG = 8
HALO = 3
OUT_BLOCK = 1024
GATHER_LIMIT = 24 * 1024 * 1024
VMEM_LIMIT = 60 * 1024 * 1024


max_zenith = math.pi / 3.0


def extended_2(block, sides, width):
    for axis, dim in sides:
        count = lax.axis_size(axis)
        forward = [(i, i + 1) for i in range(count - 1)]
        backward = [(target, source) for source, target in forward]
        low = lax.ppermute(
            lax.slice_in_dim(block, block.shape[dim] - width, None, axis=dim), axis, forward
        )
        high = lax.ppermute(lax.slice_in_dim(block, 0, width, axis=dim), axis, backward)
        block = jnp.concatenate([low, block, high], axis=dim)
    return block


def diffuse_once(extended, along_rate, cross_rate):
    center = extended[:, 1:-1]
    along_sum = extended[:, 2:] + extended[:, :-2] - 2.0 * center
    side_pad = jnp.pad(center, ((0, 0), (0, 0), (1, 1)))
    cross_sum = side_pad[:, :, 2:] + side_pad[:, :, :-2] - 2.0 * center
    return center + along_rate * along_sum + cross_rate * cross_sum


def line_rims(smooth_field):
    return extended_2(smooth_field, (("swath", 1),), 1)


def slant_of(angle_index):
    zenith = angle_index.astype(jnp.float32) * (max_zenith / (NANG - 1))
    return 1.0 / jnp.cos(zenith) - 1.0


def on_device_plain(grid_profiles, send_lists, counts, angle_index, jacobian, observed, kappa, factor):
    slot_rows = send_lists[0]
    slots = slot_rows.shape[1]
    own_chan = observed.shape[0]
    pixel_count = observed.shape[1]
    line_count = pixel_count // XTRACK
    live_slot = jnp.arange(slots, dtype=jnp.int32)[None, :] < counts[0][:, None]
    zero_value = jnp.zeros((), grid_profiles.dtype)
    outgoing = jnp.where(live_slot[:, :, None], grid_profiles[slot_rows], zero_value)
    incoming = lax.all_to_all(outgoing, "swath", split_axis=0, concat_axis=0, tiled=True)
    pixel_profiles = incoming.reshape(pixel_count, grid_profiles.shape[1])
    model = jnp.einsum("mkc,pk->mcp", jacobian, pixel_profiles, preferred_element_type=jnp.float32)
    slant_path = slant_of(angle_index)
    model = model.reshape(3, own_chan, line_count, XTRACK)
    departure = observed.astype(jnp.float32).reshape(own_chan, line_count, XTRACK) - (
        model[0] + slant_path * model[1] + slant_path * slant_path * model[2]
    )
    along_rate = kappa[0][:, None, None]
    cross_rate = kappa[1][:, None, None]
    smooth_field = departure
    for sweep in range(3):
        smooth_field = diffuse_once(line_rims(smooth_field), along_rate, cross_rate)
    smoothed = smooth_field.reshape(own_chan, pixel_count).astype(jnp.bfloat16)
    return jnp.dot(
        factor,
        lax.all_gather(smoothed, "chan", axis=0, tiled=True),
        preferred_element_type=jnp.float32,
    )


def gather_kernel(lists_ref, counts_ref, grid_ref, out_ref):
    grid_rows = grid_ref.shape[0]
    parts, slots = lists_ref.shape
    slot_number = lax.broadcasted_iota(jnp.int32, (slots, parts), 0)
    picks = jnp.where(slot_number < counts_ref[...], lists_ref[...].T, -1)
    row_number = lax.broadcasted_iota(jnp.int32, (slots, grid_rows), 1)
    for part in range(parts):
        one_hot = (picks[:, part : part + 1] == row_number).astype(jnp.float32).astype(jnp.bfloat16)
        rows = jnp.dot(one_hot, grid_ref[...], preferred_element_type=jnp.float32)
        out_ref[part] = rows.astype(out_ref.dtype)


def gather_rows(grid_profiles, slot_rows, counts):
    parts, slots = slot_rows.shape
    return pl.pallas_call(
        gather_kernel,
        out_shape=jax.ShapeDtypeStruct((parts, slots, grid_profiles.shape[1]), grid_profiles.dtype),
        compiler_params=pltpu.CompilerParams(vmem_limit_bytes=GATHER_LIMIT),
        name="pick_rows",
    )(slot_rows, counts, grid_profiles)


def half_kernel(last, *refs):
    prof_hbm, prof_top_hbm, prof_bot_hbm, top_hbm, bot_hbm = refs[:5]
    if last:
        mid_hbm, bnd_hbm, smooth_hbm, jac_ref, rates_ref, rows_ref, shift_ref, factor_ref = refs[5:13]
        out_hbm, prof, obs, field, moved_a, moved_b, sems, smooth, out, out_sems = refs[13:]
    else:
        obs_hbm, jac_ref, rates_ref, rows_ref, shift_ref = refs[5:10]
        smooth, prof, obs, field, moved_a, moved_b, sems = refs[10:]
    own, pixels = jac_ref.shape[1], prof_hbm.shape[0]
    rim = prof_top_hbm.shape[0]
    lines = pixels // XTRACK
    wide = 2 * XTRACK
    full = pixels + 2 * rim
    total = full // XTRACK
    first = own if last else 0

    part = pl.ds(first, own)
    copies = [
        (prof_top_hbm, prof.at[pl.ds(0, rim), :]),
        (top_hbm.at[part, :], obs.at[:, pl.ds(0, rim)]),
        (prof_hbm, prof.at[pl.ds(rim, pixels), :]),
        (prof_bot_hbm, prof.at[pl.ds(rim + pixels, rim), :]),
        (bot_hbm.at[part, :], obs.at[:, pl.ds(rim + pixels, rim)]),
    ]
    if last:
        copies += [
            (bnd_hbm.at[:, pl.ds(0, rim)], obs.at[:, pl.ds(rim, rim)]),
            (mid_hbm, obs.at[:, pl.ds(2 * rim, pixels - 2 * rim)]),
            (bnd_hbm.at[:, pl.ds(rim, rim)], obs.at[:, pl.ds(pixels, rim)]),
            (smooth_hbm, smooth.at[pl.ds(0, own), :]),
        ]
    else:
        copies.append((obs_hbm, obs.at[:, pl.ds(rim, pixels)]))
    copies = [pltpu.make_async_copy(src, dst, sems.at[n]) for n, (src, dst) in enumerate(copies)]
    for copy in copies:
        copy.start()
    s1 = jnp.concatenate([rows_ref[0:1, :]] * 2, axis=1)
    s2 = jnp.concatenate([rows_ref[1:2, :]] * 2, axis=1)
    inside_top = rows_ref[2:3, :]
    inside_bot = rows_ref[3:4, :]

    def departures(t):
        at = pl.multiple_of(t * wide, wide)
        here = prof[pl.ds(at, wide), :]
        terms = [
            lax.dot_general(jac_ref[m], here, (((1,), (1,)), ((), ())), preferred_element_type=jnp.float32)
            for m in range(3)
        ]
        field[:, pl.ds(at, wide)] = obs[:, pl.ds(at, wide)].astype(jnp.float32) - (
            terms[0] + s1 * terms[1] + s2 * terms[2]
        )

    def shifts(i, moved):
        rows = pl.ds(pl.multiple_of(i * 16, 16), 16)
        tiles = []
        for j in range(total):
            here = field[rows, j * XTRACK : (j + 1) * XTRACK]
            high = here.astype(jnp.bfloat16)
            low = (here - high.astype(jnp.float32)).astype(jnp.bfloat16)
            tiles.append(jnp.concatenate([high, low], axis=1))
        moved[...] = jnp.dot(
            jnp.concatenate(tiles, axis=0), shift_ref[...], preferred_element_type=jnp.float32
        )

    def sweeps(i, moved):
        rows = pl.ds(pl.multiple_of(i * 16, 16), 16)
        chan = pl.ds(pl.multiple_of(first + i * 16, 16), 16)
        along = jnp.broadcast_to(rates_ref[rows, 0:1], (16, XTRACK))
        cross = jnp.broadcast_to(rates_ref[rows, 1:2], (16, XTRACK))
        stay = 1.0 - 2.0 * along - 2.0 * cross
        cross = [3.0 * cross, 3.0 * cross * cross, cross * cross * cross]
        fields = [{}, {}, {}, {}]
        for j in range(total):
            fields[0][j] = field[rows, j * XTRACK : (j + 1) * XTRACK]
            for k in range(1, HALO + 1):
                at = j - k
                if at < k:
                    continue
                prev = fields[k - 1]
                new = (
                    stay * prev[at]
                    + along * (prev[at - 1] + prev[at + 1])
                    + cross[k - 1] * moved[at * 16 : (at + 1) * 16, (k - 1) * XTRACK : k * XTRACK]
                )
                if at < HALO:
                    new = new * inside_top
                if at >= HALO + lines:
                    new = new * inside_bot
                fields[k][at] = new
                del prev[at - 1]
                if k == HALO:
                    line = at - HALO
                    smooth[chan, line * XTRACK : (line + 1) * XTRACK] = new.astype(smooth.dtype)

    for copy in copies[:8]:
        copy.wait()
    pl.loop(0, total // 2, unroll=4)(departures)

    groups = own // 16
    shifts(0, moved_a)

    @pl.loop(0, groups // 2)
    def _(h):
        shifts(2 * h + 1, moved_b)
        sweeps(2 * h, moved_a)
        shifts(jnp.minimum(2 * h + 2, groups - 1), moved_a)
        sweeps(2 * h + 1, moved_b)

    if groups % 2:
        sweeps(groups - 1, moved_a)

    if not last:
        return
    copies[8].wait()

    def out_copy(t):
        at = pl.multiple_of(t * OUT_BLOCK, OUT_BLOCK)
        return pltpu.make_async_copy(
            out.at[:, pl.ds(at, OUT_BLOCK)], out_hbm.at[:, pl.ds(at, OUT_BLOCK)], out_sems.at[t]
        )

    @pl.loop(0, pixels // OUT_BLOCK)
    def _(t):
        at = pl.multiple_of(t * OUT_BLOCK, OUT_BLOCK)
        out[:, pl.ds(at, OUT_BLOCK)] = jnp.dot(
            factor_ref[...], smooth[:, pl.ds(at, OUT_BLOCK)], preferred_element_type=jnp.float32
        )
        out_copy(t).start()

    pl.loop(0, pixels // OUT_BLOCK)(lambda t: out_copy(t).wait())


def half_call(last, anys, whole):
    own, pixels = whole[0].shape[1], anys[0].shape[0]
    rim = anys[1].shape[0]
    full = pixels + 2 * rim
    scratch = [
        pltpu.VMEM((full, anys[0].shape[1]), jnp.bfloat16),
        pltpu.VMEM((own, full), jnp.bfloat16),
        pltpu.VMEM((own, full), jnp.float32),
        pltpu.VMEM((16 * (full // XTRACK), HALO * XTRACK), jnp.float32),
        pltpu.VMEM((16 * (full // XTRACK), HALO * XTRACK), jnp.float32),
        pltpu.SemaphoreType.DMA((9,)),
    ]
    if last:
        out_shape = jax.ShapeDtypeStruct((own, pixels), jnp.float32)
        out_spec = pl.BlockSpec(memory_space=pl.ANY)
        scratch += [
            pltpu.VMEM((2 * own, pixels), jnp.bfloat16),
            pltpu.VMEM((own, pixels), jnp.float32),
            pltpu.SemaphoreType.DMA((pixels // OUT_BLOCK,)),
        ]
    else:
        out_shape = jax.ShapeDtypeStruct((own, pixels), jnp.bfloat16)
        out_spec = pl.BlockSpec(memory_space=pltpu.VMEM)
    return pl.pallas_call(
        functools.partial(half_kernel, last),
        out_shape=out_shape,
        in_specs=[pl.BlockSpec(memory_space=pl.ANY)] * len(anys)
        + [pl.BlockSpec(memory_space=pltpu.VMEM)] * len(whole),
        out_specs=out_spec,
        scratch_shapes=scratch,
        compiler_params=pltpu.CompilerParams(vmem_limit_bytes=VMEM_LIMIT),
        cost_estimate=None if last else pl.CostEstimate(flops=1, bytes_accessed=1, transcendentals=0),
        name="other_half_and_factor" if last else "own_half",
    )(*anys, *whole)


def on_device_two(grid_profiles, send_lists, counts, angle_index, jacobian, observed, kappa, factor):
    own, pixels = observed.shape
    rim = HALO * XTRACK
    swath = lax.axis_size("swath")
    place = lax.axis_index("swath")
    half = lax.axis_index("chan")
    swap = [(0, 1), (1, 0)]
    forward = [(i, i + 1) for i in range(swath - 1)]
    backward = [(i + 1, i) for i in range(swath - 1)]

    def halos(block, axis):
        size = block.shape[axis]
        tail = lax.slice_in_dim(block, size - rim, size, axis=axis)
        head = lax.slice_in_dim(block, 0, rim, axis=axis)
        return lax.ppermute(tail, "swath", forward), lax.ppermute(head, "swath", backward)

    jac_own = jnp.swapaxes(jacobian, 1, 2)
    jac_half = lax.dynamic_slice_in_dim(jac_own, (place % 2) * (own // 2), own // 2, axis=1)
    jac_near = lax.ppermute(jac_half, "chan", swap)
    rates_own = kappa.T
    rates_oth = lax.ppermute(rates_own, "chan", swap)
    bnd_own = jnp.concatenate([observed[:, :rim], observed[:, pixels - rim :]], axis=1)
    bnd_oth = lax.ppermute(bnd_own, "chan", swap)
    outgoing = gather_rows(grid_profiles, send_lists[0], counts)
    outgoing, obs_late, bnd_own = lax.optimization_barrier((outgoing, observed, bnd_own))
    incoming = lax.all_to_all(outgoing, "swath", split_axis=0, concat_axis=0, tiled=True)
    middle = obs_late[:, rim : pixels - rim]
    middle, jac_near, bnd_oth = lax.optimization_barrier((middle, jac_near, bnd_oth))
    mid_oth = lax.ppermute(middle, "chan", swap)
    jac_far = lax.ppermute(jac_near, "swath", [(i, i ^ 1) for i in range(swath)])
    jac_oth = jnp.where(
        place % 2 == 0,
        jnp.concatenate([jac_near, jac_far], axis=1),
        jnp.concatenate([jac_far, jac_near], axis=1),
    )
    near = np.eye(XTRACK, k=1) + np.eye(XTRACK, k=-1)
    moves = np.concatenate([near, near @ near, near @ near @ near], axis=1)
    shift = jnp.asarray(np.concatenate([moves, moves], axis=0), jnp.bfloat16)
    slant = slant_of(angle_index)
    ones = jnp.ones((XTRACK,), jnp.float32)
    rows = jnp.stack([
        slant,
        slant * slant,
        jnp.where(place > 0, ones, 0.0),
        jnp.where(place < swath - 1, ones, 0.0),
    ])
    factor_two = jnp.where(half == 0, factor, jnp.roll(factor, own, axis=1))

    bnd_own, bnd_oth, jac_oth, rates_oth, rows, factor_two = lax.optimization_barrier(
        (bnd_own, bnd_oth, jac_oth, rates_oth, rows, factor_two)
    )
    bnd_both = jnp.concatenate([bnd_own, bnd_oth], axis=0)
    obs_top = lax.ppermute(bnd_both[:, rim:], "swath", forward)
    obs_bot = lax.ppermute(bnd_both[:, :rim], "swath", backward)

    profiles = incoming.reshape(pixels, grid_profiles.shape[1])
    prof_halos = halos(profiles, 0)

    smooth_own = half_call(
        False, (profiles, *prof_halos, obs_top, obs_bot, observed), (jac_own, rates_own, rows, shift)
    )
    return half_call(
        True,
        (profiles, *prof_halos, obs_top, obs_bot, mid_oth, bnd_oth, smooth_own),
        (jac_oth, rates_oth, rows, shift, factor_two),
    )


def solution(mesh):
    in_specs = (
        P("swath", None),
        P("swath", None, None),
        P("swath", None),
        P(),
        P(None, None, "chan"),
        P("chan", "swath"),
        P(None, "chan"),
        P("chan", None),
    )
    out_specs = P("chan", "swath")
    on_device = on_device_two if mesh.shape["chan"] == 2 else on_device_plain
    return jax.shard_map(
        on_device, mesh=mesh, in_specs=in_specs, out_specs=out_specs, check_vma=False
    )
```

time: 113 us -> 106 us (0.938); the launches traced: 111 us -> 105 us
  local copies, waits for them, and re-layouts: 13 us -> 9.13 us
  Pallas kernels: 38.2 us -> 36.5 us
  other arithmetic: 5.32 us -> 3.67 us
  starting transfers between devices: 19.5 us -> 21.1 us
    ppermute x1, waiting for transfers between devices: 0.01 us -> 10.5 us  [on_device_two(): jac_near = lax.ppermute(jac_half, 'chan', swap)]
    ppermute x1, waiting for transfers between devices: 7.47 us -> 0.01 us  [on_device_two(): mid_oth = lax.ppermute(middle, 'chan', swap)]
    ppermute x1, waiting for transfers between devices: 6.52 us -> 0.01 us  [on_device_two(): bnd_oth = lax.ppermute(bnd_own, 'chan', swap)]
    ppermute x5, waiting for transfers between devices: 0.01 us -> 5.92 us  [the longest x1 4.68 us: halos(): lax.ppermute(tail, 'swath', forward)]
    all_to_all x1, waiting for transfers between devices: 20.6 us -> 17.3 us  [on_device_two(): lax.all_to_all(outgoing, 'swath', split_axis=0, concat_axis=0, tiled=True)]
    unnamed x24 -> x28, local copies, waits for them, and re-layouts: 5.07 us -> 2.98 us
    transpose x1 -> x0, other arithmetic: 1.32 us -> none  [gather_rows(): picks = jnp.where(live_slot, slot_rows, -1).T]
    pallas_call x1 -> x2, Pallas kernels: 33.4 us -> 32.6 us  [half_call(): pl.pallas_call(functools.partial(half_kernel, last), out_shape=out_shape,...]
  transfers between devices with their start and end apart: 10 -> 10, of which waited for: 3 -> 5; matrix products, arithmetic and copies ran while one was open for 14% -> 9% of each run, Pallas kernels for 0% -> 14%
where the time goes in v3:
time: 106 us; the launch traced here: 105 us
  Pallas kernels  36.5 us (34%)
  waiting for transfers between devices  34.5 us (33%)
  starting transfers between devices  21.1 us (20%)
  local copies, waits for them, and re-layouts  9.13 us (9%)
  other arithmetic  3.67 us (3%)
    pallas_call x2, Pallas kernels, half_call(): pl.pallas_call(functools.partial(half_kernel, last), out_shape=out_shape,...  32.6 us
    all_to_all x1, waiting for transfers between devices, on_device_two(): lax.all_to_all(outgoing, 'swath', split_axis=0, concat_axis=0, tiled=True)  17.3 us
    ppermute x1, waiting for transfers between devices, on_device_two(): jac_near = lax.ppermute(jac_half, 'chan', swap)  10.5 us
    all_to_all x1, starting transfers between devices, on_device_two(): lax.all_to_all(outgoing, 'swath', split_axis=0, concat_axis=0, tiled=True)  6.29 us
    ppermute x1, waiting for transfers between devices, halos(): lax.ppermute(tail, 'swath', forward)  4.68 us
    pallas_call x1, Pallas kernels, gather_rows(): pl.pallas_call(gather_kernel, out_shape=jax.ShapeDtypeStruct((parts, slot...  3.9 us
    ppermute x1, starting transfers between devices, on_device_two(): obs_bot = lax.ppermute(bnd_both[:, :rim], 'swath', backward)  3.1 us
    slice x1, local copies, waits for them, and re-layouts, on_device_two(): middle = obs_late[:, rim:pixels - rim]  3.04 us
  transfers between devices with their start and end apart: 10, of which 5 were waited for; matrix products, arithmetic and copies ran while one was open for 9% of the time, Pallas kernels for 14%

profile of v3, /device:TPU:16, one launch (start us, length us, event | category | flops | bytes accessed | tf_op | source)
XLA Modules:
  0.0 105.1 jit_solution(11590545268921202336)
XLA Ops:
  0.0 0.0 copy-start
  0.0 1.2 %fusion = (bf16[304,384]{1,0:T(8,128)(2,1)S(1)}, bf16[304,384]{1,0:T(8,128)(2,1)S(1)}) fusion(bf16[304,4096]{1,0:T(8,128)(2,1)} %refs_5_.1), kind=kLoop, calls=%fused_computation.9 | loop fusion | bytes 933888 | tf_op jit(solution)/shard_map/slice | solution.py:294
  1.2 0.1 copy-done
  1.3 0.0 copy-start.1
  1.3 0.7 copy-done.1
  2.0 0.0 copy-start.2
  2.0 0.7 copy-done.2
  2.6 3.9 %pick_rows.1 = bf16[16,256,256]{2,1,0:T(8,128)(2,1)} custom-call(s32[16,256]{1,0:T(8,128)S(1)} %bitcast.11, s32[1,16]{1,0:T(1,128)S(1)} %copy-done.2, bf16[1024,256]{1,0:T(8,128)(2,1)S(1)} %copy-done), custom_call_target="tpu_custom_call" | custom-call | tf_op jit(solution)/shard_map/pick_rows/pallas_call | solution.py:97
  6.5 0.0 copy-start.8
  6.5 0.0 copy-start.11
  6.5 6.3 %all-to-all-start = ((bf16[16,256,256]{2,1,0:T(8,128)(2,1)}), bf16[16,256,256]{2,1,0:T(8,128)(2,1)S(1)}, u32[]{:S(2)}, u32[]{:S(2)}) async-start(bf16[16,256,256]{2,1,0:T(8,128)(2,1)} %pick_rows.1), calls=%async_computation | async-start | bytes 4194304 | tf_op jit(solution)/shard_map/all_to_all | solution.py:298
  12.8 1.5 %collective-permute-start.3 = (bf16[304,768]{1,0:T(8,128)(2,1)S(1)}, bf16[304,768]{1,0:T(8,128)(2,1)S(1)}, u32[]{:S(2)}, u32[]{:S(2)}) collective-permute-start(bf16[304,768]{1,0:T(8,128)(2,1)S(1)} %pad_maximum_fusion), channel_id=1, source_target_pairs={{0,1},{1,0},{2,3},{3,2},{4,5},{5,4},{6,7},{7,6},{8,9},{9,8},{10,11... | collective-permute-start | bytes 1400840 | tf_op jit(solution)/shard_map/ppermute | solution.py:295
  14.4 0.0 copy-done.8
  14.4 0.7 dynamic-slice_bitcast_fusion
  15.1 0.0 copy-start.4
  15.1 0.5 collective-permute-start.2
  15.6 0.0 copy-done.11
  15.6 0.8 copy.10
  16.4 1.5 %collective-permute-start.5 = (f32[304,2]{1,0:T(8,128)}, f32[304,2]{1,0:T(8,128)}, u32[]{:S(2)}, u32[]{:S(2)}) collective-permute-start(f32[304,2]{1,0:T(8,128)} %bitcast.16), channel_id=1, source_target_pairs={{0,1},{1,0},{2,3},{3,2},{4,5},{5,4},{6,7},{7,6},{8,9},{9,8},{10,11... | collective-permute-start | bytes 7304 | tf_op jit(solution)/shard_map/ppermute | solution.py:293
  17.9 3.0 %slice.33 = bf16[304,3328]{1,0:T(8,128)(2,1)} slice(bf16[304,4096]{1,0:T(8,128)(2,1)} %refs_5_.1), slice={[0:304], [384:3712]} | slice | bytes 4046848 | tf_op jit(solution)/shard_map/slice | solution.py:299
  21.0 0.0 copy-start.12
  21.0 10.5 %collective-permute-done.2 = bf16[3,152,256]{2,1,0:T(8,128)(2,1)} collective-permute-done((bf16[3,152,256]{2,1,0:T(8,128)(2,1)}, bf16[3,152,256]{2,1,0:T(8,128)(2,1)}, u32[]{:S(2)}, u32[]{:S(2)}) %collective-permute-start.2) | collective-permute-done | bytes 233504 | tf_op jit(solution)/shard_map/ppermute | solution.py:291
  31.5 0.0 collective-permute-done.3.refs_6_
  31.5 0.0 copy-start.7
  31.5 1.5 %collective-permute-start.8 = (bf16[304,3328]{1,0:T(8,128)(2,1)}, bf16[304,3328]{1,0:T(8,128)(2,1)}, u32[]{:S(2)}, u32[]{:S(2)}) collective-permute-start(bf16[304,3328]{1,0:T(8,128)(2,1)} %slice.33), channel_id=1, source_target_pairs={{0,1},{1,0},{2,3},{3,2},{4,5},{5,4},{6,7},{7,6},{8,9},{9,8},{10,11... | collective-permute-start | bytes 6070280 | tf_op jit(solution)/shard_map/ppermute | solution.py:301
  33.0 0.0 copy-done.4
  33.0 0.1 fusion.3
  33.1 1.0 maximum_select_fusion.1.refs_12_
  34.1 0.0 collective-permute-start.4
  34.1 0.0 copy-done.12
  34.2 0.1 pad.4.clone
  34.3 0.1 pad.5.clone
  34.3 0.7 maximum_maximum_fusion.refs_8_.refs_10_
  35.0 0.8 collective-permute-done.4
  35.8 2.0 %maximum_select_fusion.refs_8_ = bf16[3,304,256]{2,1,0:T(8,128)(2,1)} fusion(bf16[3,152,256]{2,1,0:T(8,128)(2,1)S(1)} %collective-permute-done.4, bf16[3,152,256]{2,1,0:T(8,128)(2,1)} %collective-permute-done.2, pred[]{:T(512)S(6)} %eq.9), kind=kLoop, calls=%fused_computation.1 | loop fusion | flops 2101248 | bytes 933889 | tf_op jit(solution)/shard_map/jit(_where)/select_n | solution.py:303
  37.8 0.0 collective-permute-done.5.refs_9_
  37.9 0.0 copy-done.7
  37.9 0.9 fusion.2
  38.8 3.1 %collective-permute-start.7 = (bf16[608,384]{1,0:T(8,128)(2,1)}, bf16[608,384]{1,0:T(8,128)(2,1)S(1)}, u32[]{:S(2)}, u32[]{:S(2)}) collective-permute-start(bf16[608,384]{1,0:T(8,128)(2,1)} %get-tuple-element.35), channel_id=1, source_target_pairs={{2,0},{4,2},{6,4},{8,6},{10,8},{12,10},{14,12},{16,14},{18,16},{20... | collective-permute-start | bytes 1400840 | tf_op jit(solution)/shard_map/ppermute | solution.py:326
  41.9 1.9 %collective-permute-start.6 = (bf16[608,384]{1,0:T(8,128)(2,1)S(1)}, bf16[608,384]{1,0:T(8,128)(2,1)S(1)}, u32[]{:S(2)}, u32[]{:S(2)}) collective-permute-start(bf16[608,384]{1,0:T(8,128)(2,1)S(1)} %get-tuple-element.36), channel_id=1, source_target_pairs={{0,2},{2,4},{4,6},{6,8},{8,10},{10,12},{12,14},{14,16},{16,18},{18... | collective-permute-start | bytes 1400840 | tf_op jit(solution)/shard_map/ppermute | solution.py:325
  43.8 17.3 %all-to-all-done = bf16[16,256,256]{2,1,0:T(8,128)(2,1)S(1)} async-done(((bf16[16,256,256]{2,1,0:T(8,128)(2,1)}), bf16[16,256,256]{2,1,0:T(8,128)(2,1)S(1)}, u32[]{:S(2)}, u32[]{:S(2)}) %all-to-all-start) | async-done | bytes 2097184 | tf_op jit(solution)/shard_map/all_to_all | solution.py:298
  61.0 0.0 copy-start.3
  61.1 2.8 %collective-permute-start.1 = (bf16[384,256]{1,0:T(8,128)(2,1)S(1)}, bf16[384,256]{1,0:T(8,128)(2,1)S(1)}, u32[]{:S(2)}, u32[]{:S(2)}) collective-permute-start(bf16[384,256]{1,0:T(8,128)(2,1)S(1)} %get-tuple-element.33), channel_id=1, source_target_pairs={{2,0},{4,2},{6,4},{8,6},{10,8},{12,10},{14,12},{16,14},{18,16},{20... | collective-permute-start | bytes 589832 | tf_op jit(solution)/shard_map/ppermute | solution.py:287
  63.9 1.9 %collective-permute-start = (bf16[384,256]{1,0:T(8,128)(2,1)S(1)}, bf16[384,256]{1,0:T(8,128)(2,1)S(1)}, u32[]{:S(2)}, u32[]{:S(2)}) collective-permute-start(bf16[384,256]{1,0:T(8,128)(2,1)S(1)} %get-tuple-element.34), channel_id=1, source_target_pairs={{0,2},{2,4},{4,6},{6,8},{8,10},{10,12},{12,14},{14,16},{16,18},{18... | collective-permute-start | bytes 589832 | tf_op jit(solution)/shard_map/ppermute | solution.py:287
  65.8 0.0 collective-permute-done.7.refs_4_
  65.8 0.0 copy-start.5
  65.8 0.0 collective-permute-done.6.refs_3_
  65.8 0.0 copy-start.6
  65.8 1.2 %collective-permute-done.1.refs_2_ = bf16[384,256]{1,0:T(8,128)(2,1)S(1)} collective-permute-done((bf16[384,256]{1,0:T(8,128)(2,1)S(1)}, bf16[384,256]{1,0:T(8,128)(2,1)S(1)}, u32[]{:S(2)}, u32[]{:S(2)}) %collective-permute-start.1) | collective-permute-done | bytes 196640 | tf_op jit(solution)/shard_map/ppermute | solution.py:287
  67.1 0.0 copy-start.9
  67.1 4.7 %collective-permute-done.refs_1_ = bf16[384,256]{1,0:T(8,128)(2,1)S(1)} collective-permute-done((bf16[384,256]{1,0:T(8,128)(2,1)S(1)}, bf16[384,256]{1,0:T(8,128)(2,1)S(1)}, u32[]{:S(2)}, u32[]{:S(2)}) %collective-permute-start) | collective-permute-done | bytes 196640 | tf_op jit(solution)/shard_map/ppermute | solution.py:287
  71.7 0.0 copy-start.10
  71.8 0.0 copy-done.3
  71.8 0.0 copy-done.5
  71.8 0.0 copy-done.6
  71.8 0.0 copy-done.9
  71.8 0.7 copy-done.10
  72.4 15.2 %own_half.1.refs_7_ = bf16[304,4096]{1,0:T(8,128)(2,1)} custom-call(bf16[4096,256]{1,0:T(8,128)(2,1)} %bitcast.13, bf16[384,256]{1,0:T(8,128)(2,1)} %copy-done.10, bf16[384,256]{1,0:T(8,128)(2,1)} %copy-done.9, bf16[608,384]{1,0:T(8,128)(2,1)} %copy-done.6, bf16[608,384]{1,0:T(8,128)(2,1)} %copy-done.5, bf16[304,4096]{1,0:T(8,128)(2,1)} %refs_5_.1, ...), custom_call_target="tpu_custom_call" | custom-call | flops 1 | bytes 1 | tf_op jit(solution)/shard_map/own_half/pallas_call | solution.py:260
  87.6 0.0 collective-permute-done.8.refs_5_
  87.6 17.5 %other_half_and_factor.1 = f32[304,4096]{1,0:T(8,128)} custom-call(bf16[4096,256]{1,0:T(8,128)(2,1)} %bitcast.14, bf16[384,256]{1,0:T(8,128)(2,1)} %copy-done.10, bf16[384,256]{1,0:T(8,128)(2,1)} %copy-done.9, bf16[608,384]{1,0:T(8,128)(2,1)} %copy-done.6, bf16[608,384]{1,0:T(8,128)(2,1)} %copy-done.5, bf16[304,3328]{1,0:T(8,128)(2,1)} %collective-permute-done.8.refs_5_, ...), custom_call_target="tpu_custom_call" | custom-call | tf_op jit(solution)/shard_map/other_half_and_factor/pallas_call | solution.py:260
  (5 shorter events, 0.2 us)
Async XLA Ops:
  0.0 1.3 %copy-start = (bf16[1024,256]{1,0:T(8,128)(2,1)S(1)}, bf16[1024,256]{1,0:T(8,128)(2,1)}, u32[]{:S(2)}) copy-start(bf16[1024,256]{1,0:T(8,128)(2,1)} %grid_ref.1) | copy-start | bytes 1572868
  1.3 0.7 copy-start.1
  2.0 0.7 copy-start.2
  6.5 7.8 %copy-start.8 = (bf16[3,256,304]{1,2,0:T(8,128)(2,1)S(1)}, bf16[3,256,304]{1,2,0:T(8,128)(2,1)}, u32[]{:S(2)}) copy-start(bf16[3,256,304]{1,2,0:T(8,128)(2,1)} %param.13) | copy-start | bytes 1400836
  6.5 9.1 %copy-start.11 = (f32[2,304]{1,0:T(2,128)S(1)}, f32[2,304]{1,0:T(2,128)}, u32[]{:S(2)}) copy-start(f32[2,304]{1,0:T(2,128)} %param.15) | copy-start | bytes 7300
  6.5 54.5 %all-to-all-start = ((bf16[16,256,256]{2,1,0:T(8,128)(2,1)}), bf16[16,256,256]{2,1,0:T(8,128)(2,1)S(1)}, u32[]{:S(2)}, u32[]{:S(2)}) async-start(bf16[16,256,256]{2,1,0:T(8,128)(2,1)} %pick_rows.1), calls=%async_computation | async-start | bytes 4194304 | tf_op jit(solution)/shard_map/all_to_all | solution.py:298
  12.8 18.7 %collective-permute-start.3 = (bf16[304,768]{1,0:T(8,128)(2,1)S(1)}, bf16[304,768]{1,0:T(8,128)(2,1)S(1)}, u32[]{:S(2)}, u32[]{:S(2)}) collective-permute-start(bf16[304,768]{1,0:T(8,128)(2,1)S(1)} %pad_maximum_fusion), channel_id=1, source_target_pairs={{0,1},{1,0},{2,3},{3,2},{4,5},{5,4},{6,7},{7,6},{8,9},{9,8},{10,11... | collective-permute-start | bytes 1400840 | tf_op jit(solution)/shard_map/ppermute | solution.py:295
  15.1 17.9 %copy-start.4 = (bf16[304,608]{1,0:T(8,128)(2,1)S(1)}, bf16[304,608]{1,0:T(8,128)(2,1)}, u32[]{:S(2)}) copy-start(bf16[304,608]{1,0:T(8,128)(2,1)} %param.16) | copy-start | bytes 1108996
  15.1 16.4 %collective-permute-start.2 = (bf16[3,152,256]{2,1,0:T(8,128)(2,1)}, bf16[3,152,256]{2,1,0:T(8,128)(2,1)}, u32[]{:S(2)}, u32[]{:S(2)}) collective-permute-start(bf16[3,152,256]{2,1,0:T(8,128)(2,1)} %dynamic-slice_bitcast_fusion), channel_id=1, source_target_pairs={{0,1},{1,0},{2,3},{3,2},{4,5},{5,4},{6,7},{7,6},{8,9},{9,8},{10,11... | collective-permute-start | bytes 700424 | tf_op jit(solution)/shard_map/ppermute | solution.py:291
  16.4 21.4 %collective-permute-start.5 = (f32[304,2]{1,0:T(8,128)}, f32[304,2]{1,0:T(8,128)}, u32[]{:S(2)}, u32[]{:S(2)}) collective-permute-start(f32[304,2]{1,0:T(8,128)} %bitcast.16), channel_id=1, source_target_pairs={{0,1},{1,0},{2,3},{3,2},{4,5},{5,4},{6,7},{7,6},{8,9},{9,8},{10,11... | collective-permute-start | bytes 7304 | tf_op jit(solution)/shard_map/ppermute | solution.py:293
  21.0 13.1 %copy-start.12 = (s32[128]{0:T(128)S(1)}, s32[128]{0:T(128)}, u32[]{:S(2)}) copy-start(s32[128]{0:T(128)} %param.12) | copy-start | bytes 1540
  31.5 6.4 %copy-start.7 = (bf16[304,768]{1,0:T(8,128)(2,1)}, bf16[304,768]{1,0:T(8,128)(2,1)S(1)}, u32[]{:S(2)}) copy-start(bf16[304,768]{1,0:T(8,128)(2,1)S(1)} %collective-permute-done.3.refs_6_) | copy-start | bytes 1400836
  31.5 56.1 %collective-permute-start.8 = (bf16[304,3328]{1,0:T(8,128)(2,1)}, bf16[304,3328]{1,0:T(8,128)(2,1)}, u32[]{:S(2)}, u32[]{:S(2)}) collective-permute-start(bf16[304,3328]{1,0:T(8,128)(2,1)} %slice.33), channel_id=1, source_target_pairs={{0,1},{1,0},{2,3},{3,2},{4,5},{5,4},{6,7},{7,6},{8,9},{9,8},{10,11... | collective-permute-start | bytes 6070280 | tf_op jit(solution)/shard_map/ppermute | solution.py:301
  34.1 1.7 %collective-permute-start.4 = (bf16[3,152,256]{2,1,0:T(8,128)(2,1)}, bf16[3,152,256]{2,1,0:T(8,128)(2,1)S(1)}, u32[]{:S(2)}, u32[]{:S(2)}) collective-permute-start(bf16[3,152,256]{2,1,0:T(8,128)(2,1)} %collective-permute-done.2), channel_id=1, source_target_pairs={{0,2},{2,0},{4,6},{6,4},{8,10},{10,8},{12,14},{14,12},{16,18},{18,... | collective-permute-start | bytes 700424 | tf_op jit(solution)/shard_map/ppermute | solution.py:302
  38.8 27.0 %collective-permute-start.7 = (bf16[608,384]{1,0:T(8,128)(2,1)}, bf16[608,384]{1,0:T(8,128)(2,1)S(1)}, u32[]{:S(2)}, u32[]{:S(2)}) collective-permute-start(bf16[608,384]{1,0:T(8,128)(2,1)} %get-tuple-element.35), channel_id=1, source_target_pairs={{2,0},{4,2},{6,4},{8,6},{10,8},{12,10},{14,12},{16,14},{18,16},{20... | collective-permute-start | bytes 1400840 | tf_op jit(solution)/shard_map/ppermute | solution.py:326
  41.9 23.9 %collective-permute-start.6 = (bf16[608,384]{1,0:T(8,128)(2,1)S(1)}, bf16[608,384]{1,0:T(8,128)(2,1)S(1)}, u32[]{:S(2)}, u32[]{:S(2)}) collective-permute-start(bf16[608,384]{1,0:T(8,128)(2,1)S(1)} %get-tuple-element.36), channel_id=1, source_target_pairs={{0,2},{2,4},{4,6},{6,8},{8,10},{10,12},{12,14},{14,16},{16,18},{18... | collective-permute-start | bytes 1400840 | tf_op jit(solution)/shard_map/ppermute | solution.py:325
  61.0 10.7 %copy-start.3 = (bf16[16,256,256]{2,1,0:T(8,128)(2,1)}, bf16[16,256,256]{2,1,0:T(8,128)(2,1)S(1)}, u32[]{:S(2)}) copy-start(bf16[16,256,256]{2,1,0:T(8,128)(2,1)S(1)} %all-to-all-done) | copy-start | bytes 6291460
  61.1 6.0 %collective-permute-start.1 = (bf16[384,256]{1,0:T(8,128)(2,1)S(1)}, bf16[384,256]{1,0:T(8,128)(2,1)S(1)}, u32[]{:S(2)}, u32[]{:S(2)}) collective-permute-start(bf16[384,256]{1,0:T(8,128)(2,1)S(1)} %get-tuple-element.33), channel_id=1, source_target_pairs={{2,0},{4,2},{6,4},{8,6},{10,8},{12,10},{14,12},{16,14},{18,16},{20... | collective-permute-start | bytes 589832 | tf_op jit(solution)/shard_map/ppermute | solution.py:287
  63.9 7.9 %collective-permute-start = (bf16[384,256]{1,0:T(8,128)(2,1)S(1)}, bf16[384,256]{1,0:T(8,128)(2,1)S(1)}, u32[]{:S(2)}, u32[]{:S(2)}) collective-permute-start(bf16[384,256]{1,0:T(8,128)(2,1)S(1)} %get-tuple-element.34), channel_id=1, source_target_pairs={{0,2},{2,4},{4,6},{6,8},{8,10},{10,12},{12,14},{14,16},{16,18},{18... | collective-permute-start | bytes 589832 | tf_op jit(solution)/shard_map/ppermute | solution.py:287
  65.8 6.0 %copy-start.5 = (bf16[608,384]{1,0:T(8,128)(2,1)}, bf16[608,384]{1,0:T(8,128)(2,1)S(1)}, u32[]{:S(2)}) copy-start(bf16[608,384]{1,0:T(8,128)(2,1)S(1)} %collective-permute-done.7.refs_4_) | copy-start | bytes 1400836
  65.8 5.9 %copy-start.6 = (bf16[608,384]{1,0:T(8,128)(2,1)}, bf16[608,384]{1,0:T(8,128)(2,1)S(1)}, u32[]{:S(2)}) copy-start(bf16[608,384]{1,0:T(8,128)(2,1)S(1)} %collective-permute-done.6.refs_3_) | copy-start | bytes 1400836
  67.1 4.7 %copy-start.9 = (bf16[384,256]{1,0:T(8,128)(2,1)}, bf16[384,256]{1,0:T(8,128)(2,1)S(1)}, u32[]{:S(2)}) copy-start(bf16[384,256]{1,0:T(8,128)(2,1)S(1)} %collective-permute-done.1.refs_2_) | copy-start | bytes 589828
  71.7 0.7 copy-start.10

commit v4 on v3

--- a/solution.py
+++ b/solution.py
@@ -12,9 +12,12 @@
 XTRACK = 128
 NANG = 8
 HALO = 3
-OUT_BLOCK = 1024
+OUT_BLOCK = 512
 GATHER_LIMIT = 24 * 1024 * 1024
-VMEM_LIMIT = 60 * 1024 * 1024
+OWN_LIMIT = 60 * 1024 * 1024
+LAST_LIMIT = 60 * 1024 * 1024
+SEGMENTS = 4
+AHEAD = 2
 
 
 max_zenith = math.pi / 3.0
@@ -103,41 +106,67 @@
 
 
 def half_kernel(last, *refs):
-    prof_hbm, prof_top_hbm, prof_bot_hbm, top_hbm, bot_hbm = refs[:5]
+    prof_hbm, prof_top_hbm, prof_bot_hbm, top_hbm, bot_hbm, jac_hbm = refs[:6]
     if last:
-        mid_hbm, bnd_hbm, smooth_hbm, jac_ref, rates_ref, rows_ref, shift_ref, factor_ref = refs[5:13]
-        out_hbm, prof, obs, field, moved_a, moved_b, sems, smooth, out, out_sems = refs[13:]
+        mid_hbm, bnd_hbm, smooth_hbm, factor_hbm, rates_ref, rows_ref, shift_ref = refs[6:13]
+        out_hbm, prof, obs, jac_ref, field, moved_a, moved_b, smooth, sems, out_sems, out, factor_ref = refs[13:]
     else:
-        obs_hbm, jac_ref, rates_ref, rows_ref, shift_ref = refs[5:10]
-        smooth, prof, obs, field, moved_a, moved_b, sems = refs[10:]
-    own, pixels = jac_ref.shape[1], prof_hbm.shape[0]
+        obs_hbm, rates_ref, rows_ref, shift_ref = refs[6:10]
+        out_hbm, prof, obs, jac_ref, field, moved_a, moved_b, smooth, sems, out_sems = refs[10:]
+    own, pixels = jac_hbm.shape[1], prof_hbm.shape[0]
     rim = prof_top_hbm.shape[0]
     lines = pixels // XTRACK
     wide = 2 * XTRACK
     full = pixels + 2 * rim
     total = full // XTRACK
     first = own if last else 0
-
+    groups = own // 16
+
+    blocks = full // wide
+    cuts = [blocks * n // SEGMENTS for n in range(SEGMENTS + 1)]
     part = pl.ds(first, own)
-    copies = [
-        (prof_top_hbm, prof.at[pl.ds(0, rim), :]),
-        (top_hbm.at[part, :], obs.at[:, pl.ds(0, rim)]),
-        (prof_hbm, prof.at[pl.ds(rim, pixels), :]),
-        (prof_bot_hbm, prof.at[pl.ds(rim + pixels, rim), :]),
-        (bot_hbm.at[part, :], obs.at[:, pl.ds(rim + pixels, rim)]),
-    ]
+    waits = []
+    copies = []
+
+    def fetch(src, dst):
+        copy = pltpu.make_async_copy(src, dst, sems.at[len(copies)])
+        copies.append(copy)
+        waits[-1].append(copy)
+
+    for n in range(SEGMENTS):
+        waits.append([])
+        if n == 0:
+            fetch(jac_hbm, jac_ref)
+            fetch(prof_top_hbm, prof.at[pl.ds(0, rim), :])
+            fetch(top_hbm.at[part, :], obs.at[:, pl.ds(0, rim)])
+        low = max(cuts[n] * wide - rim, 0)
+        high = min(cuts[n + 1] * wide - rim, pixels)
+        fetch(prof_hbm.at[pl.ds(low, high - low), :], prof.at[pl.ds(rim + low, high - low), :])
+        if last:
+            spans = [(bnd_hbm, 0, 0, rim), (mid_hbm, 0, rim, pixels - rim), (bnd_hbm, rim, pixels - rim, pixels)]
+        else:
+            spans = [(obs_hbm, 0, 0, pixels)]
+        for src, origin, begin, end in spans:
+            begin_n, end_n = max(begin, low), min(end, high)
+            if begin_n < end_n:
+                fetch(
+                    src.at[:, pl.ds(origin + begin_n - begin, end_n - begin_n)],
+                    obs.at[:, pl.ds(rim + begin_n, end_n - begin_n)],
+                )
+        if n == SEGMENTS - 1:
+            fetch(prof_bot_hbm, prof.at[pl.ds(rim + pixels, rim), :])
+            fetch(bot_hbm.at[part, :], obs.at[:, pl.ds(rim + pixels, rim)])
     if last:
-        copies += [
-            (bnd_hbm.at[:, pl.ds(0, rim)], obs.at[:, pl.ds(rim, rim)]),
-            (mid_hbm, obs.at[:, pl.ds(2 * rim, pixels - 2 * rim)]),
-            (bnd_hbm.at[:, pl.ds(rim, rim)], obs.at[:, pl.ds(pixels, rim)]),
-            (smooth_hbm, smooth.at[pl.ds(0, own), :]),
-        ]
-    else:
-        copies.append((obs_hbm, obs.at[:, pl.ds(rim, pixels)]))
-    copies = [pltpu.make_async_copy(src, dst, sems.at[n]) for n, (src, dst) in enumerate(copies)]
-    for copy in copies:
-        copy.start()
+        waits.append([])
+        fetch(smooth_hbm, smooth.at[pl.ds(0, own), :])
+        fetch(factor_hbm, factor_ref)
+
+    def start(n):
+        for copy in waits[n] if n < len(waits) else []:
+            copy.start()
+
+    for n in range(AHEAD):
+        start(n)
     s1 = jnp.concatenate([rows_ref[0:1, :]] * 2, axis=1)
     s2 = jnp.concatenate([rows_ref[1:2, :]] * 2, axis=1)
     inside_top = rows_ref[2:3, :]
@@ -157,7 +186,7 @@
     def shifts(i, moved):
         rows = pl.ds(pl.multiple_of(i * 16, 16), 16)
         tiles = []
-        for j in range(total):
+        for j in range(1, total - 1):
             here = field[rows, j * XTRACK : (j + 1) * XTRACK]
             high = here.astype(jnp.bfloat16)
             low = (here - high.astype(jnp.float32)).astype(jnp.bfloat16)
@@ -184,7 +213,7 @@
                 new = (
                     stay * prev[at]
                     + along * (prev[at - 1] + prev[at + 1])
-                    + cross[k - 1] * moved[at * 16 : (at + 1) * 16, (k - 1) * XTRACK : k * XTRACK]
+                    + cross[k - 1] * moved[(at - 1) * 16 : at * 16, (k - 1) * XTRACK : k * XTRACK]
                 )
                 if at < HALO:
                     new = new * inside_top
@@ -196,26 +225,38 @@
                     line = at - HALO
                     smooth[chan, line * XTRACK : (line + 1) * XTRACK] = new.astype(smooth.dtype)
 
-    for copy in copies[:8]:
-        copy.wait()
-    pl.loop(0, total // 2, unroll=4)(departures)
-
-    groups = own // 16
+    for n in range(SEGMENTS):
+        for copy in waits[n]:
+            copy.wait()
+        start(n + AHEAD)
+        pl.loop(cuts[n], cuts[n + 1], unroll=cuts[n + 1] - cuts[n])(departures)
+
+    def smooth_copy(n, size):
+        rows = pl.ds(pl.multiple_of(n, 16), size)
+        return pltpu.make_async_copy(smooth.at[rows, :], out_hbm.at[rows, :], out_sems.at[0])
+
     shifts(0, moved_a)
 
-    @pl.loop(0, groups // 2)
+    @pl.loop(0, groups // 2, unroll=groups // 2)
     def _(h):
         shifts(2 * h + 1, moved_b)
         sweeps(2 * h, moved_a)
         shifts(jnp.minimum(2 * h + 2, groups - 1), moved_a)
         sweeps(2 * h + 1, moved_b)
+        if not last:
+            smooth_copy(32 * h, 32).start()
 
     if groups % 2:
         sweeps(groups - 1, moved_a)
+        if not last:
+            smooth_copy(16 * (groups - 1), 16).start()
 
     if not last:
+        smooth_copy(0, own).wait()
         return
-    copies[8].wait()
+
+    for copy in waits[SEGMENTS]:
+        copy.wait()
 
     def out_copy(t):
         at = pl.multiple_of(t * OUT_BLOCK, OUT_BLOCK)
@@ -223,7 +264,7 @@
             out.at[:, pl.ds(at, OUT_BLOCK)], out_hbm.at[:, pl.ds(at, OUT_BLOCK)], out_sems.at[t]
         )
 
-    @pl.loop(0, pixels // OUT_BLOCK)
+    @pl.loop(0, pixels // OUT_BLOCK, unroll=pixels // OUT_BLOCK)
     def _(t):
         at = pl.multiple_of(t * OUT_BLOCK, OUT_BLOCK)
         out[:, pl.ds(at, OUT_BLOCK)] = jnp.dot(
@@ -235,37 +276,31 @@
 
 
 def half_call(last, anys, whole):
-    own, pixels = whole[0].shape[1], anys[0].shape[0]
+    own, pixels = anys[5].shape[1], anys[0].shape[0]
     rim = anys[1].shape[0]
     full = pixels + 2 * rim
+    dtype = jnp.float32 if last else jnp.bfloat16
     scratch = [
         pltpu.VMEM((full, anys[0].shape[1]), jnp.bfloat16),
         pltpu.VMEM((own, full), jnp.bfloat16),
+        pltpu.VMEM(anys[5].shape, jnp.bfloat16),
         pltpu.VMEM((own, full), jnp.float32),
-        pltpu.VMEM((16 * (full // XTRACK), HALO * XTRACK), jnp.float32),
-        pltpu.VMEM((16 * (full // XTRACK), HALO * XTRACK), jnp.float32),
-        pltpu.SemaphoreType.DMA((9,)),
+        pltpu.VMEM((16 * (full // XTRACK - 2), HALO * XTRACK), jnp.float32),
+        pltpu.VMEM((16 * (full // XTRACK - 2), HALO * XTRACK), jnp.float32),
+        pltpu.VMEM((2 * own if last else own, pixels), jnp.bfloat16),
+        pltpu.SemaphoreType.DMA((32,)),
+        pltpu.SemaphoreType.DMA((pixels // OUT_BLOCK,)),
     ]
     if last:
-        out_shape = jax.ShapeDtypeStruct((own, pixels), jnp.float32)
-        out_spec = pl.BlockSpec(memory_space=pl.ANY)
-        scratch += [
-            pltpu.VMEM((2 * own, pixels), jnp.bfloat16),
-            pltpu.VMEM((own, pixels), jnp.float32),
-            pltpu.SemaphoreType.DMA((pixels // OUT_BLOCK,)),
-        ]
-    else:
-        out_shape = jax.ShapeDtypeStruct((own, pixels), jnp.bfloat16)
-        out_spec = pl.BlockSpec(memory_space=pltpu.VMEM)
+        scratch += [pltpu.VMEM((own, pixels), jnp.float32), pltpu.VMEM((own, 2 * own), jnp.bfloat16)]
     return pl.pallas_call(
         functools.partial(half_kernel, last),
-        out_shape=out_shape,
+        out_shape=jax.ShapeDtypeStruct((own, pixels), dtype),
         in_specs=[pl.BlockSpec(memory_space=pl.ANY)] * len(anys)
         + [pl.BlockSpec(memory_space=pltpu.VMEM)] * len(whole),
-        out_specs=out_spec,
+        out_specs=pl.BlockSpec(memory_space=pl.ANY),
         scratch_shapes=scratch,
-        compiler_params=pltpu.CompilerParams(vmem_limit_bytes=VMEM_LIMIT),
-        cost_estimate=None if last else pl.CostEstimate(flops=1, bytes_accessed=1, transcendentals=0),
+        compiler_params=pltpu.CompilerParams(vmem_limit_bytes=LAST_LIMIT if last else OWN_LIMIT),
         name="other_half_and_factor" if last else "own_half",
     )(*anys, *whole)
 
@@ -291,10 +326,10 @@
     jac_near = lax.ppermute(jac_half, "chan", swap)
     rates_own = kappa.T
     rates_oth = lax.ppermute(rates_own, "chan", swap)
-    bnd_own = jnp.concatenate([observed[:, :rim], observed[:, pixels - rim :]], axis=1)
+    outgoing = gather_rows(grid_profiles, send_lists[0], counts)
+    outgoing, obs_late = lax.optimization_barrier((outgoing, observed))
+    bnd_own = jnp.concatenate([obs_late[:, :rim], obs_late[:, pixels - rim :]], axis=1)
     bnd_oth = lax.ppermute(bnd_own, "chan", swap)
-    outgoing = gather_rows(grid_profiles, send_lists[0], counts)
-    outgoing, obs_late, bnd_own = lax.optimization_barrier((outgoing, observed, bnd_own))
     incoming = lax.all_to_all(outgoing, "swath", split_axis=0, concat_axis=0, tiled=True)
     middle = obs_late[:, rim : pixels - rim]
     middle, jac_near, bnd_oth = lax.optimization_barrier((middle, jac_near, bnd_oth))
@@ -329,12 +364,14 @@
     prof_halos = halos(profiles, 0)
 
     smooth_own = half_call(
-        False, (profiles, *prof_halos, obs_top, obs_bot, observed), (jac_own, rates_own, rows, shift)
+        False,
+        (profiles, *prof_halos, obs_top, obs_bot, jac_own, observed),
+        (rates_own, rows, shift),
     )
     return half_call(
         True,
-        (profiles, *prof_halos, obs_top, obs_bot, mid_oth, bnd_oth, smooth_own),
-        (jac_oth, rates_oth, rows, shift, factor_two),
+        (profiles, *prof_halos, obs_top, obs_bot, jac_oth, mid_oth, bnd_oth, smooth_own, factor_two),
+        (rates_oth, rows, shift),
     )
 
 

time: 106 us -> 97.1 us (0.916)
  Pallas kernels: 36.5 us -> 28.1 us
  waiting for transfers between devices: 34.5 us -> 32.9 us
  local copies, waits for them, and re-layouts: 9.13 us -> 10.2 us
    pallas_call x2, Pallas kernels: 32.6 us -> 24.2 us  [half_call(): pl.pallas_call(functools.partial(half_kernel, last), out_shape=jax.ShapeD...]
    all_to_all x1, waiting for transfers between devices: 17.3 us -> 15.8 us  [on_device_two(): lax.all_to_all(outgoing, 'swath', split_axis=0, concat_axis=0, tiled=True)]
  transfers between devices with their start and end apart: 10 -> 10, of which waited for: 5 -> 5; matrix products, arithmetic and copies ran while one was open for 9% -> 11% of each run, Pallas kernels for 14% -> 11%
where the time goes in v4:
time: 97.1 us; the launch traced here: 96.6 us
  waiting for transfers between devices  32.9 us (34%)
  Pallas kernels  28.1 us (29%)
  starting transfers between devices  21.3 us (22%)
  local copies, waits for them, and re-layouts  10.2 us (11%)
  other arithmetic  3.68 us (4%)
    pallas_call x2, Pallas kernels, half_call(): pl.pallas_call(functools.partial(half_kernel, last), out_shape=jax.ShapeD...  24.2 us
    all_to_all x1, waiting for transfers between devices, on_device_two(): lax.all_to_all(outgoing, 'swath', split_axis=0, concat_axis=0, tiled=True)  15.8 us
    ppermute x1, waiting for transfers between devices, on_device_two(): jac_near = lax.ppermute(jac_half, 'chan', swap)  10.5 us
    all_to_all x1, starting transfers between devices, on_device_two(): lax.all_to_all(outgoing, 'swath', split_axis=0, concat_axis=0, tiled=True)  6.29 us
    ppermute x1, waiting for transfers between devices, halos(): lax.ppermute(tail, 'swath', forward)  4.68 us
    unnamed x28, local copies, waits for them, and re-layouts  3.96 us
    pallas_call x1, Pallas kernels, gather_rows(): pl.pallas_call(gather_kernel, out_shape=jax.ShapeDtypeStruct((parts, slot...  3.9 us
    ppermute x1, starting transfers between devices, on_device_two(): obs_bot = lax.ppermute(bnd_both[:, :rim], 'swath', backward)  3.1 us
  transfers between devices with their start and end apart: 10, of which 5 were waited for; matrix products, arithmetic and copies ran while one was open for 11% of the time, Pallas kernels for 11%

profile of v4, /device:TPU:16, one launch (start us, length us, event | category | flops | bytes accessed | tf_op | source)
XLA Modules:
  0.0 96.6 jit_solution(5738252425281615467)
XLA Ops:
  0.0 0.0 copy-start
  0.0 1.0 %copy-done = bf16[1024,256]{1,0:T(8,128)(2,1)S(1)} copy-done((bf16[1024,256]{1,0:T(8,128)(2,1)S(1)}, bf16[1024,256]{1,0:T(8,128)(2,1)}, u32[]{:S(2)}) %copy-start) | copy-done | bytes 524312
  1.0 0.0 copy-start.1
  1.0 0.7 copy-done.1
  1.8 0.0 copy-start.2
  1.8 0.7 copy-done.2
  2.4 3.9 %pick_rows.1 = bf16[16,256,256]{2,1,0:T(8,128)(2,1)} custom-call(s32[16,256]{1,0:T(8,128)S(1)} %bitcast.11, s32[1,16]{1,0:T(1,128)S(1)} %copy-done.2, bf16[1024,256]{1,0:T(8,128)(2,1)S(1)} %copy-done), custom_call_target="tpu_custom_call" | custom-call | tf_op jit(solution)/shard_map/pick_rows/pallas_call | solution.py:100
  6.3 0.0 copy-start.8
  6.3 6.3 %all-to-all-start = ((bf16[16,256,256]{2,1,0:T(8,128)(2,1)}), bf16[16,256,256]{2,1,0:T(8,128)(2,1)S(1)}, u32[]{:S(2)}, u32[]{:S(2)}) async-start(bf16[16,256,256]{2,1,0:T(8,128)(2,1)} %pick_rows.1), calls=%async_computation | async-start | bytes 4194304 | tf_op jit(solution)/shard_map/all_to_all | solution.py:333
  12.6 0.0 copy-start.11
  12.6 1.1 %fusion = (bf16[304,384]{1,0:T(8,128)(2,1)S(1)}, bf16[304,384]{1,0:T(8,128)(2,1)S(1)}) fusion(bf16[304,4096]{1,0:T(8,128)(2,1)} %refs_6_.1), kind=kLoop, calls=%fused_computation.9 | loop fusion | bytes 933888 | tf_op jit(solution)/shard_map/slice | solution.py:331
  13.8 1.6 %collective-permute-start.3 = (bf16[304,768]{1,0:T(8,128)(2,1)S(1)}, bf16[304,768]{1,0:T(8,128)(2,1)S(1)}, u32[]{:S(2)}, u32[]{:S(2)}) collective-permute-start(bf16[304,768]{1,0:T(8,128)(2,1)S(1)} %pad_maximum_fusion), channel_id=1, source_target_pairs={{0,1},{1,0},{2,3},{3,2},{4,5},{5,4},{6,7},{7,6},{8,9},{9,8},{10,11... | collective-permute-start | bytes 1400840 | tf_op jit(solution)/shard_map/ppermute | solution.py:332
  15.4 0.0 copy-done.8
  15.4 0.7 dynamic-slice_bitcast_fusion
  16.1 0.0 copy-start.4
  16.1 0.5 collective-permute-start.2
  16.6 0.0 copy-done.11
  16.6 0.8 copy.10
  17.4 1.5 %collective-permute-start.5 = (f32[304,2]{1,0:T(8,128)}, f32[304,2]{1,0:T(8,128)}, u32[]{:S(2)}, u32[]{:S(2)}) collective-permute-start(f32[304,2]{1,0:T(8,128)} %bitcast.16), channel_id=1, source_target_pairs={{0,1},{1,0},{2,3},{3,2},{4,5},{5,4},{6,7},{7,6},{8,9},{9,8},{10,11... | collective-permute-start | bytes 7304 | tf_op jit(solution)/shard_map/ppermute | solution.py:328
  18.9 3.0 %slice.33 = bf16[304,3328]{1,0:T(8,128)(2,1)} slice(bf16[304,4096]{1,0:T(8,128)(2,1)} %refs_6_.1), slice={[0:304], [384:3712]} | slice | bytes 4046848 | tf_op jit(solution)/shard_map/slice | solution.py:334
  22.0 0.0 copy-start.12
  22.0 10.5 %collective-permute-done.2 = bf16[3,152,256]{2,1,0:T(8,128)(2,1)} collective-permute-done((bf16[3,152,256]{2,1,0:T(8,128)(2,1)}, bf16[3,152,256]{2,1,0:T(8,128)(2,1)}, u32[]{:S(2)}, u32[]{:S(2)}) %collective-permute-start.2) | collective-permute-done | bytes 233504 | tf_op jit(solution)/shard_map/ppermute | solution.py:326
  32.5 0.0 collective-permute-done.3.refs_7_
  32.5 0.0 copy-start.7
  32.5 1.5 %collective-permute-start.8 = (bf16[304,3328]{1,0:T(8,128)(2,1)}, bf16[304,3328]{1,0:T(8,128)(2,1)}, u32[]{:S(2)}, u32[]{:S(2)}) collective-permute-start(bf16[304,3328]{1,0:T(8,128)(2,1)} %slice.33), channel_id=1, source_target_pairs={{0,1},{1,0},{2,3},{3,2},{4,5},{5,4},{6,7},{7,6},{8,9},{9,8},{10,11... | collective-permute-start | bytes 6070280 | tf_op jit(solution)/shard_map/ppermute | solution.py:336
  34.0 0.0 copy-done.4
  34.0 0.1 fusion.3
  34.2 1.0 %maximum_select_fusion.1.refs_9_ = bf16[304,608]{1,0:T(8,128)(2,1)} fusion(bf16[304,608]{1,0:T(8,128)(2,1)S(1)} %copy-done.4, bf16[304,304]{1,0:T(8,128)(2,1)S(1)} %get-tuple-element.36, bf16[304,304]{1,0:T(8,128)(2,1)S(1)} %get-tuple-element.35, pred[]{:T(512)S(6)} %eq.10), kind=kLoop, calls=%fused_computation.2 | loop fusion | flops 924160 | bytes 1108993 | tf_op jit(solution)/shard_map/jit(_where)/select_n | solution.py:354
  35.1 0.0 collective-permute-start.4
  35.1 0.0 copy-done.12
  35.2 0.1 pad.4.clone
  35.3 0.1 pad.5.clone
  35.3 0.7 maximum_maximum_fusion.refs_8_.refs_11_
  36.0 0.8 collective-permute-done.4
  36.8 2.0 %maximum_select_fusion.refs_5_ = bf16[3,304,256]{2,1,0:T(8,128)(2,1)} fusion(bf16[3,152,256]{2,1,0:T(8,128)(2,1)S(1)} %collective-permute-done.4, bf16[3,152,256]{2,1,0:T(8,128)(2,1)} %collective-permute-done.2, pred[]{:T(512)S(6)} %eq.9), kind=kLoop, calls=%fused_computation.1 | loop fusion | flops 2101248 | bytes 933889 | tf_op jit(solution)/shard_map/jit(_where)/select_n | solution.py:338
  38.8 0.0 collective-permute-done.5.refs_10_
  38.9 0.0 copy-done.7
  38.9 1.1 %fusion.2 = (bf16[608,384]{1,0:T(8,128)(2,1)}, bf16[608,384]{1,0:T(8,128)(2,1)}) fusion(bf16[608,768]{1,0:T(8,128)(2,1)S(1)} %constant_dynamic-update-slice_fusion), kind=kLoop, calls=%fused_computation.11 | loop fusion | bytes 1867776 | tf_op jit(solution)/shard_map/slice | solution.py:361
  39.9 3.1 %collective-permute-start.7 = (bf16[608,384]{1,0:T(8,128)(2,1)}, bf16[608,384]{1,0:T(8,128)(2,1)S(1)}, u32[]{:S(2)}, u32[]{:S(2)}) collective-permute-start(bf16[608,384]{1,0:T(8,128)(2,1)} %get-tuple-element.33), channel_id=1, source_target_pairs={{2,0},{4,2},{6,4},{8,6},{10,8},{12,10},{14,12},{16,14},{18,16},{20... | collective-permute-start | bytes 1400840 | tf_op jit(solution)/shard_map/ppermute | solution.py:361
  43.0 1.9 %collective-permute-start.6 = (bf16[608,384]{1,0:T(8,128)(2,1)}, bf16[608,384]{1,0:T(8,128)(2,1)S(1)}, u32[]{:S(2)}, u32[]{:S(2)}) collective-permute-start(bf16[608,384]{1,0:T(8,128)(2,1)} %get-tuple-element.34), channel_id=1, source_target_pairs={{0,2},{2,4},{4,6},{6,8},{8,10},{10,12},{12,14},{14,16},{16,18},{18... | collective-permute-start | bytes 1400840 | tf_op jit(solution)/shard_map/ppermute | solution.py:360
  45.0 15.8 %all-to-all-done = bf16[16,256,256]{2,1,0:T(8,128)(2,1)S(1)} async-done(((bf16[16,256,256]{2,1,0:T(8,128)(2,1)}), bf16[16,256,256]{2,1,0:T(8,128)(2,1)S(1)}, u32[]{:S(2)}, u32[]{:S(2)}) %all-to-all-start) | async-done | bytes 2097184 | tf_op jit(solution)/shard_map/all_to_all | solution.py:333
  60.8 0.0 copy-start.3
  60.8 2.8 %collective-permute-start.1 = (bf16[384,256]{1,0:T(8,128)(2,1)S(1)}, bf16[384,256]{1,0:T(8,128)(2,1)S(1)}, u32[]{:S(2)}, u32[]{:S(2)}) collective-permute-start(bf16[384,256]{1,0:T(8,128)(2,1)S(1)} %get-tuple-element.31), channel_id=1, source_target_pairs={{2,0},{4,2},{6,4},{8,6},{10,8},{12,10},{14,12},{16,14},{18,16},{20... | collective-permute-start | bytes 589832 | tf_op jit(solution)/shard_map/ppermute | solution.py:322
  63.6 2.1 %collective-permute-start = (bf16[384,256]{1,0:T(8,128)(2,1)S(1)}, bf16[384,256]{1,0:T(8,128)(2,1)S(1)}, u32[]{:S(2)}, u32[]{:S(2)}) collective-permute-start(bf16[384,256]{1,0:T(8,128)(2,1)S(1)} %get-tuple-element.32), channel_id=1, source_target_pairs={{0,2},{2,4},{4,6},{6,8},{8,10},{10,12},{12,14},{14,16},{16,18},{18... | collective-permute-start | bytes 589832 | tf_op jit(solution)/shard_map/ppermute | solution.py:322
  65.7 0.0 collective-permute-done.7.refs_4_
  65.8 0.0 copy-start.5
  65.8 0.0 collective-permute-done.6.refs_3_
  65.8 0.0 copy-start.6
  65.8 1.1 %collective-permute-done.1.refs_2_ = bf16[384,256]{1,0:T(8,128)(2,1)S(1)} collective-permute-done((bf16[384,256]{1,0:T(8,128)(2,1)S(1)}, bf16[384,256]{1,0:T(8,128)(2,1)S(1)}, u32[]{:S(2)}, u32[]{:S(2)}) %collective-permute-start.1) | collective-permute-done | bytes 196640 | tf_op jit(solution)/shard_map/ppermute | solution.py:322
  66.8 0.0 copy-start.9
  66.8 4.7 %collective-permute-done.refs_1_ = bf16[384,256]{1,0:T(8,128)(2,1)S(1)} collective-permute-done((bf16[384,256]{1,0:T(8,128)(2,1)S(1)}, bf16[384,256]{1,0:T(8,128)(2,1)S(1)}, u32[]{:S(2)}, u32[]{:S(2)}) %collective-permute-start) | collective-permute-done | bytes 196640 | tf_op jit(solution)/shard_map/ppermute | solution.py:322
  71.5 0.0 copy-start.10
  71.5 0.0 copy-done.3
  71.5 0.0 copy-done.5
  71.5 0.0 copy-done.6
  71.5 0.0 copy-done.9
  71.5 0.7 copy-done.10
  72.2 10.8 %own_half.1.refs_8_ = bf16[304,4096]{1,0:T(8,128)(2,1)} custom-call(bf16[4096,256]{1,0:T(8,128)(2,1)} %bitcast.13, bf16[384,256]{1,0:T(8,128)(2,1)} %copy-done.10, bf16[384,256]{1,0:T(8,128)(2,1)} %copy-done.9, bf16[608,384]{1,0:T(8,128)(2,1)} %copy-done.6, bf16[608,384]{1,0:T(8,128)(2,1)} %copy-done.5, bf16[3,304,256]{2,1,0:T(8,128)(2,1)} %bitcast.15, ...), custom_call_target="tpu_custom_call" | custom-call | tf_op jit(solution)/shard_map/own_half/pallas_call | solution.py:296
  83.1 0.0 collective-permute-done.8.refs_6_
  83.1 13.3 %other_half_and_factor.1 = f32[304,4096]{1,0:T(8,128)} custom-call(bf16[4096,256]{1,0:T(8,128)(2,1)} %bitcast.14, bf16[384,256]{1,0:T(8,128)(2,1)} %copy-done.10, bf16[384,256]{1,0:T(8,128)(2,1)} %copy-done.9, bf16[608,384]{1,0:T(8,128)(2,1)} %copy-done.6, bf16[608,384]{1,0:T(8,128)(2,1)} %copy-done.5, bf16[3,304,256]{2,1,0:T(8,128)(2,1)} %maximum_select_fusion.refs_5_, ...), custom_call_target="tpu_custom_call" | custom-call | tf_op jit(solution)/shard_map/other_half_and_factor/pallas_call | solution.py:296
  (5 shorter events, 0.2 us)
Async XLA Ops:
  0.0 1.0 %copy-start = (bf16[1024,256]{1,0:T(8,128)(2,1)S(1)}, bf16[1024,256]{1,0:T(8,128)(2,1)}, u32[]{:S(2)}) copy-start(bf16[1024,256]{1,0:T(8,128)(2,1)} %grid_ref.1) | copy-start | bytes 1572868
  1.0 0.7 copy-start.1
  1.8 0.7 copy-start.2
  6.3 9.0 %copy-start.8 = (bf16[3,256,304]{1,2,0:T(8,128)(2,1)S(1)}, bf16[3,256,304]{1,2,0:T(8,128)(2,1)}, u32[]{:S(2)}) copy-start(bf16[3,256,304]{1,2,0:T(8,128)(2,1)} %param.13) | copy-start | bytes 1400836
  6.3 54.5 %all-to-all-start = ((bf16[16,256,256]{2,1,0:T(8,128)(2,1)}), bf16[16,256,256]{2,1,0:T(8,128)(2,1)S(1)}, u32[]{:S(2)}, u32[]{:S(2)}) async-start(bf16[16,256,256]{2,1,0:T(8,128)(2,1)} %pick_rows.1), calls=%async_computation | async-start | bytes 4194304 | tf_op jit(solution)/shard_map/all_to_all | solution.py:333
  12.6 4.0 %copy-start.11 = (f32[2,304]{1,0:T(2,128)S(1)}, f32[2,304]{1,0:T(2,128)}, u32[]{:S(2)}) copy-start(f32[2,304]{1,0:T(2,128)} %param.15) | copy-start | bytes 7300
  13.8 18.7 %collective-permute-start.3 = (bf16[304,768]{1,0:T(8,128)(2,1)S(1)}, bf16[304,768]{1,0:T(8,128)(2,1)S(1)}, u32[]{:S(2)}, u32[]{:S(2)}) collective-permute-start(bf16[304,768]{1,0:T(8,128)(2,1)S(1)} %pad_maximum_fusion), channel_id=1, source_target_pairs={{0,1},{1,0},{2,3},{3,2},{4,5},{5,4},{6,7},{7,6},{8,9},{9,8},{10,11... | collective-permute-start | bytes 1400840 | tf_op jit(solution)/shard_map/ppermute | solution.py:332
  16.1 17.9 %copy-start.4 = (bf16[304,608]{1,0:T(8,128)(2,1)S(1)}, bf16[304,608]{1,0:T(8,128)(2,1)}, u32[]{:S(2)}) copy-start(bf16[304,608]{1,0:T(8,128)(2,1)} %param.16) | copy-start | bytes 1108996
  16.1 16.4 %collective-permute-start.2 = (bf16[3,152,256]{2,1,0:T(8,128)(2,1)}, bf16[3,152,256]{2,1,0:T(8,128)(2,1)}, u32[]{:S(2)}, u32[]{:S(2)}) collective-permute-start(bf16[3,152,256]{2,1,0:T(8,128)(2,1)} %dynamic-slice_bitcast_fusion), channel_id=1, source_target_pairs={{0,1},{1,0},{2,3},{3,2},{4,5},{5,4},{6,7},{7,6},{8,9},{9,8},{10,11... | collective-permute-start | bytes 700424 | tf_op jit(solution)/shard_map/ppermute | solution.py:326
  17.4 21.4 %collective-permute-start.5 = (f32[304,2]{1,0:T(8,128)}, f32[304,2]{1,0:T(8,128)}, u32[]{:S(2)}, u32[]{:S(2)}) collective-permute-start(f32[304,2]{1,0:T(8,128)} %bitcast.16), channel_id=1, source_target_pairs={{0,1},{1,0},{2,3},{3,2},{4,5},{5,4},{6,7},{7,6},{8,9},{9,8},{10,11... | collective-permute-start | bytes 7304 | tf_op jit(solution)/shard_map/ppermute | solution.py:328
  22.0 13.2 %copy-start.12 = (s32[128]{0:T(128)S(1)}, s32[128]{0:T(128)}, u32[]{:S(2)}) copy-start(s32[128]{0:T(128)} %param.12) | copy-start | bytes 1540
  32.5 6.4 %copy-start.7 = (bf16[304,768]{1,0:T(8,128)(2,1)}, bf16[304,768]{1,0:T(8,128)(2,1)S(1)}, u32[]{:S(2)}) copy-start(bf16[304,768]{1,0:T(8,128)(2,1)S(1)} %collective-permute-done.3.refs_7_) | copy-start | bytes 1400836
  32.5 50.6 %collective-permute-start.8 = (bf16[304,3328]{1,0:T(8,128)(2,1)}, bf16[304,3328]{1,0:T(8,128)(2,1)}, u32[]{:S(2)}, u32[]{:S(2)}) collective-permute-start(bf16[304,3328]{1,0:T(8,128)(2,1)} %slice.33), channel_id=1, source_target_pairs={{0,1},{1,0},{2,3},{3,2},{4,5},{5,4},{6,7},{7,6},{8,9},{9,8},{10,11... | collective-permute-start | bytes 6070280 | tf_op jit(solution)/shard_map/ppermute | solution.py:336
  35.1 1.7 %collective-permute-start.4 = (bf16[3,152,256]{2,1,0:T(8,128)(2,1)}, bf16[3,152,256]{2,1,0:T(8,128)(2,1)S(1)}, u32[]{:S(2)}, u32[]{:S(2)}) collective-permute-start(bf16[3,152,256]{2,1,0:T(8,128)(2,1)} %collective-permute-done.2), channel_id=1, source_target_pairs={{0,2},{2,0},{4,6},{6,4},{8,10},{10,8},{12,14},{14,12},{16,18},{18,... | collective-permute-start | bytes 700424 | tf_op jit(solution)/shard_map/ppermute | solution.py:337
  39.9 25.8 %collective-permute-start.7 = (bf16[608,384]{1,0:T(8,128)(2,1)}, bf16[608,384]{1,0:T(8,128)(2,1)S(1)}, u32[]{:S(2)}, u32[]{:S(2)}) collective-permute-start(bf16[608,384]{1,0:T(8,128)(2,1)} %get-tuple-element.33), channel_id=1, source_target_pairs={{2,0},{4,2},{6,4},{8,6},{10,8},{12,10},{14,12},{16,14},{18,16},{20... | collective-permute-start | bytes 1400840 | tf_op jit(solution)/shard_map/ppermute | solution.py:361
  43.0 22.7 %collective-permute-start.6 = (bf16[608,384]{1,0:T(8,128)(2,1)}, bf16[608,384]{1,0:T(8,128)(2,1)S(1)}, u32[]{:S(2)}, u32[]{:S(2)}) collective-permute-start(bf16[608,384]{1,0:T(8,128)(2,1)} %get-tuple-element.34), channel_id=1, source_target_pairs={{0,2},{2,4},{4,6},{6,8},{8,10},{10,12},{12,14},{14,16},{16,18},{18... | collective-permute-start | bytes 1400840 | tf_op jit(solution)/shard_map/ppermute | solution.py:360
  60.8 10.7 %copy-start.3 = (bf16[16,256,256]{2,1,0:T(8,128)(2,1)}, bf16[16,256,256]{2,1,0:T(8,128)(2,1)S(1)}, u32[]{:S(2)}) copy-start(bf16[16,256,256]{2,1,0:T(8,128)(2,1)S(1)} %all-to-all-done) | copy-start | bytes 6291460
  60.8 6.0 %collective-permute-start.1 = (bf16[384,256]{1,0:T(8,128)(2,1)S(1)}, bf16[384,256]{1,0:T(8,128)(2,1)S(1)}, u32[]{:S(2)}, u32[]{:S(2)}) collective-permute-start(bf16[384,256]{1,0:T(8,128)(2,1)S(1)} %get-tuple-element.31), channel_id=1, source_target_pairs={{2,0},{4,2},{6,4},{8,6},{10,8},{12,10},{14,12},{16,14},{18,16},{20... | collective-permute-start | bytes 589832 | tf_op jit(solution)/shard_map/ppermute | solution.py:322
  63.6 7.9 %collective-permute-start = (bf16[384,256]{1,0:T(8,128)(2,1)S(1)}, bf16[384,256]{1,0:T(8,128)(2,1)S(1)}, u32[]{:S(2)}, u32[]{:S(2)}) collective-permute-start(bf16[384,256]{1,0:T(8,128)(2,1)S(1)} %get-tuple-element.32), channel_id=1, source_target_pairs={{0,2},{2,4},{4,6},{6,8},{8,10},{10,12},{12,14},{14,16},{16,18},{18... | collective-permute-start | bytes 589832 | tf_op jit(solution)/shard_map/ppermute | solution.py:322
  65.8 5.8 %copy-start.5 = (bf16[608,384]{1,0:T(8,128)(2,1)}, bf16[608,384]{1,0:T(8,128)(2,1)S(1)}, u32[]{:S(2)}) copy-start(bf16[608,384]{1,0:T(8,128)(2,1)S(1)} %collective-permute-done.7.refs_4_) | copy-start | bytes 1400836
  65.8 5.8 %copy-start.6 = (bf16[608,384]{1,0:T(8,128)(2,1)}, bf16[608,384]{1,0:T(8,128)(2,1)S(1)}, u32[]{:S(2)}) copy-start(bf16[608,384]{1,0:T(8,128)(2,1)S(1)} %collective-permute-done.6.refs_3_) | copy-start | bytes 1400836
  66.8 4.7 %copy-start.9 = (bf16[384,256]{1,0:T(8,128)(2,1)}, bf16[384,256]{1,0:T(8,128)(2,1)S(1)}, u32[]{:S(2)}) copy-start(bf16[384,256]{1,0:T(8,128)(2,1)S(1)} %collective-permute-done.1.refs_2_) | copy-start | bytes 589828
  71.5 0.7 copy-start.10

commit v5 on v4

--- a/solution.py
+++ b/solution.py
@@ -13,7 +13,7 @@
 NANG = 8
 HALO = 3
 OUT_BLOCK = 512
-GATHER_LIMIT = 24 * 1024 * 1024
+GATHER_LIMIT = 60 * 1024 * 1024
 OWN_LIMIT = 60 * 1024 * 1024
 LAST_LIMIT = 60 * 1024 * 1024
 SEGMENTS = 4
@@ -83,23 +83,43 @@
     )
 
 
-def gather_kernel(lists_ref, counts_ref, grid_ref, out_ref):
-    grid_rows = grid_ref.shape[0]
-    parts, slots = lists_ref.shape
+def gather_kernel(lists_hbm, counts_hbm, grid_hbm, out_hbm, lists, counts, grid, out, sems, out_sem):
+    ins = [(lists_hbm, lists), (counts_hbm, counts), (grid_hbm, grid)]
+    ins = [pltpu.make_async_copy(src, dst, sems.at[n]) for n, (src, dst) in enumerate(ins)]
+    for copy in ins:
+        copy.start()
+    for copy in ins[:2]:
+        copy.wait()
+    grid_rows = grid.shape[0]
+    parts, slots = lists.shape
     slot_number = lax.broadcasted_iota(jnp.int32, (slots, parts), 0)
-    picks = jnp.where(slot_number < counts_ref[...], lists_ref[...].T, -1)
+    picks = jnp.where(slot_number < counts[...], lists[...].T, -1)
     row_number = lax.broadcasted_iota(jnp.int32, (slots, grid_rows), 1)
+    ins[2].wait()
     for part in range(parts):
         one_hot = (picks[:, part : part + 1] == row_number).astype(jnp.float32).astype(jnp.bfloat16)
-        rows = jnp.dot(one_hot, grid_ref[...], preferred_element_type=jnp.float32)
-        out_ref[part] = rows.astype(out_ref.dtype)
+        rows = jnp.dot(one_hot, grid[...], preferred_element_type=jnp.float32)
+        out[part] = rows.astype(out.dtype)
+        pltpu.make_async_copy(out.at[part], out_hbm.at[part], out_sem).start()
+    pltpu.make_async_copy(out, out_hbm, out_sem).wait()
 
 
 def gather_rows(grid_profiles, slot_rows, counts):
     parts, slots = slot_rows.shape
+    shape = (parts, slots, grid_profiles.shape[1])
     return pl.pallas_call(
         gather_kernel,
-        out_shape=jax.ShapeDtypeStruct((parts, slots, grid_profiles.shape[1]), grid_profiles.dtype),
+        out_shape=jax.ShapeDtypeStruct(shape, grid_profiles.dtype),
+        in_specs=[pl.BlockSpec(memory_space=pl.ANY)] * 3,
+        out_specs=pl.BlockSpec(memory_space=pl.ANY),
+        scratch_shapes=[
+            pltpu.VMEM(slot_rows.shape, jnp.int32),
+            pltpu.VMEM(counts.shape, jnp.int32),
+            pltpu.VMEM(grid_profiles.shape, grid_profiles.dtype),
+            pltpu.VMEM(shape, grid_profiles.dtype),
+            pltpu.SemaphoreType.DMA((3,)),
+            pltpu.SemaphoreType.DMA,
+        ],
         compiler_params=pltpu.CompilerParams(vmem_limit_bytes=GATHER_LIMIT),
         name="pick_rows",
     )(slot_rows, counts, grid_profiles)
@@ -332,7 +352,7 @@
     bnd_oth = lax.ppermute(bnd_own, "chan", swap)
     incoming = lax.all_to_all(outgoing, "swath", split_axis=0, concat_axis=0, tiled=True)
     middle = obs_late[:, rim : pixels - rim]
-    middle, jac_near, bnd_oth = lax.optimization_barrier((middle, jac_near, bnd_oth))
+    middle, bnd_oth = lax.optimization_barrier((middle, bnd_oth))
     mid_oth = lax.ppermute(middle, "chan", swap)
     jac_far = lax.ppermute(jac_near, "swath", [(i, i ^ 1) for i in range(swath)])
     jac_oth = jnp.where(

time: 97.1 us -> 95 us (0.978)
  local copies, waits for them, and re-layouts: 10.2 us -> 7.62 us
    ppermute x1, waiting for transfers between devices: 0.01 us -> 5.4 us  [on_device_two(): bnd_oth = lax.ppermute(bnd_own, 'chan', swap)]
    ppermute x1, waiting for transfers between devices: 10.5 us -> 5.83 us  [on_device_two(): jac_near = lax.ppermute(jac_half, 'chan', swap)]
    unnamed x28 -> x22, local copies, waits for them, and re-layouts: 3.96 us -> 1.52 us
    ppermute x1, starting transfers between devices: 0.51 us -> 1.52 us  [on_device_two(): jac_near = lax.ppermute(jac_half, 'chan', swap)]
    ppermute x1, starting transfers between devices: 1.52 us -> 0.51 us  [on_device_two(): rates_oth = lax.ppermute(rates_own, 'chan', swap)]
  transfers between devices with their start and end apart: 10 -> 10, of which waited for: 5 -> 6; matrix products, arithmetic and copies ran while one was open for 11% -> 11% of each run, Pallas kernels for 11% -> 11%
where the time goes in v5:
time: 95 us; the launch traced here: 94.6 us
  waiting for transfers between devices  33.1 us (35%)
  Pallas kernels  28.5 us (30%)
  starting transfers between devices  21.3 us (22%)
  local copies, waits for them, and re-layouts  7.62 us (8%)
  other arithmetic  3.68 us (4%)
    pallas_call x2, Pallas kernels, half_call(): pl.pallas_call(functools.partial(half_kernel, last), out_shape=jax.ShapeD...  24.2 us
    all_to_all x1, waiting for transfers between devices, on_device_two(): lax.all_to_all(outgoing, 'swath', split_axis=0, concat_axis=0, tiled=True)  15.3 us
    all_to_all x1, starting transfers between devices, on_device_two(): lax.all_to_all(outgoing, 'swath', split_axis=0, concat_axis=0, tiled=True)  6.3 us
    ppermute x1, waiting for transfers between devices, on_device_two(): jac_near = lax.ppermute(jac_half, 'chan', swap)  5.83 us
    ppermute x1, waiting for transfers between devices, on_device_two(): bnd_oth = lax.ppermute(bnd_own, 'chan', swap)  5.4 us
    ppermute x1, waiting for transfers between devices, halos(): lax.ppermute(tail, 'swath', forward)  4.68 us
    pallas_call x1, Pallas kernels, gather_rows(): pl.pallas_call(gather_kernel, out_shape=jax.ShapeDtypeStruct(shape, grid_...  4.26 us
    ppermute x1, starting transfers between devices, on_device_two(): obs_bot = lax.ppermute(bnd_both[:, :rim], 'swath', backward)  3.1 us
  transfers between devices with their start and end apart: 10, of which 6 were waited for; matrix products, arithmetic and copies ran while one was open for 11% of the time, Pallas kernels for 11%

profile of v5, /device:TPU:16, one launch (start us, length us, event | category | flops | bytes accessed | tf_op | source)
XLA Modules:
  0.0 94.6 jit_solution(1547084734301245923)
XLA Ops:
  0.0 4.3 %pick_rows.1 = bf16[16,256,256]{2,1,0:T(8,128)(2,1)} custom-call(s32[16,256]{1,0:T(8,128)} %bitcast.17, s32[1,16]{1,0:T(1,128)} %counts_hbm.1, bf16[1024,256]{1,0:T(8,128)(2,1)} %grid_hbm.1), custom_call_target="tpu_custom_call" | custom-call | tf_op jit(solution)/shard_map/pick_rows/pallas_call | solution.py:110
  4.3 0.0 copy-start.8
  4.3 0.0 copy-start.5
  4.3 6.3 %all-to-all-start = ((bf16[16,256,256]{2,1,0:T(8,128)(2,1)}), bf16[16,256,256]{2,1,0:T(8,128)(2,1)S(1)}, u32[]{:S(2)}, u32[]{:S(2)}) async-start(bf16[16,256,256]{2,1,0:T(8,128)(2,1)} %pick_rows.1), calls=%async_computation | async-start | bytes 4194304 | tf_op jit(solution)/shard_map/all_to_all | solution.py:353
  10.6 1.1 %fusion = (bf16[304,384]{1,0:T(8,128)(2,1)S(1)}, bf16[304,384]{1,0:T(8,128)(2,1)S(1)}) fusion(bf16[304,4096]{1,0:T(8,128)(2,1)} %refs_6_.1), kind=kLoop, calls=%fused_computation.9 | loop fusion | bytes 933888 | tf_op jit(solution)/shard_map/slice | solution.py:351
  11.8 1.6 %collective-permute-start.2 = (bf16[304,768]{1,0:T(8,128)(2,1)S(1)}, bf16[304,768]{1,0:T(8,128)(2,1)S(1)}, u32[]{:S(2)}, u32[]{:S(2)}) collective-permute-start(bf16[304,768]{1,0:T(8,128)(2,1)S(1)} %pad_maximum_fusion), channel_id=1, source_target_pairs={{0,1},{1,0},{2,3},{3,2},{4,5},{5,4},{6,7},{7,6},{8,9},{9,8},{10,11... | collective-permute-start | bytes 1400840 | tf_op jit(solution)/shard_map/ppermute | solution.py:352
  13.3 0.0 copy-done.8
  13.3 0.8 copy.10
  14.1 0.5 collective-permute-start.5
  14.7 0.0 copy-done.5
  14.7 0.7 dynamic-slice_bitcast_fusion
  15.4 0.0 copy-start.1
  15.4 1.5 %collective-permute-start.3 = (bf16[3,152,256]{2,1,0:T(8,128)(2,1)}, bf16[3,152,256]{2,1,0:T(8,128)(2,1)}, u32[]{:S(2)}, u32[]{:S(2)}) collective-permute-start(bf16[3,152,256]{2,1,0:T(8,128)(2,1)} %dynamic-slice_bitcast_fusion), channel_id=1, source_target_pairs={{0,1},{1,0},{2,3},{3,2},{4,5},{5,4},{6,7},{7,6},{8,9},{9,8},{10,11... | collective-permute-start | bytes 700424 | tf_op jit(solution)/shard_map/ppermute | solution.py:346
  16.9 3.1 %slice.33 = bf16[304,3328]{1,0:T(8,128)(2,1)} slice(bf16[304,4096]{1,0:T(8,128)(2,1)} %refs_6_.1), slice={[0:304], [384:3712]} | slice | bytes 4046848 | tf_op jit(solution)/shard_map/slice | solution.py:354
  20.0 0.0 copy-start.9
  20.0 5.4 %collective-permute-done.2.refs_7_ = bf16[304,768]{1,0:T(8,128)(2,1)S(1)} collective-permute-done((bf16[304,768]{1,0:T(8,128)(2,1)S(1)}, bf16[304,768]{1,0:T(8,128)(2,1)S(1)}, u32[]{:S(2)}, u32[]{:S(2)}) %collective-permute-start.2) | collective-permute-done | bytes 466976 | tf_op jit(solution)/shard_map/ppermute | solution.py:352
  25.4 0.0 copy-start.4
  25.4 1.5 %collective-permute-start.8 = (bf16[304,3328]{1,0:T(8,128)(2,1)}, bf16[304,3328]{1,0:T(8,128)(2,1)}, u32[]{:S(2)}, u32[]{:S(2)}) collective-permute-start(bf16[304,3328]{1,0:T(8,128)(2,1)} %slice.33), channel_id=1, source_target_pairs={{0,1},{1,0},{2,3},{3,2},{4,5},{5,4},{6,7},{7,6},{8,9},{9,8},{10,11... | collective-permute-start | bytes 6070280 | tf_op jit(solution)/shard_map/ppermute | solution.py:356
  26.9 0.0 copy-done.1
  26.9 0.1 fusion.3
  27.0 1.0 %maximum_select_fusion.1.refs_9_ = bf16[304,608]{1,0:T(8,128)(2,1)} fusion(bf16[304,608]{1,0:T(8,128)(2,1)S(1)} %copy-done.1, bf16[304,304]{1,0:T(8,128)(2,1)S(1)} %get-tuple-element.34, bf16[304,304]{1,0:T(8,128)(2,1)S(1)} %get-tuple-element.33, pred[]{:T(512)S(6)} %eq.10), kind=kLoop, calls=%fused_computation.2 | loop fusion | flops 924160 | bytes 1108993 | tf_op jit(solution)/shard_map/jit(_where)/select_n | solution.py:374
  28.0 5.8 %collective-permute-done.3 = bf16[3,152,256]{2,1,0:T(8,128)(2,1)} collective-permute-done((bf16[3,152,256]{2,1,0:T(8,128)(2,1)}, bf16[3,152,256]{2,1,0:T(8,128)(2,1)}, u32[]{:S(2)}, u32[]{:S(2)}) %collective-permute-start.3) | collective-permute-done | bytes 233504 | tf_op jit(solution)/shard_map/ppermute | solution.py:346
  33.8 0.0 collective-permute-start.4
  33.8 0.0 copy-done.9
  33.9 0.1 pad.4.clone
  33.9 0.1 pad.5.clone
  34.0 0.7 maximum_maximum_fusion.refs_8_.refs_11_
  34.7 0.8 collective-permute-done.4
  35.5 2.0 %maximum_select_fusion.refs_5_ = bf16[3,304,256]{2,1,0:T(8,128)(2,1)} fusion(bf16[3,152,256]{2,1,0:T(8,128)(2,1)S(1)} %collective-permute-done.4, bf16[3,152,256]{2,1,0:T(8,128)(2,1)} %collective-permute-done.3, pred[]{:T(512)S(6)} %eq.9), kind=kLoop, calls=%fused_computation.1 | loop fusion | flops 2101248 | bytes 933889 | tf_op jit(solution)/shard_map/jit(_where)/select_n | solution.py:358
  37.5 0.0 collective-permute-done.5.refs_10_
  37.6 0.0 copy-done.4
  37.6 0.9 fusion.2
  38.5 3.1 %collective-permute-start.7 = (bf16[608,384]{1,0:T(8,128)(2,1)}, bf16[608,384]{1,0:T(8,128)(2,1)S(1)}, u32[]{:S(2)}, u32[]{:S(2)}) collective-permute-start(bf16[608,384]{1,0:T(8,128)(2,1)} %get-tuple-element.31), channel_id=1, source_target_pairs={{2,0},{4,2},{6,4},{8,6},{10,8},{12,10},{14,12},{16,14},{18,16},{20... | collective-permute-start | bytes 1400840 | tf_op jit(solution)/shard_map/ppermute | solution.py:381
  41.6 1.9 %collective-permute-start.6 = (bf16[608,384]{1,0:T(8,128)(2,1)S(1)}, bf16[608,384]{1,0:T(8,128)(2,1)S(1)}, u32[]{:S(2)}, u32[]{:S(2)}) collective-permute-start(bf16[608,384]{1,0:T(8,128)(2,1)S(1)} %get-tuple-element.32), channel_id=1, source_target_pairs={{0,2},{2,4},{4,6},{6,8},{8,10},{10,12},{12,14},{14,16},{16,18},{18... | collective-permute-start | bytes 1400840 | tf_op jit(solution)/shard_map/ppermute | solution.py:380
  43.5 15.3 %all-to-all-done = bf16[16,256,256]{2,1,0:T(8,128)(2,1)S(1)} async-done(((bf16[16,256,256]{2,1,0:T(8,128)(2,1)}), bf16[16,256,256]{2,1,0:T(8,128)(2,1)S(1)}, u32[]{:S(2)}, u32[]{:S(2)}) %all-to-all-start) | async-done | bytes 2097184 | tf_op jit(solution)/shard_map/all_to_all | solution.py:353
  58.8 0.0 copy-start
  58.8 2.8 %collective-permute-start.1 = (bf16[384,256]{1,0:T(8,128)(2,1)S(1)}, bf16[384,256]{1,0:T(8,128)(2,1)S(1)}, u32[]{:S(2)}, u32[]{:S(2)}) collective-permute-start(bf16[384,256]{1,0:T(8,128)(2,1)S(1)} %get-tuple-element.29), channel_id=1, source_target_pairs={{2,0},{4,2},{6,4},{8,6},{10,8},{12,10},{14,12},{16,14},{18,16},{20... | collective-permute-start | bytes 589832 | tf_op jit(solution)/shard_map/ppermute | solution.py:342
  61.6 2.1 %collective-permute-start = (bf16[384,256]{1,0:T(8,128)(2,1)S(1)}, bf16[384,256]{1,0:T(8,128)(2,1)S(1)}, u32[]{:S(2)}, u32[]{:S(2)}) collective-permute-start(bf16[384,256]{1,0:T(8,128)(2,1)S(1)} %get-tuple-element.30), channel_id=1, source_target_pairs={{0,2},{2,4},{4,6},{6,8},{8,10},{10,12},{12,14},{14,16},{16,18},{18... | collective-permute-start | bytes 589832 | tf_op jit(solution)/shard_map/ppermute | solution.py:342
  63.7 0.0 collective-permute-done.7.refs_4_
  63.7 0.0 copy-start.2
  63.8 0.0 collective-permute-done.6.refs_3_
  63.8 0.0 copy-start.3
  63.8 1.1 %collective-permute-done.1.refs_2_ = bf16[384,256]{1,0:T(8,128)(2,1)S(1)} collective-permute-done((bf16[384,256]{1,0:T(8,128)(2,1)S(1)}, bf16[384,256]{1,0:T(8,128)(2,1)S(1)}, u32[]{:S(2)}, u32[]{:S(2)}) %collective-permute-start.1) | collective-permute-done | bytes 196640 | tf_op jit(solution)/shard_map/ppermute | solution.py:342
  64.8 0.0 copy-start.6
  64.8 4.7 %collective-permute-done.refs_1_ = bf16[384,256]{1,0:T(8,128)(2,1)S(1)} collective-permute-done((bf16[384,256]{1,0:T(8,128)(2,1)S(1)}, bf16[384,256]{1,0:T(8,128)(2,1)S(1)}, u32[]{:S(2)}, u32[]{:S(2)}) %collective-permute-start) | collective-permute-done | bytes 196640 | tf_op jit(solution)/shard_map/ppermute | solution.py:342
  69.5 0.0 copy-start.7
  69.5 0.0 copy-done
  69.5 0.0 copy-done.2
  69.5 0.0 copy-done.3
  69.5 0.0 copy-done.6
  69.5 0.6 copy-done.7
  70.2 10.9 %own_half.1.refs_8_ = bf16[304,4096]{1,0:T(8,128)(2,1)} custom-call(bf16[4096,256]{1,0:T(8,128)(2,1)} %bitcast.12, bf16[384,256]{1,0:T(8,128)(2,1)} %copy-done.7, bf16[384,256]{1,0:T(8,128)(2,1)} %copy-done.6, bf16[608,384]{1,0:T(8,128)(2,1)} %copy-done.3, bf16[608,384]{1,0:T(8,128)(2,1)} %copy-done.2, bf16[3,304,256]{2,1,0:T(8,128)(2,1)} %bitcast.14, ...), custom_call_target="tpu_custom_call" | custom-call | tf_op jit(solution)/shard_map/own_half/pallas_call | solution.py:316
  81.0 0.0 collective-permute-done.8.refs_6_
  81.1 13.3 %other_half_and_factor.1 = f32[304,4096]{1,0:T(8,128)} custom-call(bf16[4096,256]{1,0:T(8,128)(2,1)} %bitcast.13, bf16[384,256]{1,0:T(8,128)(2,1)} %copy-done.7, bf16[384,256]{1,0:T(8,128)(2,1)} %copy-done.6, bf16[608,384]{1,0:T(8,128)(2,1)} %copy-done.3, bf16[608,384]{1,0:T(8,128)(2,1)} %copy-done.2, bf16[3,304,256]{2,1,0:T(8,128)(2,1)} %maximum_select_fusion.refs_5_, ...), custom_call_target="tpu_custom_call" | custom-call | tf_op jit(solution)/shard_map/other_half_and_factor/pallas_call | solution.py:316
  (5 shorter events, 0.2 us)
Async XLA Ops:
  4.3 9.1 %copy-start.8 = (f32[2,304]{1,0:T(2,128)S(1)}, f32[2,304]{1,0:T(2,128)}, u32[]{:S(2)}) copy-start(f32[2,304]{1,0:T(2,128)} %param.15) | copy-start | bytes 7300
  4.3 10.4 %copy-start.5 = (bf16[3,256,304]{1,2,0:T(8,128)(2,1)S(1)}, bf16[3,256,304]{1,2,0:T(8,128)(2,1)}, u32[]{:S(2)}) copy-start(bf16[3,256,304]{1,2,0:T(8,128)(2,1)} %param.13) | copy-start | bytes 1400836
  4.3 54.5 %all-to-all-start = ((bf16[16,256,256]{2,1,0:T(8,128)(2,1)}), bf16[16,256,256]{2,1,0:T(8,128)(2,1)S(1)}, u32[]{:S(2)}, u32[]{:S(2)}) async-start(bf16[16,256,256]{2,1,0:T(8,128)(2,1)} %pick_rows.1), calls=%async_computation | async-start | bytes 4194304 | tf_op jit(solution)/shard_map/all_to_all | solution.py:353
  11.8 13.6 %collective-permute-start.2 = (bf16[304,768]{1,0:T(8,128)(2,1)S(1)}, bf16[304,768]{1,0:T(8,128)(2,1)S(1)}, u32[]{:S(2)}, u32[]{:S(2)}) collective-permute-start(bf16[304,768]{1,0:T(8,128)(2,1)S(1)} %pad_maximum_fusion), channel_id=1, source_target_pairs={{0,1},{1,0},{2,3},{3,2},{4,5},{5,4},{6,7},{7,6},{8,9},{9,8},{10,11... | collective-permute-start | bytes 1400840 | tf_op jit(solution)/shard_map/ppermute | solution.py:352
  14.1 23.3 %collective-permute-start.5 = (f32[304,2]{1,0:T(8,128)}, f32[304,2]{1,0:T(8,128)}, u32[]{:S(2)}, u32[]{:S(2)}) collective-permute-start(f32[304,2]{1,0:T(8,128)} %bitcast.15), channel_id=1, source_target_pairs={{0,1},{1,0},{2,3},{3,2},{4,5},{5,4},{6,7},{7,6},{8,9},{9,8},{10,11... | collective-permute-start | bytes 7304 | tf_op jit(solution)/shard_map/ppermute | solution.py:348
  15.4 11.5 %copy-start.1 = (bf16[304,608]{1,0:T(8,128)(2,1)S(1)}, bf16[304,608]{1,0:T(8,128)(2,1)}, u32[]{:S(2)}) copy-start(bf16[304,608]{1,0:T(8,128)(2,1)} %param.16) | copy-start | bytes 1108996
  15.4 18.4 %collective-permute-start.3 = (bf16[3,152,256]{2,1,0:T(8,128)(2,1)}, bf16[3,152,256]{2,1,0:T(8,128)(2,1)}, u32[]{:S(2)}, u32[]{:S(2)}) collective-permute-start(bf16[3,152,256]{2,1,0:T(8,128)(2,1)} %dynamic-slice_bitcast_fusion), channel_id=1, source_target_pairs={{0,1},{1,0},{2,3},{3,2},{4,5},{5,4},{6,7},{7,6},{8,9},{9,8},{10,11... | collective-permute-start | bytes 700424 | tf_op jit(solution)/shard_map/ppermute | solution.py:346
  20.0 13.9 %copy-start.9 = (s32[128]{0:T(128)S(1)}, s32[128]{0:T(128)}, u32[]{:S(2)}) copy-start(s32[128]{0:T(128)} %param.12) | copy-start | bytes 1540
  25.4 12.2 %copy-start.4 = (bf16[304,768]{1,0:T(8,128)(2,1)}, bf16[304,768]{1,0:T(8,128)(2,1)S(1)}, u32[]{:S(2)}) copy-start(bf16[304,768]{1,0:T(8,128)(2,1)S(1)} %collective-permute-done.2.refs_7_) | copy-start | bytes 1400836
  25.4 55.7 %collective-permute-start.8 = (bf16[304,3328]{1,0:T(8,128)(2,1)}, bf16[304,3328]{1,0:T(8,128)(2,1)}, u32[]{:S(2)}, u32[]{:S(2)}) collective-permute-start(bf16[304,3328]{1,0:T(8,128)(2,1)} %slice.33), channel_id=1, source_target_pairs={{0,1},{1,0},{2,3},{3,2},{4,5},{5,4},{6,7},{7,6},{8,9},{9,8},{10,11... | collective-permute-start | bytes 6070280 | tf_op jit(solution)/shard_map/ppermute | solution.py:356
  33.8 1.7 %collective-permute-start.4 = (bf16[3,152,256]{2,1,0:T(8,128)(2,1)}, bf16[3,152,256]{2,1,0:T(8,128)(2,1)S(1)}, u32[]{:S(2)}, u32[]{:S(2)}) collective-permute-start(bf16[3,152,256]{2,1,0:T(8,128)(2,1)} %collective-permute-done.3), channel_id=1, source_target_pairs={{0,2},{2,0},{4,6},{6,4},{8,10},{10,8},{12,14},{14,12},{16,18},{18,... | collective-permute-start | bytes 700424 | tf_op jit(solution)/shard_map/ppermute | solution.py:357
  38.5 25.3 %collective-permute-start.7 = (bf16[608,384]{1,0:T(8,128)(2,1)}, bf16[608,384]{1,0:T(8,128)(2,1)S(1)}, u32[]{:S(2)}, u32[]{:S(2)}) collective-permute-start(bf16[608,384]{1,0:T(8,128)(2,1)} %get-tuple-element.31), channel_id=1, source_target_pairs={{2,0},{4,2},{6,4},{8,6},{10,8},{12,10},{14,12},{16,14},{18,16},{20... | collective-permute-start | bytes 1400840 | tf_op jit(solution)/shard_map/ppermute | solution.py:381
  41.6 22.2 %collective-permute-start.6 = (bf16[608,384]{1,0:T(8,128)(2,1)S(1)}, bf16[608,384]{1,0:T(8,128)(2,1)S(1)}, u32[]{:S(2)}, u32[]{:S(2)}) collective-permute-start(bf16[608,384]{1,0:T(8,128)(2,1)S(1)} %get-tuple-element.32), channel_id=1, source_target_pairs={{0,2},{2,4},{4,6},{6,8},{8,10},{10,12},{12,14},{14,16},{16,18},{18... | collective-permute-start | bytes 1400840 | tf_op jit(solution)/shard_map/ppermute | solution.py:380
  58.8 10.7 %copy-start = (bf16[16,256,256]{2,1,0:T(8,128)(2,1)}, bf16[16,256,256]{2,1,0:T(8,128)(2,1)S(1)}, u32[]{:S(2)}) copy-start(bf16[16,256,256]{2,1,0:T(8,128)(2,1)S(1)} %all-to-all-done) | copy-start | bytes 6291460
  58.8 6.0 %collective-permute-start.1 = (bf16[384,256]{1,0:T(8,128)(2,1)S(1)}, bf16[384,256]{1,0:T(8,128)(2,1)S(1)}, u32[]{:S(2)}, u32[]{:S(2)}) collective-permute-start(bf16[384,256]{1,0:T(8,128)(2,1)S(1)} %get-tuple-element.29), channel_id=1, source_target_pairs={{2,0},{4,2},{6,4},{8,6},{10,8},{12,10},{14,12},{16,14},{18,16},{20... | collective-permute-start | bytes 589832 | tf_op jit(solution)/shard_map/ppermute | solution.py:342
  61.6 7.9 %collective-permute-start = (bf16[384,256]{1,0:T(8,128)(2,1)S(1)}, bf16[384,256]{1,0:T(8,128)(2,1)S(1)}, u32[]{:S(2)}, u32[]{:S(2)}) collective-permute-start(bf16[384,256]{1,0:T(8,128)(2,1)S(1)} %get-tuple-element.30), channel_id=1, source_target_pairs={{0,2},{2,4},{4,6},{6,8},{8,10},{10,12},{12,14},{14,16},{16,18},{18... | collective-permute-start | bytes 589832 | tf_op jit(solution)/shard_map/ppermute | solution.py:342
  63.7 5.8 %copy-start.2 = (bf16[608,384]{1,0:T(8,128)(2,1)}, bf16[608,384]{1,0:T(8,128)(2,1)S(1)}, u32[]{:S(2)}) copy-start(bf16[608,384]{1,0:T(8,128)(2,1)S(1)} %collective-permute-done.7.refs_4_) | copy-start | bytes 1400836
  63.8 5.8 %copy-start.3 = (bf16[608,384]{1,0:T(8,128)(2,1)}, bf16[608,384]{1,0:T(8,128)(2,1)S(1)}, u32[]{:S(2)}) copy-start(bf16[608,384]{1,0:T(8,128)(2,1)S(1)} %collective-permute-done.6.refs_3_) | copy-start | bytes 1400836
  64.8 4.7 %copy-start.6 = (bf16[384,256]{1,0:T(8,128)(2,1)}, bf16[384,256]{1,0:T(8,128)(2,1)S(1)}, u32[]{:S(2)}) copy-start(bf16[384,256]{1,0:T(8,128)(2,1)S(1)} %collective-permute-done.1.refs_2_) | copy-start | bytes 589828
  69.5 0.7 copy-start.7

commit v6 on v5

--- a/solution.py
+++ b/solution.py
@@ -126,15 +126,15 @@
 
 
 def half_kernel(last, *refs):
-    prof_hbm, prof_top_hbm, prof_bot_hbm, top_hbm, bot_hbm, jac_hbm = refs[:6]
+    prof_hbm, prof_near_hbm, prof_next_hbm, top_hbm, bot_hbm, jac_hbm = refs[:6]
     if last:
-        mid_hbm, bnd_hbm, smooth_hbm, factor_hbm, rates_ref, rows_ref, shift_ref = refs[6:13]
-        out_hbm, prof, obs, jac_ref, field, moved_a, moved_b, smooth, sems, out_sems, out, factor_ref = refs[13:]
+        mid_hbm, bnd_hbm, smooth_hbm, factor_hbm, odd_ref, rates_ref, rows_ref, shift_ref = refs[6:14]
+        out_hbm, prof, obs, jac_ref, field, moved_a, moved_b, smooth, sems, out_sems, out, factor_ref = refs[14:]
     else:
-        obs_hbm, rates_ref, rows_ref, shift_ref = refs[6:10]
-        out_hbm, prof, obs, jac_ref, field, moved_a, moved_b, smooth, sems, out_sems = refs[10:]
+        obs_hbm, odd_ref, rates_ref, rows_ref, shift_ref = refs[6:11]
+        out_hbm, prof, obs, jac_ref, field, moved_a, moved_b, smooth, sems, out_sems = refs[11:]
     own, pixels = jac_hbm.shape[1], prof_hbm.shape[0]
-    rim = prof_top_hbm.shape[0]
+    rim = prof_near_hbm.shape[0]
     lines = pixels // XTRACK
     wide = 2 * XTRACK
     full = pixels + 2 * rim
@@ -157,7 +157,8 @@
         waits.append([])
         if n == 0:
             fetch(jac_hbm, jac_ref)
-            fetch(prof_top_hbm, prof.at[pl.ds(0, rim), :])
+            for src, number in ((prof_near_hbm, 1 - odd_ref[0]), (prof_next_hbm, odd_ref[0])):
+                fetch(src, prof.at[pl.ds(pl.multiple_of(number * (rim + pixels), XTRACK), rim), :])
             fetch(top_hbm.at[part, :], obs.at[:, pl.ds(0, rim)])
         low = max(cuts[n] * wide - rim, 0)
         high = min(cuts[n + 1] * wide - rim, pixels)
@@ -174,7 +175,6 @@
                     obs.at[:, pl.ds(rim + begin_n, end_n - begin_n)],
                 )
         if n == SEGMENTS - 1:
-            fetch(prof_bot_hbm, prof.at[pl.ds(rim + pixels, rim), :])
             fetch(bot_hbm.at[part, :], obs.at[:, pl.ds(rim + pixels, rim)])
     if last:
         waits.append([])
@@ -221,7 +221,9 @@
         along = jnp.broadcast_to(rates_ref[rows, 0:1], (16, XTRACK))
         cross = jnp.broadcast_to(rates_ref[rows, 1:2], (16, XTRACK))
         stay = 1.0 - 2.0 * along - 2.0 * cross
+        along, cross = along / stay, cross / stay
         cross = [3.0 * cross, 3.0 * cross * cross, cross * cross * cross]
+        stay = stay * stay * stay
         fields = [{}, {}, {}, {}]
         for j in range(total):
             fields[0][j] = field[rows, j * XTRACK : (j + 1) * XTRACK]
@@ -231,7 +233,7 @@
                     continue
                 prev = fields[k - 1]
                 new = (
-                    stay * prev[at]
+                    prev[at]
                     + along * (prev[at - 1] + prev[at + 1])
                     + cross[k - 1] * moved[(at - 1) * 16 : at * 16, (k - 1) * XTRACK : k * XTRACK]
                 )
@@ -243,7 +245,7 @@
                 del prev[at - 1]
                 if k == HALO:
                     line = at - HALO
-                    smooth[chan, line * XTRACK : (line + 1) * XTRACK] = new.astype(smooth.dtype)
+                    smooth[chan, line * XTRACK : (line + 1) * XTRACK] = (new * stay).astype(smooth.dtype)
 
     for n in range(SEGMENTS):
         for copy in waits[n]:
@@ -317,7 +319,8 @@
         functools.partial(half_kernel, last),
         out_shape=jax.ShapeDtypeStruct((own, pixels), dtype),
         in_specs=[pl.BlockSpec(memory_space=pl.ANY)] * len(anys)
-        + [pl.BlockSpec(memory_space=pltpu.VMEM)] * len(whole),
+        + [pl.BlockSpec(memory_space=pltpu.SMEM)]
+        + [pl.BlockSpec(memory_space=pltpu.VMEM)] * (len(whole) - 1),
         out_specs=pl.BlockSpec(memory_space=pl.ANY),
         scratch_shapes=scratch,
         compiler_params=pltpu.CompilerParams(vmem_limit_bytes=LAST_LIMIT if last else OWN_LIMIT),
@@ -334,12 +337,6 @@
     swap = [(0, 1), (1, 0)]
     forward = [(i, i + 1) for i in range(swath - 1)]
     backward = [(i + 1, i) for i in range(swath - 1)]
-
-    def halos(block, axis):
-        size = block.shape[axis]
-        tail = lax.slice_in_dim(block, size - rim, size, axis=axis)
-        head = lax.slice_in_dim(block, 0, rim, axis=axis)
-        return lax.ppermute(tail, "swath", forward), lax.ppermute(head, "swath", backward)
 
     jac_own = jnp.swapaxes(jacobian, 1, 2)
     jac_half = lax.dynamic_slice_in_dim(jac_own, (place % 2) * (own // 2), own // 2, axis=1)
@@ -381,17 +378,23 @@
     obs_bot = lax.ppermute(bnd_both[:, :rim], "swath", backward)
 
     profiles = incoming.reshape(pixels, grid_profiles.shape[1])
-    prof_halos = halos(profiles, 0)
+    odd = place % 2
+    head, tail = profiles[:rim], profiles[pixels - rim :]
+    pairs = [(i, i ^ 1) for i in range(swath)]
+    between = [(i, (i + 1 if i % 2 else i - 1)) for i in range(1, swath - 1)]
+    prof_near = lax.ppermute(jnp.where(odd == 1, head, tail), "swath", pairs)
+    prof_next = lax.ppermute(jnp.where(odd == 1, tail, head), "swath", between)
+    odd = jnp.full((1,), odd, jnp.int32)
 
     smooth_own = half_call(
         False,
-        (profiles, *prof_halos, obs_top, obs_bot, jac_own, observed),
-        (rates_own, rows, shift),
+        (profiles, prof_near, prof_next, obs_top, obs_bot, jac_own, observed),
+        (odd, rates_own, rows, shift),
     )
     return half_call(
         True,
-        (profiles, *prof_halos, obs_top, obs_bot, jac_oth, mid_oth, bnd_oth, smooth_own, factor_two),
-        (rates_oth, rows, shift),
+        (profiles, prof_near, prof_next, obs_top, obs_bot, jac_oth, mid_oth, bnd_oth, smooth_own, factor_two),
+        (odd, rates_oth, rows, shift),
     )
 
 

time: 95 us -> 92.7 us (0.976); the launches traced: 94.6 us -> 91.2 us
  starting transfers between devices: 21.3 us -> 19.5 us
    ppermute x2, waiting for transfers between devices: 5.74 us -> 3.47 us  [the longest x1 3.47 us: on_device_two(): prof_next = lax.ppermute(jnp.where(odd == 1, tail, head), 'swath', between)]
    ppermute x2, starting transfers between devices: 4.88 us -> 3.03 us  [the longest x1 2.96 us: on_device_two(): prof_next = lax.ppermute(jnp.where(odd == 1, tail, head), 'swath', between)]
    ppermute x1, waiting for transfers between devices: 0.01 us -> 1.46 us  [on_device_two(): obs_top = lax.ppermute(bnd_both[:, rim:], 'swath', forward)]
  transfers between devices with their start and end apart: 10 -> 10, of which waited for: 6 -> 6; matrix products, arithmetic and copies ran while one was open for 11% -> 12% of each run, Pallas kernels for 11% -> 11%
where the time goes in v6:
time: 92.7 us; the launch traced here: 91.2 us
  waiting for transfers between devices  32.3 us (35%)
  Pallas kernels  27.7 us (30%)
  starting transfers between devices  19.5 us (21%)
  local copies, waits for them, and re-layouts  7.66 us (8%)
  other arithmetic  3.71 us (4%)
    pallas_call x2, Pallas kernels, half_call(): pl.pallas_call(functools.partial(half_kernel, last), out_shape=jax.ShapeD...  23.5 us
    all_to_all x1, waiting for transfers between devices, on_device_two(): lax.all_to_all(outgoing, 'swath', split_axis=0, concat_axis=0, tiled=True)  15.3 us
    all_to_all x1, starting transfers between devices, on_device_two(): lax.all_to_all(outgoing, 'swath', split_axis=0, concat_axis=0, tiled=True)  6.3 us
    ppermute x1, waiting for transfers between devices, on_device_two(): jac_near = lax.ppermute(jac_half, 'chan', swap)  5.83 us
    ppermute x1, waiting for transfers between devices, on_device_two(): bnd_oth = lax.ppermute(bnd_own, 'chan', swap)  5.4 us
    pallas_call x1, Pallas kernels, gather_rows(): pl.pallas_call(gather_kernel, out_shape=jax.ShapeDtypeStruct(shape, grid_...  4.26 us
    ppermute x1, waiting for transfers between devices, on_device_two(): prof_next = lax.ppermute(jnp.where(odd == 1, tail, head), 'swath', between)  3.47 us
    ppermute x1, starting transfers between devices, on_device_two(): obs_bot = lax.ppermute(bnd_both[:, :rim], 'swath', backward)  3.1 us
  transfers between devices with their start and end apart: 10, of which 6 were waited for; matrix products, arithmetic and copies ran while one was open for 12% of the time, Pallas kernels for 11%

profile of v6, /device:TPU:16, one launch (start us, length us, event | category | flops | bytes accessed | tf_op | source)
XLA Modules:
  0.0 91.2 jit_solution(18406140769394176188)
XLA Ops:
  0.0 4.3 %pick_rows.1 = bf16[16,256,256]{2,1,0:T(8,128)(2,1)} custom-call(s32[16,256]{1,0:T(8,128)} %bitcast.18, s32[1,16]{1,0:T(1,128)} %counts_hbm.1, bf16[1024,256]{1,0:T(8,128)(2,1)} %grid_hbm.1), custom_call_target="tpu_custom_call" | custom-call | tf_op jit(solution)/shard_map/pick_rows/pallas_call | solution.py:110
  4.3 0.0 copy-start.8
  4.3 0.0 copy-start.5
  4.3 6.3 %all-to-all-start = ((bf16[16,256,256]{2,1,0:T(8,128)(2,1)}), bf16[16,256,256]{2,1,0:T(8,128)(2,1)S(1)}, u32[]{:S(2)}, u32[]{:S(2)}) async-start(bf16[16,256,256]{2,1,0:T(8,128)(2,1)} %pick_rows.1), calls=%async_computation | async-start | bytes 4194304 | tf_op jit(solution)/shard_map/all_to_all | solution.py:350
  10.6 1.1 %fusion = (bf16[304,384]{1,0:T(8,128)(2,1)S(1)}, bf16[304,384]{1,0:T(8,128)(2,1)S(1)}) fusion(bf16[304,4096]{1,0:T(8,128)(2,1)} %refs_6_.1), kind=kLoop, calls=%fused_computation.11 | loop fusion | bytes 933888 | tf_op jit(solution)/shard_map/slice | solution.py:348
  11.8 1.6 %collective-permute-start.2 = (bf16[304,768]{1,0:T(8,128)(2,1)S(1)}, bf16[304,768]{1,0:T(8,128)(2,1)S(1)}, u32[]{:S(2)}, u32[]{:S(2)}) collective-permute-start(bf16[304,768]{1,0:T(8,128)(2,1)S(1)} %pad_maximum_fusion), channel_id=1, source_target_pairs={{0,1},{1,0},{2,3},{3,2},{4,5},{5,4},{6,7},{7,6},{8,9},{9,8},{10,11... | collective-permute-start | bytes 1400840 | tf_op jit(solution)/shard_map/ppermute | solution.py:349
  13.3 0.0 copy-done.8
  13.3 0.8 copy.10
  14.1 0.5 collective-permute-start.5
  14.7 0.0 copy-done.5
  14.7 0.7 dynamic-slice_bitcast_fusion
  15.4 0.0 copy-start.1
  15.4 1.5 %collective-permute-start.3 = (bf16[3,152,256]{2,1,0:T(8,128)(2,1)}, bf16[3,152,256]{2,1,0:T(8,128)(2,1)}, u32[]{:S(2)}, u32[]{:S(2)}) collective-permute-start(bf16[3,152,256]{2,1,0:T(8,128)(2,1)} %dynamic-slice_bitcast_fusion), channel_id=1, source_target_pairs={{0,1},{1,0},{2,3},{3,2},{4,5},{5,4},{6,7},{7,6},{8,9},{9,8},{10,11... | collective-permute-start | bytes 700424 | tf_op jit(solution)/shard_map/ppermute | solution.py:343
  16.9 3.1 %slice.33 = bf16[304,3328]{1,0:T(8,128)(2,1)} slice(bf16[304,4096]{1,0:T(8,128)(2,1)} %refs_6_.1), slice={[0:304], [384:3712]} | slice | bytes 4046848 | tf_op jit(solution)/shard_map/slice | solution.py:351
  20.0 0.0 copy-start.9
  20.0 5.4 %collective-permute-done.2.refs_7_ = bf16[304,768]{1,0:T(8,128)(2,1)S(1)} collective-permute-done((bf16[304,768]{1,0:T(8,128)(2,1)S(1)}, bf16[304,768]{1,0:T(8,128)(2,1)S(1)}, u32[]{:S(2)}, u32[]{:S(2)}) %collective-permute-start.2) | collective-permute-done | bytes 466976 | tf_op jit(solution)/shard_map/ppermute | solution.py:349
  25.4 0.0 copy-start.2
  25.4 1.5 %collective-permute-start.8 = (bf16[304,3328]{1,0:T(8,128)(2,1)}, bf16[304,3328]{1,0:T(8,128)(2,1)}, u32[]{:S(2)}, u32[]{:S(2)}) collective-permute-start(bf16[304,3328]{1,0:T(8,128)(2,1)} %slice.33), channel_id=1, source_target_pairs={{0,1},{1,0},{2,3},{3,2},{4,5},{5,4},{6,7},{7,6},{8,9},{9,8},{10,11... | collective-permute-start | bytes 6070280 | tf_op jit(solution)/shard_map/ppermute | solution.py:353
  26.9 0.0 copy-done.1
  26.9 0.1 fusion.2
  27.0 1.0 %maximum_select_fusion.1.refs_9_ = bf16[304,608]{1,0:T(8,128)(2,1)} fusion(bf16[304,608]{1,0:T(8,128)(2,1)S(1)} %copy-done.1, bf16[304,304]{1,0:T(8,128)(2,1)S(1)} %get-tuple-element.34, bf16[304,304]{1,0:T(8,128)(2,1)S(1)} %get-tuple-element.33, pred[]{:T(512)S(6)} %eq.16), kind=kLoop, calls=%fused_computation.2 | loop fusion | flops 924160 | bytes 1108993 | tf_op jit(solution)/shard_map/jit(_where)/select_n | solution.py:371
  28.0 5.8 %collective-permute-done.3 = bf16[3,152,256]{2,1,0:T(8,128)(2,1)} collective-permute-done((bf16[3,152,256]{2,1,0:T(8,128)(2,1)}, bf16[3,152,256]{2,1,0:T(8,128)(2,1)}, u32[]{:S(2)}, u32[]{:S(2)}) %collective-permute-start.3) | collective-permute-done | bytes 233504 | tf_op jit(solution)/shard_map/ppermute | solution.py:343
  33.8 0.0 collective-permute-start.4
  33.8 0.0 copy-done.9
  33.9 0.1 pad.4.clone
  33.9 0.1 pad.5.clone
  34.0 0.7 maximum_maximum_fusion.refs_9_.refs_12_
  34.7 0.8 collective-permute-done.4
  35.5 2.0 %maximum_select_fusion.refs_5_ = bf16[3,304,256]{2,1,0:T(8,128)(2,1)} fusion(bf16[3,152,256]{2,1,0:T(8,128)(2,1)S(1)} %collective-permute-done.4, bf16[3,152,256]{2,1,0:T(8,128)(2,1)} %collective-permute-done.3, pred[]{:T(512)S(6)} %eq.15), kind=kLoop, calls=%fused_computation.1 | loop fusion | flops 2101248 | bytes 933889 | tf_op jit(solution)/shard_map/jit(_where)/select_n | solution.py:355
  37.5 0.0 collective-permute-done.5.refs_11_
  37.6 0.0 copy-done.2
  37.6 0.9 fusion.1
  38.5 3.1 %collective-permute-start.7 = (bf16[608,384]{1,0:T(8,128)(2,1)}, bf16[608,384]{1,0:T(8,128)(2,1)S(1)}, u32[]{:S(2)}, u32[]{:S(2)}) collective-permute-start(bf16[608,384]{1,0:T(8,128)(2,1)} %get-tuple-element.31), channel_id=1, source_target_pairs={{2,0},{4,2},{6,4},{8,6},{10,8},{12,10},{14,12},{16,14},{18,16},{20... | collective-permute-start | bytes 1400840 | tf_op jit(solution)/shard_map/ppermute | solution.py:378
  41.6 1.9 %collective-permute-start.6 = (bf16[608,384]{1,0:T(8,128)(2,1)S(1)}, bf16[608,384]{1,0:T(8,128)(2,1)S(1)}, u32[]{:S(2)}, u32[]{:S(2)}) collective-permute-start(bf16[608,384]{1,0:T(8,128)(2,1)S(1)} %get-tuple-element.32), channel_id=1, source_target_pairs={{0,2},{2,4},{4,6},{6,8},{8,10},{10,12},{12,14},{14,16},{16,18},{18... | collective-permute-start | bytes 1400840 | tf_op jit(solution)/shard_map/ppermute | solution.py:377
  43.5 15.3 %all-to-all-done = bf16[16,256,256]{2,1,0:T(8,128)(2,1)S(1)} async-done(((bf16[16,256,256]{2,1,0:T(8,128)(2,1)}), bf16[16,256,256]{2,1,0:T(8,128)(2,1)S(1)}, u32[]{:S(2)}, u32[]{:S(2)}) %all-to-all-start) | async-done | bytes 2097184 | tf_op jit(solution)/shard_map/all_to_all | solution.py:350
  58.8 0.0 copy-start
  58.8 3.0 %collective-permute-start.1 = (bf16[384,256]{1,0:T(8,128)(2,1)S(1)}, bf16[384,256]{1,0:T(8,128)(2,1)S(1)}, u32[]{:S(2)}, u32[]{:S(2)}) collective-permute-start(bf16[384,256]{1,0:T(8,128)(2,1)S(1)} %get-tuple-element.29), channel_id=1, source_target_pairs={{2,4},{4,2},{6,8},{8,6},{10,12},{12,10},{14,16},{16,14},{18,20},{2... | collective-permute-start | bytes 589832 | tf_op jit(solution)/shard_map/ppermute | solution.py:386
  61.8 0.1 collective-permute-start
  61.9 0.0 collective-permute-done.7.refs_4_
  61.9 0.0 copy-start.3
  61.9 1.5 %collective-permute-done.6.refs_3_ = bf16[608,384]{1,0:T(8,128)(2,1)S(1)} collective-permute-done((bf16[608,384]{1,0:T(8,128)(2,1)S(1)}, bf16[608,384]{1,0:T(8,128)(2,1)S(1)}, u32[]{:S(2)}, u32[]{:S(2)}) %collective-permute-start.6) | collective-permute-done | bytes 466976 | tf_op jit(solution)/shard_map/ppermute | solution.py:377
  63.4 0.0 copy-start.4
  63.4 3.5 %collective-permute-done.1.refs_2_ = bf16[384,256]{1,0:T(8,128)(2,1)S(1)} collective-permute-done((bf16[384,256]{1,0:T(8,128)(2,1)S(1)}, bf16[384,256]{1,0:T(8,128)(2,1)S(1)}, u32[]{:S(2)}, u32[]{:S(2)}) %collective-permute-start.1) | collective-permute-done | bytes 196640 | tf_op jit(solution)/shard_map/ppermute | solution.py:386
  66.8 0.0 copy-start.6
  66.8 0.0 collective-permute-done.refs_1_
  66.8 0.0 copy-start.7
  66.8 0.0 copy-done
  66.9 0.0 copy-done.3
  66.9 0.0 copy-done.4
  66.9 0.6 copy-done.6
  67.5 0.1 copy-done.7
  67.6 10.5 %own_half.1.refs_8_ = bf16[304,4096]{1,0:T(8,128)(2,1)} custom-call(bf16[4096,256]{1,0:T(8,128)(2,1)} %bitcast.13, bf16[384,256]{1,0:T(8,128)(2,1)} %copy-done.7, bf16[384,256]{1,0:T(8,128)(2,1)} %copy-done.6, bf16[608,384]{1,0:T(8,128)(2,1)} %copy-done.4, bf16[608,384]{1,0:T(8,128)(2,1)} %copy-done.3, bf16[3,304,256]{2,1,0:T(8,128)(2,1)} %bitcast.15, ...), custom_call_target="tpu_custom_call" | custom-call | tf_op jit(solution)/shard_map/own_half/pallas_call | solution.py:318
  78.1 0.0 collective-permute-done.8.refs_6_
  78.1 13.0 %other_half_and_factor.1 = f32[304,4096]{1,0:T(8,128)} custom-call(bf16[4096,256]{1,0:T(8,128)(2,1)} %bitcast.14, bf16[384,256]{1,0:T(8,128)(2,1)} %copy-done.7, bf16[384,256]{1,0:T(8,128)(2,1)} %copy-done.6, bf16[608,384]{1,0:T(8,128)(2,1)} %copy-done.4, bf16[608,384]{1,0:T(8,128)(2,1)} %copy-done.3, bf16[3,304,256]{2,1,0:T(8,128)(2,1)} %maximum_select_fusion.refs_5_, ...), custom_call_target="tpu_custom_call" | custom-call | tf_op jit(solution)/shard_map/other_half_and_factor/pallas_call | solution.py:318
  (5 shorter events, 0.2 us)
Async XLA Ops:
  4.3 9.1 %copy-start.8 = (f32[2,304]{1,0:T(2,128)S(1)}, f32[2,304]{1,0:T(2,128)}, u32[]{:S(2)}) copy-start(f32[2,304]{1,0:T(2,128)} %param.15) | copy-start | bytes 7300
  4.3 10.4 %copy-start.5 = (bf16[3,256,304]{1,2,0:T(8,128)(2,1)S(1)}, bf16[3,256,304]{1,2,0:T(8,128)(2,1)}, u32[]{:S(2)}) copy-start(bf16[3,256,304]{1,2,0:T(8,128)(2,1)} %param.13) | copy-start | bytes 1400836
  4.3 54.5 %all-to-all-start = ((bf16[16,256,256]{2,1,0:T(8,128)(2,1)}), bf16[16,256,256]{2,1,0:T(8,128)(2,1)S(1)}, u32[]{:S(2)}, u32[]{:S(2)}) async-start(bf16[16,256,256]{2,1,0:T(8,128)(2,1)} %pick_rows.1), calls=%async_computation | async-start | bytes 4194304 | tf_op jit(solution)/shard_map/all_to_all | solution.py:350
  11.8 13.6 %collective-permute-start.2 = (bf16[304,768]{1,0:T(8,128)(2,1)S(1)}, bf16[304,768]{1,0:T(8,128)(2,1)S(1)}, u32[]{:S(2)}, u32[]{:S(2)}) collective-permute-start(bf16[304,768]{1,0:T(8,128)(2,1)S(1)} %pad_maximum_fusion), channel_id=1, source_target_pairs={{0,1},{1,0},{2,3},{3,2},{4,5},{5,4},{6,7},{7,6},{8,9},{9,8},{10,11... | collective-permute-start | bytes 1400840 | tf_op jit(solution)/shard_map/ppermute | solution.py:349
  14.1 23.3 %collective-permute-start.5 = (f32[304,2]{1,0:T(8,128)}, f32[304,2]{1,0:T(8,128)}, u32[]{:S(2)}, u32[]{:S(2)}) collective-permute-start(f32[304,2]{1,0:T(8,128)} %bitcast.16), channel_id=1, source_target_pairs={{0,1},{1,0},{2,3},{3,2},{4,5},{5,4},{6,7},{7,6},{8,9},{9,8},{10,11... | collective-permute-start | bytes 7304 | tf_op jit(solution)/shard_map/ppermute | solution.py:345
  15.4 11.5 %copy-start.1 = (bf16[304,608]{1,0:T(8,128)(2,1)S(1)}, bf16[304,608]{1,0:T(8,128)(2,1)}, u32[]{:S(2)}) copy-start(bf16[304,608]{1,0:T(8,128)(2,1)} %param.16) | copy-start | bytes 1108996
  15.4 18.4 %collective-permute-start.3 = (bf16[3,152,256]{2,1,0:T(8,128)(2,1)}, bf16[3,152,256]{2,1,0:T(8,128)(2,1)}, u32[]{:S(2)}, u32[]{:S(2)}) collective-permute-start(bf16[3,152,256]{2,1,0:T(8,128)(2,1)} %dynamic-slice_bitcast_fusion), channel_id=1, source_target_pairs={{0,1},{1,0},{2,3},{3,2},{4,5},{5,4},{6,7},{7,6},{8,9},{9,8},{10,11... | collective-permute-start | bytes 700424 | tf_op jit(solution)/shard_map/ppermute | solution.py:343
  20.0 13.9 %copy-start.9 = (s32[128]{0:T(128)S(1)}, s32[128]{0:T(128)}, u32[]{:S(2)}) copy-start(s32[128]{0:T(128)} %param.12) | copy-start | bytes 1540
  25.4 12.2 %copy-start.2 = (bf16[304,768]{1,0:T(8,128)(2,1)}, bf16[304,768]{1,0:T(8,128)(2,1)S(1)}, u32[]{:S(2)}) copy-start(bf16[304,768]{1,0:T(8,128)(2,1)S(1)} %collective-permute-done.2.refs_7_) | copy-start | bytes 1400836
  25.4 52.7 %collective-permute-start.8 = (bf16[304,3328]{1,0:T(8,128)(2,1)}, bf16[304,3328]{1,0:T(8,128)(2,1)}, u32[]{:S(2)}, u32[]{:S(2)}) collective-permute-start(bf16[304,3328]{1,0:T(8,128)(2,1)} %slice.33), channel_id=1, source_target_pairs={{0,1},{1,0},{2,3},{3,2},{4,5},{5,4},{6,7},{7,6},{8,9},{9,8},{10,11... | collective-permute-start | bytes 6070280 | tf_op jit(solution)/shard_map/ppermute | solution.py:353
  33.8 1.7 %collective-permute-start.4 = (bf16[3,152,256]{2,1,0:T(8,128)(2,1)}, bf16[3,152,256]{2,1,0:T(8,128)(2,1)S(1)}, u32[]{:S(2)}, u32[]{:S(2)}) collective-permute-start(bf16[3,152,256]{2,1,0:T(8,128)(2,1)} %collective-permute-done.3), channel_id=1, source_target_pairs={{0,2},{2,0},{4,6},{6,4},{8,10},{10,8},{12,14},{14,12},{16,18},{18,... | collective-permute-start | bytes 700424 | tf_op jit(solution)/shard_map/ppermute | solution.py:354
  38.5 23.4 %collective-permute-start.7 = (bf16[608,384]{1,0:T(8,128)(2,1)}, bf16[608,384]{1,0:T(8,128)(2,1)S(1)}, u32[]{:S(2)}, u32[]{:S(2)}) collective-permute-start(bf16[608,384]{1,0:T(8,128)(2,1)} %get-tuple-element.31), channel_id=1, source_target_pairs={{2,0},{4,2},{6,4},{8,6},{10,8},{12,10},{14,12},{16,14},{18,16},{20... | collective-permute-start | bytes 1400840 | tf_op jit(solution)/shard_map/ppermute | solution.py:378
  41.6 21.8 %collective-permute-start.6 = (bf16[608,384]{1,0:T(8,128)(2,1)S(1)}, bf16[608,384]{1,0:T(8,128)(2,1)S(1)}, u32[]{:S(2)}, u32[]{:S(2)}) collective-permute-start(bf16[608,384]{1,0:T(8,128)(2,1)S(1)} %get-tuple-element.32), channel_id=1, source_target_pairs={{0,2},{2,4},{4,6},{6,8},{8,10},{10,12},{12,14},{14,16},{16,18},{18... | collective-permute-start | bytes 1400840 | tf_op jit(solution)/shard_map/ppermute | solution.py:377
  58.8 8.0 %copy-start = (bf16[16,256,256]{2,1,0:T(8,128)(2,1)}, bf16[16,256,256]{2,1,0:T(8,128)(2,1)S(1)}, u32[]{:S(2)}) copy-start(bf16[16,256,256]{2,1,0:T(8,128)(2,1)S(1)} %all-to-all-done) | copy-start | bytes 6291460
  58.8 8.0 %collective-permute-start.1 = (bf16[384,256]{1,0:T(8,128)(2,1)S(1)}, bf16[384,256]{1,0:T(8,128)(2,1)S(1)}, u32[]{:S(2)}, u32[]{:S(2)}) collective-permute-start(bf16[384,256]{1,0:T(8,128)(2,1)S(1)} %get-tuple-element.29), channel_id=1, source_target_pairs={{2,4},{4,2},{6,8},{8,6},{10,12},{12,10},{14,16},{16,14},{18,20},{2... | collective-permute-start | bytes 589832 | tf_op jit(solution)/shard_map/ppermute | solution.py:386
  61.8 5.0 %collective-permute-start = (bf16[384,256]{1,0:T(8,128)(2,1)S(1)}, bf16[384,256]{1,0:T(8,128)(2,1)S(1)}, u32[]{:S(2)}, u32[]{:S(2)}) collective-permute-start(bf16[384,256]{1,0:T(8,128)(2,1)S(1)} %get-tuple-element.30), channel_id=1, source_target_pairs={{0,2},{2,0},{4,6},{6,4},{8,10},{10,8},{12,14},{14,12},{16,18},{18,... | collective-permute-start | bytes 589832 | tf_op jit(solution)/shard_map/ppermute | solution.py:385
  61.9 5.0 %copy-start.3 = (bf16[608,384]{1,0:T(8,128)(2,1)}, bf16[608,384]{1,0:T(8,128)(2,1)S(1)}, u32[]{:S(2)}) copy-start(bf16[608,384]{1,0:T(8,128)(2,1)S(1)} %collective-permute-done.7.refs_4_) | copy-start | bytes 1400836
  63.4 3.5 %copy-start.4 = (bf16[608,384]{1,0:T(8,128)(2,1)}, bf16[608,384]{1,0:T(8,128)(2,1)S(1)}, u32[]{:S(2)}) copy-start(bf16[608,384]{1,0:T(8,128)(2,1)S(1)} %collective-permute-done.6.refs_3_) | copy-start | bytes 1400836
  66.8 0.7 copy-start.6
  66.8 0.7 copy-start.7

commit v7 on v6

--- a/solution.py
+++ b/solution.py
@@ -128,12 +128,14 @@
 def half_kernel(last, *refs):
     prof_hbm, prof_near_hbm, prof_next_hbm, top_hbm, bot_hbm, jac_hbm = refs[:6]
     if last:
-        mid_hbm, bnd_hbm, smooth_hbm, factor_hbm, odd_ref, rates_ref, rows_ref, shift_ref = refs[6:14]
-        out_hbm, prof, obs, jac_ref, field, moved_a, moved_b, smooth, sems, out_sems, out, factor_ref = refs[14:]
+        mid_hbm, bnd_hbm, smooth_hbm, factor_hbm, rates_hbm, rows_hbm, shift_hbm = refs[6:13]
+        out_hbm, *refs, out, factor_ref = refs[13:]
     else:
-        obs_hbm, odd_ref, rates_ref, rows_ref, shift_ref = refs[6:11]
-        out_hbm, prof, obs, jac_ref, field, moved_a, moved_b, smooth, sems, out_sems = refs[11:]
+        obs_hbm, rates_hbm, rows_hbm, shift_hbm = refs[6:10]
+        out_hbm, *refs = refs[10:]
+    prof, obs, jac_ref, field, moved_a, moved_b, smooth, rates_ref, rows_ref, shift_ref, sems, out_sems = refs
     own, pixels = jac_hbm.shape[1], prof_hbm.shape[0]
+    odd = lax.rem(lax.axis_index("swath"), 2)
     rim = prof_near_hbm.shape[0]
     lines = pixels // XTRACK
     wide = 2 * XTRACK
@@ -157,7 +159,10 @@
         waits.append([])
         if n == 0:
             fetch(jac_hbm, jac_ref)
-            for src, number in ((prof_near_hbm, 1 - odd_ref[0]), (prof_next_hbm, odd_ref[0])):
+            fetch(rows_hbm, rows_ref)
+            fetch(rates_hbm, rates_ref)
+            fetch(shift_hbm, shift_ref)
+            for src, number in ((prof_near_hbm, 1 - odd), (prof_next_hbm, odd)):
                 fetch(src, prof.at[pl.ds(pl.multiple_of(number * (rim + pixels), XTRACK), rim), :])
             fetch(top_hbm.at[part, :], obs.at[:, pl.ds(0, rim)])
         low = max(cuts[n] * wide - rim, 0)
@@ -187,6 +192,8 @@
 
     for n in range(AHEAD):
         start(n)
+    for copy in waits[0]:
+        copy.wait()
     s1 = jnp.concatenate([rows_ref[0:1, :]] * 2, axis=1)
     s2 = jnp.concatenate([rows_ref[1:2, :]] * 2, axis=1)
     inside_top = rows_ref[2:3, :]
@@ -248,7 +255,7 @@
                     smooth[chan, line * XTRACK : (line + 1) * XTRACK] = (new * stay).astype(smooth.dtype)
 
     for n in range(SEGMENTS):
-        for copy in waits[n]:
+        for copy in waits[n] if n else []:
             copy.wait()
         start(n + AHEAD)
         pl.loop(cuts[n], cuts[n + 1], unroll=cuts[n + 1] - cuts[n])(departures)
@@ -297,7 +304,7 @@
     pl.loop(0, pixels // OUT_BLOCK)(lambda t: out_copy(t).wait())
 
 
-def half_call(last, anys, whole):
+def half_call(last, anys, small):
     own, pixels = anys[5].shape[1], anys[0].shape[0]
     rim = anys[1].shape[0]
     full = pixels + 2 * rim
@@ -310,6 +317,7 @@
         pltpu.VMEM((16 * (full // XTRACK - 2), HALO * XTRACK), jnp.float32),
         pltpu.VMEM((16 * (full // XTRACK - 2), HALO * XTRACK), jnp.float32),
         pltpu.VMEM((2 * own if last else own, pixels), jnp.bfloat16),
+        *[pltpu.VMEM(x.shape, x.dtype) for x in small],
         pltpu.SemaphoreType.DMA((32,)),
         pltpu.SemaphoreType.DMA((pixels // OUT_BLOCK,)),
     ]
@@ -318,14 +326,12 @@
     return pl.pallas_call(
         functools.partial(half_kernel, last),
         out_shape=jax.ShapeDtypeStruct((own, pixels), dtype),
-        in_specs=[pl.BlockSpec(memory_space=pl.ANY)] * len(anys)
-        + [pl.BlockSpec(memory_space=pltpu.SMEM)]
-        + [pl.BlockSpec(memory_space=pltpu.VMEM)] * (len(whole) - 1),
+        in_specs=[pl.BlockSpec(memory_space=pl.ANY)] * (len(anys) + len(small)),
         out_specs=pl.BlockSpec(memory_space=pl.ANY),
         scratch_shapes=scratch,
         compiler_params=pltpu.CompilerParams(vmem_limit_bytes=LAST_LIMIT if last else OWN_LIMIT),
         name="other_half_and_factor" if last else "own_half",
-    )(*anys, *whole)
+    )(*anys, *small)
 
 
 def on_device_two(grid_profiles, send_lists, counts, angle_index, jacobian, observed, kappa, factor):
@@ -384,17 +390,16 @@
     between = [(i, (i + 1 if i % 2 else i - 1)) for i in range(1, swath - 1)]
     prof_near = lax.ppermute(jnp.where(odd == 1, head, tail), "swath", pairs)
     prof_next = lax.ppermute(jnp.where(odd == 1, tail, head), "swath", between)
-    odd = jnp.full((1,), odd, jnp.int32)
 
     smooth_own = half_call(
         False,
         (profiles, prof_near, prof_next, obs_top, obs_bot, jac_own, observed),
-        (odd, rates_own, rows, shift),
+        (rates_own, rows, shift),
     )
     return half_call(
         True,
         (profiles, prof_near, prof_next, obs_top, obs_bot, jac_oth, mid_oth, bnd_oth, smooth_own, factor_two),
-        (odd, rates_oth, rows, shift),
+        (rates_oth, rows, shift),
     )
 
 

time: 92.7 us -> 90.8 us (0.980)
  Pallas kernels: 27.7 us -> 25.9 us
    pallas_call x2, Pallas kernels: 23.5 us -> 21.6 us  [half_call(): pl.pallas_call(functools.partial(half_kernel, last), out_shape=jax.ShapeD...]
where the time goes in v7:
time: 90.8 us; the launch traced here: 89.4 us
  waiting for transfers between devices  32.3 us (36%)
  Pallas kernels  25.9 us (29%)
  starting transfers between devices  19.5 us (21%)
  local copies, waits for them, and re-layouts  7.66 us (8%)
  other arithmetic  3.71 us (4%)
    pallas_call x2, Pallas kernels, half_call(): pl.pallas_call(functools.partial(half_kernel, last), out_shape=jax.ShapeD...  21.6 us
    all_to_all x1, waiting for transfers between devices, on_device_two(): lax.all_to_all(outgoing, 'swath', split_axis=0, concat_axis=0, tiled=True)  15.3 us
    all_to_all x1, starting transfers between devices, on_device_two(): lax.all_to_all(outgoing, 'swath', split_axis=0, concat_axis=0, tiled=True)  6.3 us
    ppermute x1, waiting for transfers between devices, on_device_two(): jac_near = lax.ppermute(jac_half, 'chan', swap)  5.83 us
    ppermute x1, waiting for transfers between devices, on_device_two(): bnd_oth = lax.ppermute(bnd_own, 'chan', swap)  5.4 us
    pallas_call x1, Pallas kernels, gather_rows(): pl.pallas_call(gather_kernel, out_shape=jax.ShapeDtypeStruct(shape, grid_...  4.26 us
    ppermute x1, waiting for transfers between devices, on_device_two(): prof_next = lax.ppermute(jnp.where(odd == 1, tail, head), 'swath', between)  3.47 us
    ppermute x1, starting transfers between devices, on_device_two(): obs_bot = lax.ppermute(bnd_both[:, :rim], 'swath', backward)  3.1 us
  transfers between devices with their start and end apart: 10, of which 6 were waited for; matrix products, arithmetic and copies ran while one was open for 12% of the time, Pallas kernels for 11%

profile of v7, /device:TPU:16, one launch (start us, length us, event | category | flops | bytes accessed | tf_op | source)
XLA Modules:
  0.0 89.4 jit_solution(5622147728141410151)
XLA Ops:
  0.0 4.3 %pick_rows.1 = bf16[16,256,256]{2,1,0:T(8,128)(2,1)} custom-call(s32[16,256]{1,0:T(8,128)} %bitcast.17, s32[1,16]{1,0:T(1,128)} %counts_hbm.1, bf16[1024,256]{1,0:T(8,128)(2,1)} %grid_hbm.1), custom_call_target="tpu_custom_call" | custom-call | tf_op jit(solution)/shard_map/pick_rows/pallas_call | solution.py:110
  4.3 0.0 copy-start.8
  4.3 0.0 copy-start.5
  4.3 6.3 %all-to-all-start = ((bf16[16,256,256]{2,1,0:T(8,128)(2,1)}), bf16[16,256,256]{2,1,0:T(8,128)(2,1)S(1)}, u32[]{:S(2)}, u32[]{:S(2)}) async-start(bf16[16,256,256]{2,1,0:T(8,128)(2,1)} %pick_rows.1), calls=%async_computation | async-start | bytes 4194304 | tf_op jit(solution)/shard_map/all_to_all | solution.py:356
  10.6 1.1 %fusion = (bf16[304,384]{1,0:T(8,128)(2,1)S(1)}, bf16[304,384]{1,0:T(8,128)(2,1)S(1)}) fusion(bf16[304,4096]{1,0:T(8,128)(2,1)} %refs_6_.1), kind=kLoop, calls=%fused_computation.11 | loop fusion | bytes 933888 | tf_op jit(solution)/shard_map/slice | solution.py:354
  11.8 1.6 %collective-permute-start.2 = (bf16[304,768]{1,0:T(8,128)(2,1)S(1)}, bf16[304,768]{1,0:T(8,128)(2,1)S(1)}, u32[]{:S(2)}, u32[]{:S(2)}) collective-permute-start(bf16[304,768]{1,0:T(8,128)(2,1)S(1)} %pad_maximum_fusion), channel_id=1, source_target_pairs={{0,1},{1,0},{2,3},{3,2},{4,5},{5,4},{6,7},{7,6},{8,9},{9,8},{10,11... | collective-permute-start | bytes 1400840 | tf_op jit(solution)/shard_map/ppermute | solution.py:355
  13.3 0.0 copy-done.8
  13.3 0.8 copy.10
  14.1 0.5 collective-permute-start.5
  14.7 0.0 copy-done.5
  14.7 0.7 dynamic-slice_bitcast_fusion
  15.4 0.0 copy-start.1
  15.4 1.5 %collective-permute-start.3 = (bf16[3,152,256]{2,1,0:T(8,128)(2,1)}, bf16[3,152,256]{2,1,0:T(8,128)(2,1)}, u32[]{:S(2)}, u32[]{:S(2)}) collective-permute-start(bf16[3,152,256]{2,1,0:T(8,128)(2,1)} %dynamic-slice_bitcast_fusion), channel_id=1, source_target_pairs={{0,1},{1,0},{2,3},{3,2},{4,5},{5,4},{6,7},{7,6},{8,9},{9,8},{10,11... | collective-permute-start | bytes 700424 | tf_op jit(solution)/shard_map/ppermute | solution.py:349
  16.9 3.1 %slice.33 = bf16[304,3328]{1,0:T(8,128)(2,1)} slice(bf16[304,4096]{1,0:T(8,128)(2,1)} %refs_6_.1), slice={[0:304], [384:3712]} | slice | bytes 4046848 | tf_op jit(solution)/shard_map/slice | solution.py:357
  20.0 0.0 copy-start.9
  20.0 5.4 %collective-permute-done.2.refs_7_ = bf16[304,768]{1,0:T(8,128)(2,1)S(1)} collective-permute-done((bf16[304,768]{1,0:T(8,128)(2,1)S(1)}, bf16[304,768]{1,0:T(8,128)(2,1)S(1)}, u32[]{:S(2)}, u32[]{:S(2)}) %collective-permute-start.2) | collective-permute-done | bytes 466976 | tf_op jit(solution)/shard_map/ppermute | solution.py:355
  25.4 0.0 copy-start.4
  25.4 1.5 %collective-permute-start.8 = (bf16[304,3328]{1,0:T(8,128)(2,1)}, bf16[304,3328]{1,0:T(8,128)(2,1)}, u32[]{:S(2)}, u32[]{:S(2)}) collective-permute-start(bf16[304,3328]{1,0:T(8,128)(2,1)} %slice.33), channel_id=1, source_target_pairs={{0,1},{1,0},{2,3},{3,2},{4,5},{5,4},{6,7},{7,6},{8,9},{9,8},{10,11... | collective-permute-start | bytes 6070280 | tf_op jit(solution)/shard_map/ppermute | solution.py:359
  26.9 0.0 copy-done.1
  26.9 0.1 fusion.2
  27.0 1.0 %maximum_select_fusion.1.refs_9_ = bf16[304,608]{1,0:T(8,128)(2,1)} fusion(bf16[304,608]{1,0:T(8,128)(2,1)S(1)} %copy-done.1, bf16[304,304]{1,0:T(8,128)(2,1)S(1)} %get-tuple-element.34, bf16[304,304]{1,0:T(8,128)(2,1)S(1)} %get-tuple-element.33, pred[]{:T(512)S(6)} %eq.16), kind=kLoop, calls=%fused_computation.2 | loop fusion | flops 924160 | bytes 1108993 | tf_op jit(solution)/shard_map/jit(_where)/select_n | solution.py:377
  28.0 5.8 %collective-permute-done.3 = bf16[3,152,256]{2,1,0:T(8,128)(2,1)} collective-permute-done((bf16[3,152,256]{2,1,0:T(8,128)(2,1)}, bf16[3,152,256]{2,1,0:T(8,128)(2,1)}, u32[]{:S(2)}, u32[]{:S(2)}) %collective-permute-start.3) | collective-permute-done | bytes 233504 | tf_op jit(solution)/shard_map/ppermute | solution.py:349
  33.8 0.0 collective-permute-start.4
  33.8 0.0 copy-done.9
  33.9 0.1 pad.4.clone
  33.9 0.1 pad.5.clone
  34.0 0.7 maximum_maximum_fusion.refs_8_.refs_11_
  34.7 0.8 collective-permute-done.4
  35.5 2.0 %maximum_select_fusion.refs_5_ = bf16[3,304,256]{2,1,0:T(8,128)(2,1)} fusion(bf16[3,152,256]{2,1,0:T(8,128)(2,1)S(1)} %collective-permute-done.4, bf16[3,152,256]{2,1,0:T(8,128)(2,1)} %collective-permute-done.3, pred[]{:T(512)S(6)} %eq.15), kind=kLoop, calls=%fused_computation.1 | loop fusion | flops 2101248 | bytes 933889 | tf_op jit(solution)/shard_map/jit(_where)/select_n | solution.py:361
  37.5 0.0 collective-permute-done.5.refs_10_
  37.6 0.0 copy-done.4
  37.6 0.9 fusion.1
  38.5 3.1 %collective-permute-start.7 = (bf16[608,384]{1,0:T(8,128)(2,1)}, bf16[608,384]{1,0:T(8,128)(2,1)S(1)}, u32[]{:S(2)}, u32[]{:S(2)}) collective-permute-start(bf16[608,384]{1,0:T(8,128)(2,1)} %get-tuple-element.31), channel_id=1, source_target_pairs={{2,0},{4,2},{6,4},{8,6},{10,8},{12,10},{14,12},{16,14},{18,16},{20... | collective-permute-start | bytes 1400840 | tf_op jit(solution)/shard_map/ppermute | solution.py:384
  41.6 1.9 %collective-permute-start.6 = (bf16[608,384]{1,0:T(8,128)(2,1)S(1)}, bf16[608,384]{1,0:T(8,128)(2,1)S(1)}, u32[]{:S(2)}, u32[]{:S(2)}) collective-permute-start(bf16[608,384]{1,0:T(8,128)(2,1)S(1)} %get-tuple-element.32), channel_id=1, source_target_pairs={{0,2},{2,4},{4,6},{6,8},{8,10},{10,12},{12,14},{14,16},{16,18},{18... | collective-permute-start | bytes 1400840 | tf_op jit(solution)/shard_map/ppermute | solution.py:383
  43.5 15.3 %all-to-all-done = bf16[16,256,256]{2,1,0:T(8,128)(2,1)S(1)} async-done(((bf16[16,256,256]{2,1,0:T(8,128)(2,1)}), bf16[16,256,256]{2,1,0:T(8,128)(2,1)S(1)}, u32[]{:S(2)}, u32[]{:S(2)}) %all-to-all-start) | async-done | bytes 2097184 | tf_op jit(solution)/shard_map/all_to_all | solution.py:356
  58.8 0.0 copy-start
  58.8 3.0 %collective-permute-start.1 = (bf16[384,256]{1,0:T(8,128)(2,1)S(1)}, bf16[384,256]{1,0:T(8,128)(2,1)S(1)}, u32[]{:S(2)}, u32[]{:S(2)}) collective-permute-start(bf16[384,256]{1,0:T(8,128)(2,1)S(1)} %get-tuple-element.29), channel_id=1, source_target_pairs={{2,4},{4,2},{6,8},{8,6},{10,12},{12,10},{14,16},{16,14},{18,20},{2... | collective-permute-start | bytes 589832 | tf_op jit(solution)/shard_map/ppermute | solution.py:392
  61.8 0.1 collective-permute-start
  61.9 0.0 collective-permute-done.7.refs_4_
  61.9 0.0 copy-start.2
  61.9 1.5 %collective-permute-done.6.refs_3_ = bf16[608,384]{1,0:T(8,128)(2,1)S(1)} collective-permute-done((bf16[608,384]{1,0:T(8,128)(2,1)S(1)}, bf16[608,384]{1,0:T(8,128)(2,1)S(1)}, u32[]{:S(2)}, u32[]{:S(2)}) %collective-permute-start.6) | collective-permute-done | bytes 466976 | tf_op jit(solution)/shard_map/ppermute | solution.py:383
  63.4 0.0 copy-start.3
  63.4 3.5 %collective-permute-done.1.refs_2_ = bf16[384,256]{1,0:T(8,128)(2,1)S(1)} collective-permute-done((bf16[384,256]{1,0:T(8,128)(2,1)S(1)}, bf16[384,256]{1,0:T(8,128)(2,1)S(1)}, u32[]{:S(2)}, u32[]{:S(2)}) %collective-permute-start.1) | collective-permute-done | bytes 196640 | tf_op jit(solution)/shard_map/ppermute | solution.py:392
  66.8 0.0 copy-start.6
  66.8 0.0 collective-permute-done.refs_1_
  66.8 0.0 copy-start.7
  66.8 0.0 copy-done
  66.9 0.0 copy-done.2
  66.9 0.0 copy-done.3
  66.9 0.6 copy-done.6
  67.5 0.1 copy-done.7
  67.6 9.6 %own_half.1.refs_8_ = bf16[304,4096]{1,0:T(8,128)(2,1)} custom-call(bf16[4096,256]{1,0:T(8,128)(2,1)} %bitcast.12, bf16[384,256]{1,0:T(8,128)(2,1)} %copy-done.7, bf16[384,256]{1,0:T(8,128)(2,1)} %copy-done.6, bf16[608,384]{1,0:T(8,128)(2,1)} %copy-done.3, bf16[608,384]{1,0:T(8,128)(2,1)} %copy-done.2, bf16[3,304,256]{2,1,0:T(8,128)(2,1)} %bitcast.14, ...), custom_call_target="tpu_custom_call" | custom-call | tf_op jit(solution)/shard_map/own_half/pallas_call | solution.py:326
  77.2 0.0 collective-permute-done.8.refs_6_
  77.2 12.1 %other_half_and_factor.1 = f32[304,4096]{1,0:T(8,128)} custom-call(bf16[4096,256]{1,0:T(8,128)(2,1)} %bitcast.13, bf16[384,256]{1,0:T(8,128)(2,1)} %copy-done.7, bf16[384,256]{1,0:T(8,128)(2,1)} %copy-done.6, bf16[608,384]{1,0:T(8,128)(2,1)} %copy-done.3, bf16[608,384]{1,0:T(8,128)(2,1)} %copy-done.2, bf16[3,304,256]{2,1,0:T(8,128)(2,1)} %maximum_select_fusion.refs_5_, ...), custom_call_target="tpu_custom_call" | custom-call | tf_op jit(solution)/shard_map/other_half_and_factor/pallas_call | solution.py:326
  (5 shorter events, 0.2 us)
Async XLA Ops:
  4.3 9.1 %copy-start.8 = (f32[2,304]{1,0:T(2,128)S(1)}, f32[2,304]{1,0:T(2,128)}, u32[]{:S(2)}) copy-start(f32[2,304]{1,0:T(2,128)} %param.15) | copy-start | bytes 7300
  4.3 10.4 %copy-start.5 = (bf16[3,256,304]{1,2,0:T(8,128)(2,1)S(1)}, bf16[3,256,304]{1,2,0:T(8,128)(2,1)}, u32[]{:S(2)}) copy-start(bf16[3,256,304]{1,2,0:T(8,128)(2,1)} %param.13) | copy-start | bytes 1400836
  4.3 54.5 %all-to-all-start = ((bf16[16,256,256]{2,1,0:T(8,128)(2,1)}), bf16[16,256,256]{2,1,0:T(8,128)(2,1)S(1)}, u32[]{:S(2)}, u32[]{:S(2)}) async-start(bf16[16,256,256]{2,1,0:T(8,128)(2,1)} %pick_rows.1), calls=%async_computation | async-start | bytes 4194304 | tf_op jit(solution)/shard_map/all_to_all | solution.py:356
  11.8 13.6 %collective-permute-start.2 = (bf16[304,768]{1,0:T(8,128)(2,1)S(1)}, bf16[304,768]{1,0:T(8,128)(2,1)S(1)}, u32[]{:S(2)}, u32[]{:S(2)}) collective-permute-start(bf16[304,768]{1,0:T(8,128)(2,1)S(1)} %pad_maximum_fusion), channel_id=1, source_target_pairs={{0,1},{1,0},{2,3},{3,2},{4,5},{5,4},{6,7},{7,6},{8,9},{9,8},{10,11... | collective-permute-start | bytes 1400840 | tf_op jit(solution)/shard_map/ppermute | solution.py:355
  14.1 23.3 %collective-permute-start.5 = (f32[304,2]{1,0:T(8,128)}, f32[304,2]{1,0:T(8,128)}, u32[]{:S(2)}, u32[]{:S(2)}) collective-permute-start(f32[304,2]{1,0:T(8,128)} %bitcast.15), channel_id=1, source_target_pairs={{0,1},{1,0},{2,3},{3,2},{4,5},{5,4},{6,7},{7,6},{8,9},{9,8},{10,11... | collective-permute-start | bytes 7304 | tf_op jit(solution)/shard_map/ppermute | solution.py:351
  15.4 11.5 %copy-start.1 = (bf16[304,608]{1,0:T(8,128)(2,1)S(1)}, bf16[304,608]{1,0:T(8,128)(2,1)}, u32[]{:S(2)}) copy-start(bf16[304,608]{1,0:T(8,128)(2,1)} %param.16) | copy-start | bytes 1108996
  15.4 18.4 %collective-permute-start.3 = (bf16[3,152,256]{2,1,0:T(8,128)(2,1)}, bf16[3,152,256]{2,1,0:T(8,128)(2,1)}, u32[]{:S(2)}, u32[]{:S(2)}) collective-permute-start(bf16[3,152,256]{2,1,0:T(8,128)(2,1)} %dynamic-slice_bitcast_fusion), channel_id=1, source_target_pairs={{0,1},{1,0},{2,3},{3,2},{4,5},{5,4},{6,7},{7,6},{8,9},{9,8},{10,11... | collective-permute-start | bytes 700424 | tf_op jit(solution)/shard_map/ppermute | solution.py:349
  20.0 13.9 %copy-start.9 = (s32[128]{0:T(128)S(1)}, s32[128]{0:T(128)}, u32[]{:S(2)}) copy-start(s32[128]{0:T(128)} %param.12) | copy-start | bytes 1540
  25.4 12.2 %copy-start.4 = (bf16[304,768]{1,0:T(8,128)(2,1)}, bf16[304,768]{1,0:T(8,128)(2,1)S(1)}, u32[]{:S(2)}) copy-start(bf16[304,768]{1,0:T(8,128)(2,1)S(1)} %collective-permute-done.2.refs_7_) | copy-start | bytes 1400836
  25.4 51.8 %collective-permute-start.8 = (bf16[304,3328]{1,0:T(8,128)(2,1)}, bf16[304,3328]{1,0:T(8,128)(2,1)}, u32[]{:S(2)}, u32[]{:S(2)}) collective-permute-start(bf16[304,3328]{1,0:T(8,128)(2,1)} %slice.33), channel_id=1, source_target_pairs={{0,1},{1,0},{2,3},{3,2},{4,5},{5,4},{6,7},{7,6},{8,9},{9,8},{10,11... | collective-permute-start | bytes 6070280 | tf_op jit(solution)/shard_map/ppermute | solution.py:359
  33.8 1.7 %collective-permute-start.4 = (bf16[3,152,256]{2,1,0:T(8,128)(2,1)}, bf16[3,152,256]{2,1,0:T(8,128)(2,1)S(1)}, u32[]{:S(2)}, u32[]{:S(2)}) collective-permute-start(bf16[3,152,256]{2,1,0:T(8,128)(2,1)} %collective-permute-done.3), channel_id=1, source_target_pairs={{0,2},{2,0},{4,6},{6,4},{8,10},{10,8},{12,14},{14,12},{16,18},{18,... | collective-permute-start | bytes 700424 | tf_op jit(solution)/shard_map/ppermute | solution.py:360
  38.5 23.4 %collective-permute-start.7 = (bf16[608,384]{1,0:T(8,128)(2,1)}, bf16[608,384]{1,0:T(8,128)(2,1)S(1)}, u32[]{:S(2)}, u32[]{:S(2)}) collective-permute-start(bf16[608,384]{1,0:T(8,128)(2,1)} %get-tuple-element.31), channel_id=1, source_target_pairs={{2,0},{4,2},{6,4},{8,6},{10,8},{12,10},{14,12},{16,14},{18,16},{20... | collective-permute-start | bytes 1400840 | tf_op jit(solution)/shard_map/ppermute | solution.py:384
  41.6 21.8 %collective-permute-start.6 = (bf16[608,384]{1,0:T(8,128)(2,1)S(1)}, bf16[608,384]{1,0:T(8,128)(2,1)S(1)}, u32[]{:S(2)}, u32[]{:S(2)}) collective-permute-start(bf16[608,384]{1,0:T(8,128)(2,1)S(1)} %get-tuple-element.32), channel_id=1, source_target_pairs={{0,2},{2,4},{4,6},{6,8},{8,10},{10,12},{12,14},{14,16},{16,18},{18... | collective-permute-start | bytes 1400840 | tf_op jit(solution)/shard_map/ppermute | solution.py:383
  58.8 8.0 %copy-start = (bf16[16,256,256]{2,1,0:T(8,128)(2,1)}, bf16[16,256,256]{2,1,0:T(8,128)(2,1)S(1)}, u32[]{:S(2)}) copy-start(bf16[16,256,256]{2,1,0:T(8,128)(2,1)S(1)} %all-to-all-done) | copy-start | bytes 6291460
  58.8 8.0 %collective-permute-start.1 = (bf16[384,256]{1,0:T(8,128)(2,1)S(1)}, bf16[384,256]{1,0:T(8,128)(2,1)S(1)}, u32[]{:S(2)}, u32[]{:S(2)}) collective-permute-start(bf16[384,256]{1,0:T(8,128)(2,1)S(1)} %get-tuple-element.29), channel_id=1, source_target_pairs={{2,4},{4,2},{6,8},{8,6},{10,12},{12,10},{14,16},{16,14},{18,20},{2... | collective-permute-start | bytes 589832 | tf_op jit(solution)/shard_map/ppermute | solution.py:392
  61.8 5.0 %collective-permute-start = (bf16[384,256]{1,0:T(8,128)(2,1)S(1)}, bf16[384,256]{1,0:T(8,128)(2,1)S(1)}, u32[]{:S(2)}, u32[]{:S(2)}) collective-permute-start(bf16[384,256]{1,0:T(8,128)(2,1)S(1)} %get-tuple-element.30), channel_id=1, source_target_pairs={{0,2},{2,0},{4,6},{6,4},{8,10},{10,8},{12,14},{14,12},{16,18},{18,... | collective-permute-start | bytes 589832 | tf_op jit(solution)/shard_map/ppermute | solution.py:391
  61.9 5.0 %copy-start.2 = (bf16[608,384]{1,0:T(8,128)(2,1)}, bf16[608,384]{1,0:T(8,128)(2,1)S(1)}, u32[]{:S(2)}) copy-start(bf16[608,384]{1,0:T(8,128)(2,1)S(1)} %collective-permute-done.7.refs_4_) | copy-start | bytes 1400836
  63.4 3.5 %copy-start.3 = (bf16[608,384]{1,0:T(8,128)(2,1)}, bf16[608,384]{1,0:T(8,128)(2,1)S(1)}, u32[]{:S(2)}) copy-start(bf16[608,384]{1,0:T(8,128)(2,1)S(1)} %collective-permute-done.6.refs_3_) | copy-start | bytes 1400836
  66.8 0.7 copy-start.6
  66.8 0.7 copy-start.7

commit v8 on v7

--- a/solution.py
+++ b/solution.py
@@ -345,8 +345,9 @@
     backward = [(i + 1, i) for i in range(swath - 1)]
 
     jac_own = jnp.swapaxes(jacobian, 1, 2)
-    jac_half = lax.dynamic_slice_in_dim(jac_own, (place % 2) * (own // 2), own // 2, axis=1)
-    jac_near = lax.ppermute(jac_half, "chan", swap)
+    quarter = own // 4
+    jac_part = lax.dynamic_slice_in_dim(jac_own, (place % 4) * quarter, quarter, axis=1)
+    jac_near = lax.ppermute(jac_part, "chan", swap)
     rates_own = kappa.T
     rates_oth = lax.ppermute(rates_own, "chan", swap)
     outgoing = gather_rows(grid_profiles, send_lists[0], counts)
@@ -357,12 +358,14 @@
     middle = obs_late[:, rim : pixels - rim]
     middle, bnd_oth = lax.optimization_barrier((middle, bnd_oth))
     mid_oth = lax.ppermute(middle, "chan", swap)
-    jac_far = lax.ppermute(jac_near, "swath", [(i, i ^ 1) for i in range(swath)])
-    jac_oth = jnp.where(
-        place % 2 == 0,
-        jnp.concatenate([jac_near, jac_far], axis=1),
-        jnp.concatenate([jac_far, jac_near], axis=1),
-    )
+    jac_oth = jac_near
+    for step in (1, 2):
+        jac_far = lax.ppermute(jac_oth, "swath", [(i, i ^ step) for i in range(swath)])
+        jac_oth = jnp.where(
+            place // step % 2 == 0,
+            jnp.concatenate([jac_oth, jac_far], axis=1),
+            jnp.concatenate([jac_far, jac_oth], axis=1),
+        )
     near = np.eye(XTRACK, k=1) + np.eye(XTRACK, k=-1)
     moves = np.concatenate([near, near @ near, near @ near @ near], axis=1)
     shift = jnp.asarray(np.concatenate([moves, moves], axis=0), jnp.bfloat16)
@@ -376,14 +379,15 @@
     ])
     factor_two = jnp.where(half == 0, factor, jnp.roll(factor, own, axis=1))
 
-    bnd_own, bnd_oth, jac_oth, rates_oth, rows, factor_two = lax.optimization_barrier(
-        (bnd_own, bnd_oth, jac_oth, rates_oth, rows, factor_two)
+    bnd_own, bnd_oth, rates_oth, rows, factor_two = lax.optimization_barrier(
+        (bnd_own, bnd_oth, rates_oth, rows, factor_two)
     )
     bnd_both = jnp.concatenate([bnd_own, bnd_oth], axis=0)
     obs_top = lax.ppermute(bnd_both[:, rim:], "swath", forward)
     obs_bot = lax.ppermute(bnd_both[:, :rim], "swath", backward)
 
     profiles = incoming.reshape(pixels, grid_profiles.shape[1])
+    profiles, jac_oth = lax.optimization_barrier((profiles, jac_oth))
     odd = place % 2
     head, tail = profiles[:rim], profiles[pixels - rim :]
     pairs = [(i, i ^ 1) for i in range(swath)]
@@ -415,7 +419,8 @@
         P("chan", None),
     )
     out_specs = P("chan", "swath")
-    on_device = on_device_two if mesh.shape["chan"] == 2 else on_device_plain
+    two = mesh.shape["chan"] == 2 and mesh.shape["swath"] % 4 == 0
+    on_device = on_device_two if two else on_device_plain
     return jax.shard_map(
         on_device, mesh=mesh, in_specs=in_specs, out_specs=out_specs, check_vma=False
     )

time: 90.8 us -> 90.6 us (level)
  waiting for transfers between devices: 32.3 us -> 31.3 us
  other arithmetic: 3.71 us -> 2.79 us
    ppermute x1, starting transfers between devices: 3.1 us -> 1.91 us  [on_device_two(): obs_bot = lax.ppermute(bnd_both[:, :rim], 'swath', backward)]
    all_to_all x1, waiting for transfers between devices: 15.3 us -> 14.2 us  [on_device_two(): lax.all_to_all(outgoing, 'swath', split_axis=0, concat_axis=0, tiled=True)]
    ppermute x1, waiting for transfers between devices: 5.4 us -> 4.39 us  [on_device_two(): bnd_oth = lax.ppermute(bnd_own, 'chan', swap)]
    ppermute x1, starting transfers between devices: 0.51 us -> 1.52 us  [on_device_two(): rates_oth = lax.ppermute(rates_own, 'chan', swap)]
    select_n x1 -> x2, other arithmetic: 1.97 us -> 1.05 us  [on_device_two(): jnp.where(place // step % 2 == 0, jnp.concatenate([jac_oth, jac_far], axi...]
    ppermute x2 -> x3, waiting for transfers between devices: 6.65 us -> 7.51 us  [the longest x2 7.51 us: on_device_two(): lax.ppermute(jac_oth, 'swath', [(i, i ^ step) for i in range(swath)])]
    ppermute x2 -> x3, starting transfers between devices: 1.52 us -> 2.11 us  [the longest x2 1.6 us: on_device_two(): lax.ppermute(jac_oth, 'swath', [(i, i ^ step) for i in range(swath)])]
  transfers between devices with their start and end apart: 10 -> 11, of which waited for: 6 -> 7; matrix products, arithmetic and copies ran while one was open for 12% -> 12% of each run, Pallas kernels for 11% -> 11%
where the time goes in v8:
time: 90.6 us; the launch traced here: 89.2 us
  waiting for transfers between devices  31.3 us (35%)
  Pallas kernels  25.9 us (29%)
  starting transfers between devices  20.3 us (22%)
  local copies, waits for them, and re-layouts  8.52 us (9%)
  other arithmetic  2.79 us (3%)
    pallas_call x2, Pallas kernels, half_call(): pl.pallas_call(functools.partial(half_kernel, last), out_shape=jax.ShapeD...  21.6 us
    all_to_all x1, waiting for transfers between devices, on_device_two(): lax.all_to_all(outgoing, 'swath', split_axis=0, concat_axis=0, tiled=True)  14.2 us
    ppermute x2, waiting for transfers between devices, on_device_two(): lax.ppermute(jac_oth, 'swath', [(i, i ^ step) for i in range(swath)])  7.51 us
    all_to_all x1, starting transfers between devices, on_device_two(): lax.all_to_all(outgoing, 'swath', split_axis=0, concat_axis=0, tiled=True)  6.17 us
    ppermute x1, waiting for transfers between devices, on_device_two(): bnd_oth = lax.ppermute(bnd_own, 'chan', swap)  4.39 us
    pallas_call x1, Pallas kernels, gather_rows(): pl.pallas_call(gather_kernel, out_shape=jax.ShapeDtypeStruct(shape, grid_...  4.26 us
    ppermute x1, waiting for transfers between devices, on_device_two(): prof_next = lax.ppermute(jnp.where(odd == 1, tail, head), 'swath', between)  3.47 us
    slice x1, local copies, waits for them, and re-layouts, on_device_two(): middle = obs_late[:, rim:pixels - rim]  3.05 us
  transfers between devices with their start and end apart: 11, of which 7 were waited for; matrix products, arithmetic and copies ran while one was open for 12% of the time, Pallas kernels for 11%

profile of v8, /device:TPU:16, one launch (start us, length us, event | category | flops | bytes accessed | tf_op | source)
XLA Modules:
  0.0 89.2 jit_solution(774984050626395319)
XLA Ops:
  0.0 4.3 %pick_rows.1 = bf16[16,256,256]{2,1,0:T(8,128)(2,1)} custom-call(s32[16,256]{1,0:T(8,128)} %bitcast.17, s32[1,16]{1,0:T(1,128)} %counts_hbm.1, bf16[1024,256]{1,0:T(8,128)(2,1)} %grid_hbm.1), custom_call_target="tpu_custom_call" | custom-call | tf_op jit(solution)/shard_map/pick_rows/pallas_call | solution.py:110
  4.3 6.2 %all-to-all-start = ((bf16[16,256,256]{2,1,0:T(8,128)(2,1)}), bf16[16,256,256]{2,1,0:T(8,128)(2,1)S(1)}, u32[]{:S(2)}, u32[]{:S(2)}) async-start(bf16[16,256,256]{2,1,0:T(8,128)(2,1)} %pick_rows.1), calls=%async_computation | async-start | bytes 4194304 | tf_op jit(solution)/shard_map/all_to_all | solution.py:357
  10.4 0.0 copy-start.7
  10.4 1.1 %fusion = (bf16[304,384]{1,0:T(8,128)(2,1)S(1)}, bf16[304,384]{1,0:T(8,128)(2,1)S(1)}) fusion(bf16[304,4096]{1,0:T(8,128)(2,1)} %refs_6_.1), kind=kLoop, calls=%fused_computation.12 | loop fusion | bytes 933888 | tf_op jit(solution)/shard_map/slice | solution.py:355
  11.6 1.6 %collective-permute-start.5 = (bf16[304,768]{1,0:T(8,128)(2,1)S(1)}, bf16[304,768]{1,0:T(8,128)(2,1)S(1)}, u32[]{:S(2)}, u32[]{:S(2)}) collective-permute-start(bf16[304,768]{1,0:T(8,128)(2,1)S(1)} %pad_maximum_fusion), channel_id=1, source_target_pairs={{0,1},{1,0},{2,3},{3,2},{4,5},{5,4},{6,7},{7,6},{8,9},{9,8},{10,11... | collective-permute-start | bytes 1400840 | tf_op jit(solution)/shard_map/ppermute | solution.py:356
  13.2 1.6 %dynamic-slice_bitcast_fusion = bf16[3,76,256]{2,1,0:T(8,128)(2,1)} fusion(bf16[3,256,304]{1,2,0:T(8,128)(2,1)} %param.13, s32[]{:T(128)S(6)} %select_n.79), kind=kLoop, calls=%fused_computation.6 | loop fusion | bytes 233476 | tf_op jit(solution)/shard_map/dynamic_slice | solution.py:349
  14.8 0.5 collective-permute-start
  15.3 0.0 copy-done.7
  15.3 0.8 copy.10
  16.1 0.0 copy-start.1
  16.1 1.5 %collective-permute-start.6 = (f32[304,2]{1,0:T(8,128)}, f32[304,2]{1,0:T(8,128)}, u32[]{:S(2)}, u32[]{:S(2)}) collective-permute-start(f32[304,2]{1,0:T(8,128)} %bitcast.15), channel_id=1, source_target_pairs={{0,1},{1,0},{2,3},{3,2},{4,5},{5,4},{6,7},{7,6},{8,9},{9,8},{10,11... | collective-permute-start | bytes 7304 | tf_op jit(solution)/shard_map/ppermute | solution.py:352
  17.6 3.1 %slice.33 = bf16[304,3328]{1,0:T(8,128)(2,1)} slice(bf16[304,4096]{1,0:T(8,128)(2,1)} %refs_6_.1), slice={[0:304], [384:3712]} | slice | bytes 4046848 | tf_op jit(solution)/shard_map/slice | solution.py:358
  20.7 0.0 copy-start.8
  20.7 0.1 pad.4.clone
  20.8 0.1 pad.5.clone
  20.8 4.4 %collective-permute-done.5.refs_7_ = bf16[304,768]{1,0:T(8,128)(2,1)S(1)} collective-permute-done((bf16[304,768]{1,0:T(8,128)(2,1)S(1)}, bf16[304,768]{1,0:T(8,128)(2,1)S(1)}, u32[]{:S(2)}, u32[]{:S(2)}) %collective-permute-start.5) | collective-permute-done | bytes 466976 | tf_op jit(solution)/shard_map/ppermute | solution.py:356
  25.2 0.0 copy-start.4
  25.2 1.5 %collective-permute-start.9 = (bf16[304,3328]{1,0:T(8,128)(2,1)}, bf16[304,3328]{1,0:T(8,128)(2,1)}, u32[]{:S(2)}, u32[]{:S(2)}) collective-permute-start(bf16[304,3328]{1,0:T(8,128)(2,1)} %slice.33), channel_id=1, source_target_pairs={{0,1},{1,0},{2,3},{3,2},{4,5},{5,4},{6,7},{7,6},{8,9},{9,8},{10,11... | collective-permute-start | bytes 6070280 | tf_op jit(solution)/shard_map/ppermute | solution.py:360
  26.7 0.0 copy-done.1
  26.7 0.1 fusion.2
  26.9 1.0 %maximum_select_fusion.1.refs_9_ = bf16[304,608]{1,0:T(8,128)(2,1)} fusion(bf16[304,608]{1,0:T(8,128)(2,1)S(1)} %copy-done.1, bf16[304,304]{1,0:T(8,128)(2,1)S(1)} %get-tuple-element.36, bf16[304,304]{1,0:T(8,128)(2,1)S(1)} %get-tuple-element.35, pred[]{:T(512)S(6)} %eq.21), kind=kLoop, calls=%fused_computation.2 | loop fusion | flops 924160 | bytes 1108993 | tf_op jit(solution)/shard_map/jit(_where)/select_n | solution.py:380
  27.8 0.0 copy-done.8
  27.9 0.0 collective-permute-done
  27.9 0.1 collective-permute-start.1
  28.0 0.7 maximum_maximum_fusion.refs_8_.refs_11_
  28.6 0.7 collective-permute-done.1
  29.3 0.1 maximum_select_fusion.2
  29.4 1.5 %collective-permute-start.2 = (bf16[3,152,256]{2,1,0:T(8,128)(2,1)S(1)}, bf16[3,152,256]{2,1,0:T(8,128)(2,1)S(1)}, u32[]{:S(2)}, u32[]{:S(2)}) collective-permute-start(bf16[3,152,256]{2,1,0:T(8,128)(2,1)S(1)} %maximum_select_fusion.2), channel_id=1, source_target_pairs={{0,4},{2,6},{4,0},{6,2},{8,12},{10,14},{12,8},{14,10},{16,20},{18,... | collective-permute-start | bytes 700424 | tf_op jit(solution)/shard_map/ppermute | solution.py:363
  30.9 0.4 collective-permute-done.6.refs_10_
  31.4 0.0 copy-done.4
  31.4 0.9 fusion.1
  32.3 1.9 %collective-permute-start.8 = (bf16[608,384]{1,0:T(8,128)(2,1)}, bf16[608,384]{1,0:T(8,128)(2,1)S(1)}, u32[]{:S(2)}, u32[]{:S(2)}) collective-permute-start(bf16[608,384]{1,0:T(8,128)(2,1)} %get-tuple-element.33), channel_id=1, source_target_pairs={{2,0},{4,2},{6,4},{8,6},{10,8},{12,10},{14,12},{16,14},{18,16},{20... | collective-permute-start | bytes 1400840 | tf_op jit(solution)/shard_map/ppermute | solution.py:387
  34.2 2.4 %collective-permute-start.7 = (bf16[608,384]{1,0:T(8,128)(2,1)S(1)}, bf16[608,384]{1,0:T(8,128)(2,1)S(1)}, u32[]{:S(2)}, u32[]{:S(2)}) collective-permute-start(bf16[608,384]{1,0:T(8,128)(2,1)S(1)} %get-tuple-element.34), channel_id=1, source_target_pairs={{0,2},{2,4},{4,6},{6,8},{8,10},{10,12},{12,14},{14,16},{16,18},{18... | collective-permute-start | bytes 1400840 | tf_op jit(solution)/shard_map/ppermute | solution.py:386
  36.6 6.9 %collective-permute-done.2 = bf16[3,152,256]{2,1,0:T(8,128)(2,1)S(1)} collective-permute-done((bf16[3,152,256]{2,1,0:T(8,128)(2,1)S(1)}, bf16[3,152,256]{2,1,0:T(8,128)(2,1)S(1)}, u32[]{:S(2)}, u32[]{:S(2)}) %collective-permute-start.2) | collective-permute-done | bytes 233504 | tf_op jit(solution)/shard_map/ppermute | solution.py:363
  43.4 1.0 %maximum_select_fusion.refs_5_ = bf16[3,304,256]{2,1,0:T(8,128)(2,1)} fusion(bf16[3,152,256]{2,1,0:T(8,128)(2,1)S(1)} %collective-permute-done.2, bf16[3,152,256]{2,1,0:T(8,128)(2,1)S(1)} %maximum_select_fusion.2, pred[]{:T(512)S(6)} %eq.18), kind=kLoop, calls=%fused_computation | loop fusion | flops 2101248 | bytes 933889 | tf_op jit(solution)/shard_map/jit(_where)/select_n | solution.py:364
  44.4 14.2 %all-to-all-done = bf16[16,256,256]{2,1,0:T(8,128)(2,1)S(1)} async-done(((bf16[16,256,256]{2,1,0:T(8,128)(2,1)}), bf16[16,256,256]{2,1,0:T(8,128)(2,1)S(1)}, u32[]{:S(2)}, u32[]{:S(2)}) %all-to-all-start) | async-done | bytes 2097184 | tf_op jit(solution)/shard_map/all_to_all | solution.py:357
  58.6 0.0 copy-start
  58.6 3.1 %collective-permute-start.4 = (bf16[384,256]{1,0:T(8,128)(2,1)S(1)}, bf16[384,256]{1,0:T(8,128)(2,1)S(1)}, u32[]{:S(2)}, u32[]{:S(2)}) collective-permute-start(bf16[384,256]{1,0:T(8,128)(2,1)S(1)} %get-tuple-element.31), channel_id=1, source_target_pairs={{2,4},{4,2},{6,8},{8,6},{10,12},{12,10},{14,16},{16,14},{18,20},{2... | collective-permute-start | bytes 589832 | tf_op jit(solution)/shard_map/ppermute | solution.py:396
  61.7 0.1 collective-permute-start.3
  61.8 0.0 collective-permute-done.8.refs_4_
  61.8 0.0 copy-start.2
  61.8 1.4 %collective-permute-done.7.refs_3_ = bf16[608,384]{1,0:T(8,128)(2,1)S(1)} collective-permute-done((bf16[608,384]{1,0:T(8,128)(2,1)S(1)}, bf16[608,384]{1,0:T(8,128)(2,1)S(1)}, u32[]{:S(2)}, u32[]{:S(2)}) %collective-permute-start.7) | collective-permute-done | bytes 466976 | tf_op jit(solution)/shard_map/ppermute | solution.py:386
  63.2 0.0 copy-start.3
  63.2 3.5 %collective-permute-done.4.refs_2_ = bf16[384,256]{1,0:T(8,128)(2,1)S(1)} collective-permute-done((bf16[384,256]{1,0:T(8,128)(2,1)S(1)}, bf16[384,256]{1,0:T(8,128)(2,1)S(1)}, u32[]{:S(2)}, u32[]{:S(2)}) %collective-permute-start.4) | collective-permute-done | bytes 196640 | tf_op jit(solution)/shard_map/ppermute | solution.py:396
  66.6 0.0 copy-start.5
  66.6 0.0 collective-permute-done.3.refs_1_
  66.6 0.0 copy-start.6
  66.6 0.0 copy-done
  66.7 0.0 copy-done.2
  66.7 0.0 copy-done.3
  66.7 0.6 copy-done.5
  67.3 0.1 copy-done.6
  67.4 9.6 %own_half.1.refs_8_ = bf16[304,4096]{1,0:T(8,128)(2,1)} custom-call(bf16[4096,256]{1,0:T(8,128)(2,1)} %bitcast.12, bf16[384,256]{1,0:T(8,128)(2,1)} %copy-done.6, bf16[384,256]{1,0:T(8,128)(2,1)} %copy-done.5, bf16[608,384]{1,0:T(8,128)(2,1)} %copy-done.3, bf16[608,384]{1,0:T(8,128)(2,1)} %copy-done.2, bf16[3,304,256]{2,1,0:T(8,128)(2,1)} %bitcast.14, ...), custom_call_target="tpu_custom_call" | custom-call | tf_op jit(solution)/shard_map/own_half/pallas_call | solution.py:326
  77.0 0.0 collective-permute-done.9.refs_6_
  77.0 12.1 %other_half_and_factor.1 = f32[304,4096]{1,0:T(8,128)} custom-call(bf16[4096,256]{1,0:T(8,128)(2,1)} %bitcast.13, bf16[384,256]{1,0:T(8,128)(2,1)} %copy-done.6, bf16[384,256]{1,0:T(8,128)(2,1)} %copy-done.5, bf16[608,384]{1,0:T(8,128)(2,1)} %copy-done.3, bf16[608,384]{1,0:T(8,128)(2,1)} %copy-done.2, bf16[3,304,256]{2,1,0:T(8,128)(2,1)} %maximum_select_fusion.refs_5_, ...), custom_call_target="tpu_custom_call" | custom-call | tf_op jit(solution)/shard_map/other_half_and_factor/pallas_call | solution.py:326
  (5 shorter events, 0.2 us)
Async XLA Ops:
  4.3 54.3 %all-to-all-start = ((bf16[16,256,256]{2,1,0:T(8,128)(2,1)}), bf16[16,256,256]{2,1,0:T(8,128)(2,1)S(1)}, u32[]{:S(2)}, u32[]{:S(2)}) async-start(bf16[16,256,256]{2,1,0:T(8,128)(2,1)} %pick_rows.1), calls=%async_computation | async-start | bytes 4194304 | tf_op jit(solution)/shard_map/all_to_all | solution.py:357
  10.4 4.9 %copy-start.7 = (f32[2,304]{1,0:T(2,128)S(1)}, f32[2,304]{1,0:T(2,128)}, u32[]{:S(2)}) copy-start(f32[2,304]{1,0:T(2,128)} %param.15) | copy-start | bytes 7300
  11.6 13.6 %collective-permute-start.5 = (bf16[304,768]{1,0:T(8,128)(2,1)S(1)}, bf16[304,768]{1,0:T(8,128)(2,1)S(1)}, u32[]{:S(2)}, u32[]{:S(2)}) collective-permute-start(bf16[304,768]{1,0:T(8,128)(2,1)S(1)} %pad_maximum_fusion), channel_id=1, source_target_pairs={{0,1},{1,0},{2,3},{3,2},{4,5},{5,4},{6,7},{7,6},{8,9},{9,8},{10,11... | collective-permute-start | bytes 1400840 | tf_op jit(solution)/shard_map/ppermute | solution.py:356
  14.8 13.1 %collective-permute-start = (bf16[3,76,256]{2,1,0:T(8,128)(2,1)}, bf16[3,76,256]{2,1,0:T(8,128)(2,1)S(1)}, u32[]{:S(2)}, u32[]{:S(2)}) collective-permute-start(bf16[3,76,256]{2,1,0:T(8,128)(2,1)} %dynamic-slice_bitcast_fusion), channel_id=1, source_target_pairs={{0,1},{1,0},{2,3},{3,2},{4,5},{5,4},{6,7},{7,6},{8,9},{9,8},{10,11... | collective-permute-start | bytes 350216 | tf_op jit(solution)/shard_map/ppermute | solution.py:350
  16.1 10.6 %copy-start.1 = (bf16[304,608]{1,0:T(8,128)(2,1)S(1)}, bf16[304,608]{1,0:T(8,128)(2,1)}, u32[]{:S(2)}) copy-start(bf16[304,608]{1,0:T(8,128)(2,1)} %param.16) | copy-start | bytes 1108996
  16.1 15.2 %collective-permute-start.6 = (f32[304,2]{1,0:T(8,128)}, f32[304,2]{1,0:T(8,128)}, u32[]{:S(2)}, u32[]{:S(2)}) collective-permute-start(f32[304,2]{1,0:T(8,128)} %bitcast.15), channel_id=1, source_target_pairs={{0,1},{1,0},{2,3},{3,2},{4,5},{5,4},{6,7},{7,6},{8,9},{9,8},{10,11... | collective-permute-start | bytes 7304 | tf_op jit(solution)/shard_map/ppermute | solution.py:352
  20.7 7.2 %copy-start.8 = (s32[128]{0:T(128)S(1)}, s32[128]{0:T(128)}, u32[]{:S(2)}) copy-start(s32[128]{0:T(128)} %param.12) | copy-start | bytes 1540
  25.2 6.2 %copy-start.4 = (bf16[304,768]{1,0:T(8,128)(2,1)}, bf16[304,768]{1,0:T(8,128)(2,1)S(1)}, u32[]{:S(2)}) copy-start(bf16[304,768]{1,0:T(8,128)(2,1)S(1)} %collective-permute-done.5.refs_7_) | copy-start | bytes 1400836
  25.2 51.7 %collective-permute-start.9 = (bf16[304,3328]{1,0:T(8,128)(2,1)}, bf16[304,3328]{1,0:T(8,128)(2,1)}, u32[]{:S(2)}, u32[]{:S(2)}) collective-permute-start(bf16[304,3328]{1,0:T(8,128)(2,1)} %slice.33), channel_id=1, source_target_pairs={{0,1},{1,0},{2,3},{3,2},{4,5},{5,4},{6,7},{7,6},{8,9},{9,8},{10,11... | collective-permute-start | bytes 6070280 | tf_op jit(solution)/shard_map/ppermute | solution.py:360
  27.9 1.4 %collective-permute-start.1 = (bf16[3,76,256]{2,1,0:T(8,128)(2,1)S(1)}, bf16[3,76,256]{2,1,0:T(8,128)(2,1)S(1)}, u32[]{:S(2)}, u32[]{:S(2)}) collective-permute-start(bf16[3,76,256]{2,1,0:T(8,128)(2,1)S(1)} %collective-permute-done), channel_id=1, source_target_pairs={{0,2},{2,0},{4,6},{6,4},{8,10},{10,8},{12,14},{14,12},{16,18},{18,... | collective-permute-start | bytes 350216 | tf_op jit(solution)/shard_map/ppermute | solution.py:363
  29.4 14.1 %collective-permute-start.2 = (bf16[3,152,256]{2,1,0:T(8,128)(2,1)S(1)}, bf16[3,152,256]{2,1,0:T(8,128)(2,1)S(1)}, u32[]{:S(2)}, u32[]{:S(2)}) collective-permute-start(bf16[3,152,256]{2,1,0:T(8,128)(2,1)S(1)} %maximum_select_fusion.2), channel_id=1, source_target_pairs={{0,4},{2,6},{4,0},{6,2},{8,12},{10,14},{12,8},{14,10},{16,20},{18,... | collective-permute-start | bytes 700424 | tf_op jit(solution)/shard_map/ppermute | solution.py:363
  32.3 29.5 %collective-permute-start.8 = (bf16[608,384]{1,0:T(8,128)(2,1)}, bf16[608,384]{1,0:T(8,128)(2,1)S(1)}, u32[]{:S(2)}, u32[]{:S(2)}) collective-permute-start(bf16[608,384]{1,0:T(8,128)(2,1)} %get-tuple-element.33), channel_id=1, source_target_pairs={{2,0},{4,2},{6,4},{8,6},{10,8},{12,10},{14,12},{16,14},{18,16},{20... | collective-permute-start | bytes 1400840 | tf_op jit(solution)/shard_map/ppermute | solution.py:387
  34.2 29.0 %collective-permute-start.7 = (bf16[608,384]{1,0:T(8,128)(2,1)S(1)}, bf16[608,384]{1,0:T(8,128)(2,1)S(1)}, u32[]{:S(2)}, u32[]{:S(2)}) collective-permute-start(bf16[608,384]{1,0:T(8,128)(2,1)S(1)} %get-tuple-element.34), channel_id=1, source_target_pairs={{0,2},{2,4},{4,6},{6,8},{8,10},{10,12},{12,14},{14,16},{16,18},{18... | collective-permute-start | bytes 1400840 | tf_op jit(solution)/shard_map/ppermute | solution.py:386
  58.6 8.0 %copy-start = (bf16[16,256,256]{2,1,0:T(8,128)(2,1)}, bf16[16,256,256]{2,1,0:T(8,128)(2,1)S(1)}, u32[]{:S(2)}) copy-start(bf16[16,256,256]{2,1,0:T(8,128)(2,1)S(1)} %all-to-all-done) | copy-start | bytes 6291460
  58.6 8.0 %collective-permute-start.4 = (bf16[384,256]{1,0:T(8,128)(2,1)S(1)}, bf16[384,256]{1,0:T(8,128)(2,1)S(1)}, u32[]{:S(2)}, u32[]{:S(2)}) collective-permute-start(bf16[384,256]{1,0:T(8,128)(2,1)S(1)} %get-tuple-element.31), channel_id=1, source_target_pairs={{2,4},{4,2},{6,8},{8,6},{10,12},{12,10},{14,16},{16,14},{18,20},{2... | collective-permute-start | bytes 589832 | tf_op jit(solution)/shard_map/ppermute | solution.py:396
  61.7 4.9 %collective-permute-start.3 = (bf16[384,256]{1,0:T(8,128)(2,1)S(1)}, bf16[384,256]{1,0:T(8,128)(2,1)S(1)}, u32[]{:S(2)}, u32[]{:S(2)}) collective-permute-start(bf16[384,256]{1,0:T(8,128)(2,1)S(1)} %get-tuple-element.32), channel_id=1, source_target_pairs={{0,2},{2,0},{4,6},{6,4},{8,10},{10,8},{12,14},{14,12},{16,18},{18,... | collective-permute-start | bytes 589832 | tf_op jit(solution)/shard_map/ppermute | solution.py:395
  61.8 4.9 %copy-start.2 = (bf16[608,384]{1,0:T(8,128)(2,1)}, bf16[608,384]{1,0:T(8,128)(2,1)S(1)}, u32[]{:S(2)}) copy-start(bf16[608,384]{1,0:T(8,128)(2,1)S(1)} %collective-permute-done.8.refs_4_) | copy-start | bytes 1400836
  63.2 3.5 %copy-start.3 = (bf16[608,384]{1,0:T(8,128)(2,1)}, bf16[608,384]{1,0:T(8,128)(2,1)S(1)}, u32[]{:S(2)}) copy-start(bf16[608,384]{1,0:T(8,128)(2,1)S(1)} %collective-permute-done.7.refs_3_) | copy-start | bytes 1400836
  66.6 0.7 copy-start.5
  66.6 0.7 copy-start.6

commit v9 on v8

--- a/solution.py
+++ b/solution.py
@@ -146,7 +146,6 @@
 
     blocks = full // wide
     cuts = [blocks * n // SEGMENTS for n in range(SEGMENTS + 1)]
-    part = pl.ds(first, own)
     waits = []
     copies = []
 
@@ -164,7 +163,7 @@
             fetch(shift_hbm, shift_ref)
             for src, number in ((prof_near_hbm, 1 - odd), (prof_next_hbm, odd)):
                 fetch(src, prof.at[pl.ds(pl.multiple_of(number * (rim + pixels), XTRACK), rim), :])
-            fetch(top_hbm.at[part, :], obs.at[:, pl.ds(0, rim)])
+            fetch(top_hbm, obs.at[:, pl.ds(0, rim)])
         low = max(cuts[n] * wide - rim, 0)
         high = min(cuts[n + 1] * wide - rim, pixels)
         fetch(prof_hbm.at[pl.ds(low, high - low), :], prof.at[pl.ds(rim + low, high - low), :])
@@ -180,7 +179,7 @@
                     obs.at[:, pl.ds(rim + begin_n, end_n - begin_n)],
                 )
         if n == SEGMENTS - 1:
-            fetch(bot_hbm.at[part, :], obs.at[:, pl.ds(rim + pixels, rim)])
+            fetch(bot_hbm, obs.at[:, pl.ds(rim + pixels, rim)])
     if last:
         waits.append([])
         fetch(smooth_hbm, smooth.at[pl.ds(0, own), :])
@@ -354,9 +353,10 @@
     outgoing, obs_late = lax.optimization_barrier((outgoing, observed))
     bnd_own = jnp.concatenate([obs_late[:, :rim], obs_late[:, pixels - rim :]], axis=1)
     bnd_oth = lax.ppermute(bnd_own, "chan", swap)
+    own_rims = [lax.ppermute(bnd_own[:, rim:], "swath", forward), lax.ppermute(bnd_own[:, :rim], "swath", backward)]
     incoming = lax.all_to_all(outgoing, "swath", split_axis=0, concat_axis=0, tiled=True)
     middle = obs_late[:, rim : pixels - rim]
-    middle, bnd_oth = lax.optimization_barrier((middle, bnd_oth))
+    middle, bnd_oth, jac_near = lax.optimization_barrier((middle, bnd_oth, jac_near))
     mid_oth = lax.ppermute(middle, "chan", swap)
     jac_oth = jac_near
     for step in (1, 2):
@@ -379,12 +379,10 @@
     ])
     factor_two = jnp.where(half == 0, factor, jnp.roll(factor, own, axis=1))
 
-    bnd_own, bnd_oth, rates_oth, rows, factor_two = lax.optimization_barrier(
-        (bnd_own, bnd_oth, rates_oth, rows, factor_two)
-    )
-    bnd_both = jnp.concatenate([bnd_own, bnd_oth], axis=0)
-    obs_top = lax.ppermute(bnd_both[:, rim:], "swath", forward)
-    obs_bot = lax.ppermute(bnd_both[:, :rim], "swath", backward)
+    bnd_oth, rates_oth, rows, factor_two = lax.optimization_barrier(
+        (bnd_oth, rates_oth, rows, factor_two)
+    )
+    oth_rims = [lax.ppermute(bnd_oth[:, rim:], "swath", forward), lax.ppermute(bnd_oth[:, :rim], "swath", backward)]
 
     profiles = incoming.reshape(pixels, grid_profiles.shape[1])
     profiles, jac_oth = lax.optimization_barrier((profiles, jac_oth))
@@ -397,12 +395,12 @@
 
     smooth_own = half_call(
         False,
-        (profiles, prof_near, prof_next, obs_top, obs_bot, jac_own, observed),
+        (profiles, prof_near, prof_next, *own_rims, jac_own, observed),
         (rates_own, rows, shift),
     )
     return half_call(
         True,
-        (profiles, prof_near, prof_next, obs_top, obs_bot, jac_oth, mid_oth, bnd_oth, smooth_own, factor_two),
+        (profiles, prof_near, prof_next, *oth_rims, jac_oth, mid_oth, bnd_oth, smooth_own, factor_two),
         (rates_oth, rows, shift),
     )
 

time: 90.6 us -> 119 us (1.31)
  the two profiles are of different devices: /device:TPU:16 before, /device:TPU:9 now
where the time goes in v9:
time: 119 us
  waiting for transfers between devices  51.2 us (43%)
  starting transfers between devices  30.8 us (26%)
  Pallas kernels  25.9 us (22%)
  local copies, waits for them, and re-layouts  7 us (6%)
  other arithmetic  3.51 us (3%)
    ppermute x1, waiting for transfers between devices, on_device_two(): rates_oth = lax.ppermute(rates_own, 'chan', swap)  37.5 us
    pallas_call x2, Pallas kernels, half_call(): pl.pallas_call(functools.partial(half_kernel, last), out_shape=jax.ShapeD...  21.7 us
    ppermute x1, waiting for transfers between devices, on_device_two(): jac_near = lax.ppermute(jac_part, 'chan', swap)  9.2 us
    all_to_all x1, starting transfers between devices, on_device_two(): lax.all_to_all(outgoing, 'swath', split_axis=0, concat_axis=0, tiled=True)  6.6 us
    ppermute x1, starting transfers between devices, on_device_two(): lax.ppermute(bnd_oth[:, rim:], 'swath', forward)  5.59 us
    ppermute x1, waiting for transfers between devices, on_device_two(): prof_next = lax.ppermute(jnp.where(odd == 1, tail, head), 'swath', between)  4.5 us
    ppermute x1, starting transfers between devices, on_device_two(): lax.ppermute(bnd_oth[:, :rim], 'swath', backward)  4.3 us
    pallas_call x1, Pallas kernels, gather_rows(): pl.pallas_call(gather_kernel, out_shape=jax.ShapeDtypeStruct(shape, grid_...  4.26 us
  transfers between devices with their start and end apart: 13, of which 3 were waited for; matrix products, arithmetic and copies ran while one was open for 8% of the time, Pallas kernels for 8%

profile of v9, /device:TPU:9, one launch (start us, length us, event | category | flops | bytes accessed | tf_op | source)
XLA Modules:
  0.0 118.8 jit_solution(15489848649982027832)
XLA Ops:
  0.0 4.3 %pick_rows.1 = bf16[16,256,256]{2,1,0:T(8,128)(2,1)} custom-call(s32[16,256]{1,0:T(8,128)} %bitcast.17, s32[1,16]{1,0:T(1,128)} %counts_hbm.1, bf16[1024,256]{1,0:T(8,128)(2,1)} %grid_hbm.1), custom_call_target="tpu_custom_call" | custom-call | tf_op jit(solution)/shard_map/pick_rows/pallas_call | solution.py:110
  4.3 6.6 %all-to-all-start = ((bf16[16,256,256]{2,1,0:T(8,128)(2,1)}), bf16[16,256,256]{2,1,0:T(8,128)(2,1)S(1)}, u32[]{:S(2)}, u32[]{:S(2)}) async-start(bf16[16,256,256]{2,1,0:T(8,128)(2,1)} %pick_rows.1), calls=%async_computation | async-start | bytes 4194304 | tf_op jit(solution)/shard_map/all_to_all | solution.py:357
  10.9 1.1 fusion
  12.0 0.8 pad_maximum_fusion
  12.8 1.2 %collective-permute-start = (bf16[304,768]{1,0:T(8,128)(2,1)}, bf16[304,768]{1,0:T(8,128)(2,1)S(1)}, u32[]{:S(2)}, u32[]{:S(2)}) collective-permute-start(bf16[304,768]{1,0:T(8,128)(2,1)} %pad_maximum_fusion), channel_id=1, source_target_pairs={{0,1},{1,0},{2,3},{3,2},{4,5},{5,4},{6,7},{7,6},{8,9},{9,8},{10,11... | collective-permute-start | bytes 1400840 | tf_op jit(solution)/shard_map/ppermute | solution.py:355
  14.0 0.0 copy-start.5
  14.0 1.0 dynamic-slice_bitcast_fusion
  15.0 0.0 copy-start.6
  15.0 0.0 copy-start.1
  15.0 0.3 collective-permute-start.1
  15.3 3.1 %slice.29 = bf16[304,3328]{1,0:T(8,128)(2,1)} slice(bf16[304,4096]{1,0:T(8,128)(2,1)} %refs_6_.1), slice={[0:304], [384:3712]} | slice | bytes 4046848 | tf_op jit(solution)/shard_map/slice | solution.py:358
  18.4 9.2 %collective-permute-done.1 = bf16[3,76,256]{2,1,0:T(8,128)(2,1)S(1)} collective-permute-done((bf16[3,76,256]{2,1,0:T(8,128)(2,1)S(1)}, bf16[3,76,256]{2,1,0:T(8,128)(2,1)S(1)}, u32[]{:S(2)}, u32[]{:S(2)}) %collective-permute-start.1) | collective-permute-done | bytes 116768 | tf_op jit(solution)/shard_map/ppermute | solution.py:349
  27.6 0.0 collective-permute-done.refs_7_
  27.6 0.0 copy-start.2
  27.6 1.2 %collective-permute-start.9 = (bf16[304,3328]{1,0:T(8,128)(2,1)}, bf16[304,3328]{1,0:T(8,128)(2,1)}, u32[]{:S(2)}, u32[]{:S(2)}) collective-permute-start(bf16[304,3328]{1,0:T(8,128)(2,1)} %slice.29), channel_id=1, source_target_pairs={{0,1},{1,0},{2,3},{3,2},{4,5},{5,4},{6,7},{7,6},{8,9},{9,8},{10,11... | collective-permute-start | bytes 6070280 | tf_op jit(solution)/shard_map/ppermute | solution.py:360
  28.8 3.4 %collective-permute-start.11 = (bf16[304,384]{1,0:T(8,128)(2,1)S(1)}, bf16[304,384]{1,0:T(8,128)(2,1)}, u32[]{:S(2)}, u32[]{:S(2)}) collective-permute-start(bf16[304,384]{1,0:T(8,128)(2,1)S(1)} %get-tuple-element.29), channel_id=1, source_target_pairs={{2,0},{4,2},{6,4},{8,6},{10,8},{12,10},{14,12},{16,14},{18,16},{20... | collective-permute-start | bytes 700424 | tf_op jit(solution)/shard_map/ppermute | solution.py:356
  32.2 3.0 %collective-permute-start.10 = (bf16[304,384]{1,0:T(8,128)(2,1)S(1)}, bf16[304,384]{1,0:T(8,128)(2,1)}, u32[]{:S(2)}, u32[]{:S(2)}) collective-permute-start(bf16[304,384]{1,0:T(8,128)(2,1)S(1)} %get-tuple-element.30), channel_id=1, source_target_pairs={{0,2},{2,4},{4,6},{6,8},{8,10},{10,12},{12,14},{14,16},{16,18},{18... | collective-permute-start | bytes 700424 | tf_op jit(solution)/shard_map/ppermute | solution.py:356
  35.2 0.0 copy-done.5
  35.2 0.8 copy.10
  36.0 0.2 collective-permute-start.6
  36.2 0.1 pad.4.clone
  36.3 0.1 pad.5.clone
  36.4 0.0 copy-done.6
  36.4 0.0 copy-done.1
  36.4 0.1 fusion.2
  36.6 0.9 maximum_select_fusion.1.refs_9_
  37.5 0.0 collective-permute-start.2
  37.5 0.6 maximum_maximum_fusion.refs_8_.refs_11_
  38.1 37.5 %collective-permute-done.6.refs_10_ = f32[304,2]{1,0:T(8,128)} collective-permute-done((f32[304,2]{1,0:T(8,128)}, f32[304,2]{1,0:T(8,128)}, u32[]{:S(2)}, u32[]{:S(2)}) %collective-permute-start.6) | collective-permute-done | bytes 2464 | tf_op jit(solution)/shard_map/ppermute | solution.py:351
  75.6 0.0 collective-permute-done.2
  75.6 0.1 maximum_select_fusion.2
  75.7 1.2 %collective-permute-start.3 = (bf16[3,152,256]{2,1,0:T(8,128)(2,1)S(1)}, bf16[3,152,256]{2,1,0:T(8,128)(2,1)S(1)}, u32[]{:S(2)}, u32[]{:S(2)}) collective-permute-start(bf16[3,152,256]{2,1,0:T(8,128)(2,1)S(1)} %maximum_select_fusion.2), channel_id=1, source_target_pairs={{0,4},{2,6},{4,0},{6,2},{8,12},{10,14},{12,8},{14,10},{16,20},{18,... | collective-permute-start | bytes 700424 | tf_op jit(solution)/shard_map/ppermute | solution.py:363
  77.0 4.3 %collective-permute-start.8 = (bf16[304,384]{1,0:T(8,128)(2,1)S(1)}, bf16[304,384]{1,0:T(8,128)(2,1)}, u32[]{:S(2)}, u32[]{:S(2)}) collective-permute-start(bf16[304,384]{1,0:T(8,128)(2,1)S(1)} %get-tuple-element.33), channel_id=1, source_target_pairs={{2,0},{4,2},{6,4},{8,6},{10,8},{12,10},{14,12},{16,14},{18,16},{20... | collective-permute-start | bytes 700424 | tf_op jit(solution)/shard_map/ppermute | solution.py:385
  81.3 0.0 collective-permute-done.3
  81.3 5.6 %collective-permute-start.7 = (bf16[304,384]{1,0:T(8,128)(2,1)S(1)}, bf16[304,384]{1,0:T(8,128)(2,1)}, u32[]{:S(2)}, u32[]{:S(2)}) collective-permute-start(bf16[304,384]{1,0:T(8,128)(2,1)S(1)} %get-tuple-element.34), channel_id=1, source_target_pairs={{0,2},{2,4},{4,6},{6,8},{8,10},{10,12},{12,14},{14,16},{16,18},{18... | collective-permute-start | bytes 700424 | tf_op jit(solution)/shard_map/ppermute | solution.py:385
  86.9 1.0 maximum_select_fusion.refs_5_
  87.9 0.0 copy-done.2
  87.9 0.0 all-to-all-done
  87.9 0.0 copy-start
  87.9 0.0 collective-permute-done.11.refs_4_
  87.9 2.1 %collective-permute-start.5 = (bf16[384,256]{1,0:T(8,128)(2,1)S(1)}, bf16[384,256]{1,0:T(8,128)(2,1)S(1)}, u32[]{:S(2)}, u32[]{:S(2)}) collective-permute-start(bf16[384,256]{1,0:T(8,128)(2,1)S(1)} %get-tuple-element.31), channel_id=1, source_target_pairs={{2,4},{4,2},{6,8},{8,6},{10,12},{12,10},{14,16},{16,14},{18,20},{2... | collective-permute-start | bytes 589832 | tf_op jit(solution)/shard_map/ppermute | solution.py:394
  90.0 0.0 collective-permute-done.10.refs_3_
  90.0 1.6 %collective-permute-start.4 = (bf16[384,256]{1,0:T(8,128)(2,1)S(1)}, bf16[384,256]{1,0:T(8,128)(2,1)S(1)}, u32[]{:S(2)}, u32[]{:S(2)}) collective-permute-start(bf16[384,256]{1,0:T(8,128)(2,1)S(1)} %get-tuple-element.32), channel_id=1, source_target_pairs={{0,2},{2,0},{4,6},{6,4},{8,10},{10,8},{12,14},{14,12},{16,18},{18,... | collective-permute-start | bytes 589832 | tf_op jit(solution)/shard_map/ppermute | solution.py:393
  91.7 4.5 %collective-permute-done.5.refs_2_ = bf16[384,256]{1,0:T(8,128)(2,1)S(1)} collective-permute-done((bf16[384,256]{1,0:T(8,128)(2,1)S(1)}, bf16[384,256]{1,0:T(8,128)(2,1)S(1)}, u32[]{:S(2)}, u32[]{:S(2)}) %collective-permute-start.5) | collective-permute-done | bytes 196640 | tf_op jit(solution)/shard_map/ppermute | solution.py:394
  96.2 0.0 copy-start.3
  96.2 0.0 collective-permute-done.4.refs_1_
  96.2 0.0 copy-start.4
  96.2 0.0 copy-done
  96.2 0.7 copy-done.3
  96.8 0.1 copy-done.4
  96.9 9.6 %own_half.1.refs_8_ = bf16[304,4096]{1,0:T(8,128)(2,1)} custom-call(bf16[4096,256]{1,0:T(8,128)(2,1)} %bitcast.12, bf16[384,256]{1,0:T(8,128)(2,1)} %copy-done.4, bf16[384,256]{1,0:T(8,128)(2,1)} %copy-done.3, bf16[304,384]{1,0:T(8,128)(2,1)} %collective-permute-done.10.refs_3_, bf16[304,384]{1,0:T(8,128)(2,1)} %collective-permute-done.11.refs_4_, ...), custom_call_target="tpu_custom_call" | custom-call | tf_op jit(solution)/shard_map/own_half/pallas_call | solution.py:325
  106.5 0.0 collective-permute-done.8.refs_4_
  106.5 0.0 collective-permute-done.7.refs_3_
  106.5 0.0 collective-permute-done.9.refs_6_
  106.5 12.1 %other_half_and_factor.1 = f32[304,4096]{1,0:T(8,128)} custom-call(bf16[4096,256]{1,0:T(8,128)(2,1)} %bitcast.13, bf16[384,256]{1,0:T(8,128)(2,1)} %copy-done.4, bf16[384,256]{1,0:T(8,128)(2,1)} %copy-done.3, bf16[304,384]{1,0:T(8,128)(2,1)} %collective-permute-done.7.refs_3_, bf16[304,384]{1,0:T(8,128)(2,1)} %collective-permute-done.8.refs_4_, ...), custom_call_target="tpu_custom_call" | custom-call | tf_op jit(solution)/shard_map/other_half_and_factor/pallas_call | solution.py:325
  (3 shorter events, 0.1 us)
Async XLA Ops:
  4.3 83.6 %all-to-all-start = ((bf16[16,256,256]{2,1,0:T(8,128)(2,1)}), bf16[16,256,256]{2,1,0:T(8,128)(2,1)S(1)}, u32[]{:S(2)}, u32[]{:S(2)}) async-start(bf16[16,256,256]{2,1,0:T(8,128)(2,1)} %pick_rows.1), calls=%async_computation | async-start | bytes 4194304 | tf_op jit(solution)/shard_map/all_to_all | solution.py:357
  12.8 14.8 %collective-permute-start = (bf16[304,768]{1,0:T(8,128)(2,1)}, bf16[304,768]{1,0:T(8,128)(2,1)S(1)}, u32[]{:S(2)}, u32[]{:S(2)}) collective-permute-start(bf16[304,768]{1,0:T(8,128)(2,1)} %pad_maximum_fusion), channel_id=1, source_target_pairs={{0,1},{1,0},{2,3},{3,2},{4,5},{5,4},{6,7},{7,6},{8,9},{9,8},{10,11... | collective-permute-start | bytes 1400840 | tf_op jit(solution)/shard_map/ppermute | solution.py:355
  14.0 21.1 %copy-start.5 = (f32[2,304]{1,0:T(2,128)S(1)}, f32[2,304]{1,0:T(2,128)}, u32[]{:S(2)}) copy-start(f32[2,304]{1,0:T(2,128)} %param.15) | copy-start | bytes 7300
  15.0 21.4 %copy-start.6 = (s32[128]{0:T(128)S(1)}, s32[128]{0:T(128)}, u32[]{:S(2)}) copy-start(s32[128]{0:T(128)} %param.12) | copy-start | bytes 1540
  15.0 21.4 %copy-start.1 = (bf16[304,608]{1,0:T(8,128)(2,1)S(1)}, bf16[304,608]{1,0:T(8,128)(2,1)}, u32[]{:S(2)}) copy-start(bf16[304,608]{1,0:T(8,128)(2,1)} %param.16) | copy-start | bytes 1108996
  15.0 12.5 %collective-permute-start.1 = (bf16[3,76,256]{2,1,0:T(8,128)(2,1)S(1)}, bf16[3,76,256]{2,1,0:T(8,128)(2,1)S(1)}, u32[]{:S(2)}, u32[]{:S(2)}) collective-permute-start(bf16[3,76,256]{2,1,0:T(8,128)(2,1)S(1)} %dynamic-slice_bitcast_fusion), channel_id=1, source_target_pairs={{0,1},{1,0},{2,3},{3,2},{4,5},{5,4},{6,7},{7,6},{8,9},{9,8},{10,11... | collective-permute-start | bytes 350216 | tf_op jit(solution)/shard_map/ppermute | solution.py:349
  27.6 60.3 %copy-start.2 = (bf16[304,768]{1,0:T(8,128)(2,1)}, bf16[304,768]{1,0:T(8,128)(2,1)S(1)}, u32[]{:S(2)}) copy-start(bf16[304,768]{1,0:T(8,128)(2,1)S(1)} %collective-permute-done.refs_7_) | copy-start | bytes 1400836
  27.6 78.9 %collective-permute-start.9 = (bf16[304,3328]{1,0:T(8,128)(2,1)}, bf16[304,3328]{1,0:T(8,128)(2,1)}, u32[]{:S(2)}, u32[]{:S(2)}) collective-permute-start(bf16[304,3328]{1,0:T(8,128)(2,1)} %slice.29), channel_id=1, source_target_pairs={{0,1},{1,0},{2,3},{3,2},{4,5},{5,4},{6,7},{7,6},{8,9},{9,8},{10,11... | collective-permute-start | bytes 6070280 | tf_op jit(solution)/shard_map/ppermute | solution.py:360
  28.8 59.1 %collective-permute-start.11 = (bf16[304,384]{1,0:T(8,128)(2,1)S(1)}, bf16[304,384]{1,0:T(8,128)(2,1)}, u32[]{:S(2)}, u32[]{:S(2)}) collective-permute-start(bf16[304,384]{1,0:T(8,128)(2,1)S(1)} %get-tuple-element.29), channel_id=1, source_target_pairs={{2,0},{4,2},{6,4},{8,6},{10,8},{12,10},{14,12},{16,14},{18,16},{20... | collective-permute-start | bytes 700424 | tf_op jit(solution)/shard_map/ppermute | solution.py:356
  32.2 57.8 %collective-permute-start.10 = (bf16[304,384]{1,0:T(8,128)(2,1)S(1)}, bf16[304,384]{1,0:T(8,128)(2,1)}, u32[]{:S(2)}, u32[]{:S(2)}) collective-permute-start(bf16[304,384]{1,0:T(8,128)(2,1)S(1)} %get-tuple-element.30), channel_id=1, source_target_pairs={{0,2},{2,4},{4,6},{6,8},{8,10},{10,12},{12,14},{14,16},{16,18},{18... | collective-permute-start | bytes 700424 | tf_op jit(solution)/shard_map/ppermute | solution.py:356
  36.0 39.6 %collective-permute-start.6 = (f32[304,2]{1,0:T(8,128)}, f32[304,2]{1,0:T(8,128)}, u32[]{:S(2)}, u32[]{:S(2)}) collective-permute-start(f32[304,2]{1,0:T(8,128)} %bitcast.15), channel_id=1, source_target_pairs={{0,1},{1,0},{2,3},{3,2},{4,5},{5,4},{6,7},{7,6},{8,9},{9,8},{10,11... | collective-permute-start | bytes 7304 | tf_op jit(solution)/shard_map/ppermute | solution.py:351
  37.5 38.1 %collective-permute-start.2 = (bf16[3,76,256]{2,1,0:T(8,128)(2,1)S(1)}, bf16[3,76,256]{2,1,0:T(8,128)(2,1)S(1)}, u32[]{:S(2)}, u32[]{:S(2)}) collective-permute-start(bf16[3,76,256]{2,1,0:T(8,128)(2,1)S(1)} %collective-permute-done.1), channel_id=1, source_target_pairs={{0,2},{2,0},{4,6},{6,4},{8,10},{10,8},{12,14},{14,12},{16,18},{18,... | collective-permute-start | bytes 350216 | tf_op jit(solution)/shard_map/ppermute | solution.py:363
  75.7 5.6 %collective-permute-start.3 = (bf16[3,152,256]{2,1,0:T(8,128)(2,1)S(1)}, bf16[3,152,256]{2,1,0:T(8,128)(2,1)S(1)}, u32[]{:S(2)}, u32[]{:S(2)}) collective-permute-start(bf16[3,152,256]{2,1,0:T(8,128)(2,1)S(1)} %maximum_select_fusion.2), channel_id=1, source_target_pairs={{0,4},{2,6},{4,0},{6,2},{8,12},{10,14},{12,8},{14,10},{16,20},{18,... | collective-permute-start | bytes 700424 | tf_op jit(solution)/shard_map/ppermute | solution.py:363
  77.0 29.5 %collective-permute-start.8 = (bf16[304,384]{1,0:T(8,128)(2,1)S(1)}, bf16[304,384]{1,0:T(8,128)(2,1)}, u32[]{:S(2)}, u32[]{:S(2)}) collective-permute-start(bf16[304,384]{1,0:T(8,128)(2,1)S(1)} %get-tuple-element.33), channel_id=1, source_target_pairs={{2,0},{4,2},{6,4},{8,6},{10,8},{12,10},{14,12},{16,14},{18,16},{20... | collective-permute-start | bytes 700424 | tf_op jit(solution)/shard_map/ppermute | solution.py:385
  81.3 25.2 %collective-permute-start.7 = (bf16[304,384]{1,0:T(8,128)(2,1)S(1)}, bf16[304,384]{1,0:T(8,128)(2,1)}, u32[]{:S(2)}, u32[]{:S(2)}) collective-permute-start(bf16[304,384]{1,0:T(8,128)(2,1)S(1)} %get-tuple-element.34), channel_id=1, source_target_pairs={{0,2},{2,4},{4,6},{6,8},{8,10},{10,12},{12,14},{14,16},{16,18},{18... | collective-permute-start | bytes 700424 | tf_op jit(solution)/shard_map/ppermute | solution.py:385
  87.9 8.3 %copy-start = (bf16[16,256,256]{2,1,0:T(8,128)(2,1)}, bf16[16,256,256]{2,1,0:T(8,128)(2,1)S(1)}, u32[]{:S(2)}) copy-start(bf16[16,256,256]{2,1,0:T(8,128)(2,1)S(1)} %all-to-all-done) | copy-start | bytes 6291460
  87.9 8.2 %collective-permute-start.5 = (bf16[384,256]{1,0:T(8,128)(2,1)S(1)}, bf16[384,256]{1,0:T(8,128)(2,1)S(1)}, u32[]{:S(2)}, u32[]{:S(2)}) collective-permute-start(bf16[384,256]{1,0:T(8,128)(2,1)S(1)} %get-tuple-element.31), channel_id=1, source_target_pairs={{2,4},{4,2},{6,8},{8,6},{10,12},{12,10},{14,16},{16,14},{18,20},{2... | collective-permute-start | bytes 589832 | tf_op jit(solution)/shard_map/ppermute | solution.py:394
  90.0 6.1 %collective-permute-start.4 = (bf16[384,256]{1,0:T(8,128)(2,1)S(1)}, bf16[384,256]{1,0:T(8,128)(2,1)S(1)}, u32[]{:S(2)}, u32[]{:S(2)}) collective-permute-start(bf16[384,256]{1,0:T(8,128)(2,1)S(1)} %get-tuple-element.32), channel_id=1, source_target_pairs={{0,2},{2,0},{4,6},{6,4},{8,10},{10,8},{12,14},{14,12},{16,18},{18,... | collective-permute-start | bytes 589832 | tf_op jit(solution)/shard_map/ppermute | solution.py:393
  96.2 0.7 copy-start.3
  96.2 0.7 copy-start.4
